TPU v7x, 32 devices: a whole 2x2x4 slice. The times are simulated.
32 devices in a mesh: row: 4 (over y, core), col: 4 (over z), wave: 2 (over x).
Axes of the slice: x: 2, y: 2, z: 4, core: 2. Of those that a mesh axis runs over, the one named last changes fastest.
Arguments:
- lower_panel: float32 [16, 64, 512], P('wave', None, 'col'), may hold values from -1.5 to 1.5
- diag_inverse: float32 [16, 64, 64], P('wave'), may hold values from -0.75 to 0.75
- ancestor_inverse: float32 [2048, 2048], P('row', ('col', 'wave')), may hold values from -0.375 to 0.375
- pattern: int32 [16, 4], P('wave'), may hold values from 0 to 15, as said below
Outputs:
- inverse_panel: float32 [16, 64, 2048], P('wave', None, ('row', 'col'))
- diag_block: float32 [16, 64, 64], P('wave')
Inputs may be any that keep to these rules, and one draw needn't show every extreme that they name: `pattern`: each row holds 4 different block numbers in rising order, and every row includes 0, 15 and half of 16.
All inputs are finite; a program needn't handle non-finite values.
Results may differ from a plain program's by a relative error of at most 0.000096.
Values sent between devices are 32-bit elements; how exact they have to be, the bound alone decides.
No kernel may reach another device: no remote copies, remote signals or barrier semaphores. Data moves between devices by JAX's collectives and lax.ppermute only.
A program may use at most 128 MiB of HBM per device.

v0:
```python
import jax
import jax.numpy as jnp
from jax import lax
from jax.sharding import PartitionSpec as P

W = 64
BLK = 128


def swapped(value, axis, distance):
    mask = 2**distance
    pairs = [(source, source ^ mask) for source in range(lax.axis_size(axis))]
    return lax.ppermute(value, axis, pairs)


def select_blocks(pattern, targets):
    return (pattern[:, None, :] == targets[None, :, None]).astype(jnp.float32)


def place_blocks(onehot, packed):
    placed = jnp.einsum("sqk,swkb->swqb", onehot, packed, precision=lax.Precision.HIGHEST)
    return placed.reshape(placed.shape[0] * placed.shape[1], placed.shape[2] * placed.shape[3])


def column_product(left_cols, block_part):
    return lax.dot_general(
        left_cols, block_part, (((1,), (1,)), ((), ())), precision=lax.Precision.HIGHEST
    )


def per_device(lower_panel, diag_inverse, ancestor_inverse, pattern):
    highest = lax.Precision.HIGHEST
    sibs_here = lower_panel.shape[0]
    rows_here, cols_here = ancestor_inverse.shape
    n_col = lax.axis_size("col")
    n_wave = lax.axis_size("wave")
    row_id = lax.axis_index("row")
    col_id = lax.axis_index("col")
    wave_id = lax.axis_index("wave")
    col_blocks = cols_here // BLK
    rows_blocks = rows_here // BLK
    own_blocks = rows_blocks // n_col
    normed = jnp.einsum("svw,svk->swk", diag_inverse, lower_panel, precision=highest)
    gathered = lax.all_gather(normed, "col", axis=2, tiled=True)
    packed_count = gathered.shape[2] // BLK
    packed = gathered.reshape(sibs_here, W, packed_count, BLK)
    row_targets = (
        row_id * rows_blocks + col_id * own_blocks + jnp.arange(own_blocks, dtype=jnp.int32)
    )
    row_select = select_blocks(pattern, row_targets)
    own_rows = place_blocks(row_select, packed).reshape(sibs_here, W, own_blocks * BLK)
    row_mask = jnp.repeat(jnp.sum(row_select, axis=2), BLK, axis=1)
    partner = swapped(ancestor_inverse, "wave", 0)
    own_targets = (col_id * n_wave + wave_id) * col_blocks + jnp.arange(col_blocks, dtype=jnp.int32)
    other_targets = (col_id * n_wave + (1 - wave_id)) * col_blocks + jnp.arange(
        col_blocks, dtype=jnp.int32
    )
    own_cols = place_blocks(select_blocks(pattern, own_targets), packed)
    other_cols = place_blocks(select_blocks(pattern, other_targets), packed)
    group_sums = -(column_product(own_cols, ancestor_inverse) + column_product(other_cols, partner))
    summed = lax.psum_scatter(group_sums, "col", scatter_dimension=1, tiled=True)
    inverse_panel = summed.reshape(sibs_here, W, own_blocks * BLK) * row_mask[:, None, :]
    update = jnp.einsum("swr,sxr->swx", own_rows, inverse_panel, precision=highest)
    total_update = lax.psum(update, ("row", "col"))
    base_block = jnp.einsum("svw,svx->swx", diag_inverse, diag_inverse, precision=highest)
    return (inverse_panel, base_block - total_update)


def solution(mesh):
    return jax.shard_map(
        per_device,
        mesh=mesh,
        in_specs=(
            P("wave", None, "col"),
            P("wave", None, None),
            P("row", ("col", "wave")),
            P("wave", None),
        ),
        out_specs=(P("wave", None, ("row", "col")), P("wave", None, None)),
        check_vma=False,
    )
```

profile of v0, /device:TPU:0, one launch (start us, length us, event | category | flops | bytes accessed | tf_op | source)
XLA Modules:
  0.0 176.7 jit_solution(2909582106962489191)
XLA Ops:
  7.2 0.0 all-gather.2.cloned.1.call-start
  7.2 0.9 copy-done
  8.1 2.2 %fusion.16 = f32[8,64,128]{2,1,0:T(8,128)} fusion(f32[8,64,64]{2,1,0:T(8,128)S(1)} %copy-done, f32[8,64,128]{2,1,0:T(8,128)} %param.4), kind=kOutput, calls=%fused_computation.23 | convolution fusion | flops 50331648 | bytes 655360 | tf_op jit(solution)/shard_map/svw,svk->swk/dot_general | solution.py:43
  10.4 0.0 all-gather.2.cloned.1.call-update
  10.4 0.0 reduce-scatter.2.cloned.1.call-start
  10.5 3.0 %collective-permute-start = (f32[512,256]{1,0:T(8,128)S(1)}, f32[512,256]{1,0:T(8,128)S(1)}, u32[]{:S(2)}, u32[]{:S(2)}) collective-permute-start(f32[512,256]{1,0:T(8,128)S(1)} %copy-done.2), channel_id=1, source_target_pairs={{0,1},{1,0},{2,3},{3,2},{4,5},{5,4},{6,7},{7,6},{8,9},{9,8},{10,11... | collective-permute-start | bytes 1572872 | tf_op jit(solution)/shard_map/ppermute | solution.py:13
  13.5 0.7 copy-done.3
  14.1 0.1 copy.7
  14.2 29.2 %all-gather.2.cloned.1.call-done = f32[8,64,512]{2,1,0:T(8,128)} async-done(((f32[8,64,128]{2,1,0:T(8,128)}), f32[8,64,512]{2,1,0:T(8,128)}) %all-gather.2.cloned.1.call-update) | async-done | bytes 1048592 | tf_op jit(solution)/shard_map/all_gather | solution.py:44
  43.5 1.6 reshape.37
  45.0 1.2 fusion.6
  46.2 1.2 fusion.8
  47.3 1.0 fusion.3
  48.4 2.0 %fusion = f32[512,512]{1,0:T(8,128)} fusion(f32[512,512]{1,0:T(8,128)S(1)} %fusion.3, f32[512,256]{1,0:T(8,128)S(1)} %collective-permute-done, f32[64,8,2,128]{3,2,1,0:T(2,128)S(1)} %bitcast.38), kind=kOutput, calls=%fused_computation.1 | convolution fusion | flops 805830656 | bytes 3145728 | tf_op jit(solution)/shard_map/dot_general | solution.py:26
  50.4 0.0 reduce-scatter.2.cloned.1.call-update
  50.5 0.0 all-reduce.2.cloned.1.call-start
  50.5 0.1 copy.13
  50.6 1.2 fusion.17
  51.8 24.3 %reduce-scatter.2.cloned.1.call-done = f32[512,128]{1,0:T(8,128)} async-done(((f32[512,512]{1,0:T(8,128)}), f32[512,128]{1,0:T(8,128)}) %reduce-scatter.2.cloned.1.call-update) | async-done | bytes 262160 | tf_op jit(solution)/shard_map/reduce_scatter | solution.py:61
  76.1 1.0 broadcast_multiply_fusion
  77.1 1.2 fusion.18
  78.4 0.0 all-reduce.2.cloned.1.call-update
  78.4 89.5 %all-reduce.2.cloned.1.call-done = f32[8,64,64]{2,1,0:T(8,128)} async-done(((f32[8,64,64]{2,1,0:T(8,128)}), f32[8,64,64]{2,1,0:T(8,128)}) %all-reduce.2.cloned.1.call-update) | async-done | bytes 131088 | tf_op jit(solution)/shard_map/psum | solution.py:64
  167.9 2.2 %convolution_subtract_fusion = f32[8,64,64]{2,1,0:T(8,128)} fusion(f32[8,64,64]{2,1,0:T(8,128)} %all-reduce.2.cloned.1.call-done, f32[8,64,64]{2,1,0:T(8,128)S(1)} %copy-done), kind=kOutput, calls=%fused_computation.2 | convolution fusion | flops 25198592 | bytes 393216 | tf_op jit(solution)/shard_map/svw,svx->swx/dot_general | solution.py:65
  (10 shorter events, 0.0 us)
Async XLA Ops:
  7.2 1.0 copy-start
  7.2 3.3 %copy-start.2 = (f32[512,256]{1,0:T(8,128)S(1)}, f32[512,256]{1,0:T(8,128)}, u32[]{:S(2)}) copy-start(f32[512,256]{1,0:T(8,128)} %param.6) | copy-start | bytes 1572868
  7.2 36.3 %all-gather.2.cloned.1.call-start = ((), (), s32[]{:S(2)}) async-start(), calls=%async_computation.1 | async-start | bytes 1310720 | tf_op jit(solution)/shard_map/all_gather | solution.py:44
  10.4 65.7 %reduce-scatter.2.cloned.1.call-start = ((), (), s32[]{:S(2)}) async-start(), calls=%async_computation.2 | async-start | bytes 1310720 | tf_op jit(solution)/shard_map/reduce_scatter | solution.py:61
  10.5 37.9 %collective-permute-start = (f32[512,256]{1,0:T(8,128)S(1)}, f32[512,256]{1,0:T(8,128)S(1)}, u32[]{:S(2)}, u32[]{:S(2)}) collective-permute-start(f32[512,256]{1,0:T(8,128)S(1)} %copy-done.2), channel_id=1, source_target_pairs={{0,1},{1,0},{2,3},{3,2},{4,5},{5,4},{6,7},{7,6},{8,9},{9,8},{10,11... | collective-permute-start | bytes 1572872 | tf_op jit(solution)/shard_map/ppermute | solution.py:13
  13.5 0.7 copy-start.3
  50.5 117.4 %all-reduce.2.cloned.1.call-start = ((), (), s32[]{:S(2)}) async-start(), calls=%async_computation.3 | async-start | bytes 524288 | tf_op jit(solution)/shard_map/psum | solution.py:64
  77.1 1.3 copy-start.1
Sparse Core Ops, SparseCore 0:
  10.5 32.8 all-gather.1
  50.6 25.4 reduce-scatter.1
  80.4 87.4 all-reduce.1
where the time goes:
time: 177 us
  waiting for transfers between devices  143 us (81%)
  between operations  13.8 us (8%)
  matrix products  12.3 us (7%)
  local copies, waits for them, and re-layouts  3.33 us (2%)
  starting transfers between devices  3.12 us (2%)
    psum x1, waiting for transfers between devices, per_device(): total_update = lax.psum(update, ('row', 'col'))  89.5 us
    all_gather x1, waiting for transfers between devices, per_device(): gathered = lax.all_gather(normed, 'col', axis=2, tiled=True)  29.2 us
    reduce_scatter x1, waiting for transfers between devices, per_device(): lax.psum_scatter(group_sums, 'col', scatter_dimension=1, tiled=True)  24.3 us
  transfers between devices with their start and end apart: 4, of which 3 were waited for; matrix products, arithmetic and copies ran while one was open for 4% of the time, Pallas kernels for 0%

commit v1 on v0

v1 whole, which is shorter than its diff:
```python
import functools

import jax
import jax.numpy as jnp
from jax import lax
from jax.experimental import pallas as pl
from jax.experimental.pallas import tpu as pltpu
from jax.sharding import PartitionSpec as P

BLK = 128


def xor_permute(value, axis, distance):
    return lax.ppermute(value, axis, [(i, i ^ distance) for i in range(lax.axis_size(axis))])


def split(value):
    high = value.astype(jnp.bfloat16)
    return high, (value - high.astype(jnp.float32)).astype(jnp.bfloat16)


def product(left, right, dims):
    dot = functools.partial(lax.dot_general, dimension_numbers=(dims, ((), ())), preferred_element_type=jnp.float32)
    return dot(left[0], right[0]) + (dot(left[0], right[1]) + dot(left[1], right[0]))


def local_kernel(n_col, sibs, slots, nbk, col_blocks, pattern, ids, dinv, *refs):
    own_panel = refs[0]
    halves = refs[1:n_col]
    core_halves = refs[n_col : 2 * n_col - 1]
    mine = refs[2 * n_col - 1 : 3 * n_col - 1]
    theirs = refs[3 * n_col - 1 : 4 * n_col - 1]
    panel_out, keep_out, send_out, l_high, l_low, a_high, a_low, update = refs[4 * n_col - 1 :]
    col_id, wave_id, core, block, base_here = ids[0], ids[1], ids[2], ids[3], ids[4]
    half = sibs // 2

    def put_panel(ref, first, count, owner):
        for slot in range(slots):
            high, low = split(ref[:, :, slot * BLK : (slot + 1) * BLK])
            l_high[owner * slots + slot, pl.ds(first, count)] = high
            l_low[owner * slots + slot, pl.ds(first, count)] = low

    put_panel(own_panel, 0, sibs, col_id)
    for step in range(1, n_col):
        put_panel(halves[step - 1], core * half, half, col_id ^ step)
        put_panel(core_halves[step - 1], (1 - core) * half, half, col_id ^ step)
    for step in range(n_col):
        for group, pieces in ((wave_id, mine), (1 - wave_id, theirs)):
            for part in range(col_blocks):
                high, low = split(pieces[step][:, part * BLK : (part + 1) * BLK])
                place = ((col_id ^ step) * 2 + group) * col_blocks + part
                a_high[place] = high
                a_low[place] = low

    def sibling(s, carry):
        total = jnp.zeros((dinv.shape[1], BLK), jnp.float32)
        found, slot = False, 0
        width = min(4, nbk)
        for first in range(0, nbk, width):
            places = [pattern[s, first + k] for k in range(width)]
            left = tuple(jnp.concatenate([ref[first + k, s] for k in range(width)], axis=1) for ref in (l_high, l_low))
            right = tuple(jnp.concatenate([ref[place] for place in places], axis=1) for ref in (a_high, a_low))
            total = total + product(left, right, ((1,), (1,)))
            for k, place in enumerate(places):
                hit = place == block
                slot = jnp.where(hit, first + k, slot)
                found = jnp.logical_or(found, hit)
        inverse = dinv[s]
        factor = split(inverse)
        kept = jnp.where(found, -1.0, 0.0)
        panel = product(factor, split(total), ((0,), (0,))) * kept
        panel_out[s] = panel
        normed = product(factor, (l_high[slot, s], l_low[slot, s]), ((0,), (0,)))
        step = product(split(normed), split(panel), ((1,), (1,)))
        base = product(factor, factor, ((0,), (0,)))
        update[s] = base * jnp.where(base_here == 1, 1.0, 0.0) - step
        return carry

    if sibs * nbk <= 64:
        for s in range(sibs):
            sibling(s, 0)
    else:
        lax.fori_loop(0, sibs, sibling, 0)
    quarter = sibs // 4
    for out, part in ((keep_out, core), (send_out, 1 - core)):
        for i in range(quarter):
            pair = part * half + i
            out[i] = jnp.concatenate([update[pair], update[pair + quarter]], axis=1)


def per_device(lower_panel, diag_inverse, ancestor_inverse, pattern):
    sibs, width, packed = lower_panel.shape
    rows_here, cols_here = ancestor_inverse.shape
    n_row, n_col = lax.axis_size("row"), lax.axis_size("col")
    row_id, col_id, wave_id = (lax.axis_index(axis) for axis in ("row", "col", "wave"))
    core = row_id % 2
    own_rows = rows_here // n_col
    slots, col_blocks, nbk = packed // BLK, cols_here // BLK, pattern.shape[1]
    half, quarter = sibs // 2, sibs // 4

    panel_half = lax.dynamic_slice_in_dim(lower_panel, core * half, half, 0)
    halves = {0: panel_half}
    bit = n_col // 2
    while bit:
        for step in list(halves):
            halves[step ^ bit] = xor_permute(halves[step], "col", bit)
        bit //= 2
    core_halves = {step: xor_permute(halves[step], "row", 1) for step in range(1, n_col)}

    chunks = [
        lax.dynamic_slice_in_dim(ancestor_inverse, (col_id ^ step) * own_rows, own_rows, 0) for step in range(n_col)
    ]
    mine = [chunks[0]] + [xor_permute(chunks[step], "col", step) for step in range(1, n_col)]
    theirs = [xor_permute(piece, "wave", 1) for piece in mine]

    ids = jnp.stack(
        [col_id, wave_id, core, row_id * n_col + col_id, jnp.where((row_id == 0) & (col_id == 0), 1, 0)]
    ).astype(jnp.int32)
    operands = [lower_panel]
    operands += [halves[step] for step in range(1, n_col)] + [core_halves[step] for step in range(1, n_col)]
    operands += mine + theirs
    smem = pl.BlockSpec(memory_space=pltpu.SMEM)
    vmem = pl.BlockSpec(memory_space=pltpu.VMEM)
    n_blocks = n_col * 2 * col_blocks
    panel, keep, send = pl.pallas_call(
        functools.partial(local_kernel, n_col, sibs, slots, nbk, col_blocks),
        out_shape=(
            jax.ShapeDtypeStruct((sibs, width, BLK), jnp.float32),
            jax.ShapeDtypeStruct((quarter, width, 2 * width), jnp.float32),
            jax.ShapeDtypeStruct((quarter, width, 2 * width), jnp.float32),
        ),
        in_specs=[smem, smem] + [vmem] * (1 + len(operands)),
        out_specs=(vmem, vmem, vmem),
        scratch_shapes=[
            pltpu.VMEM((n_col * slots, sibs, width, BLK), jnp.bfloat16),
            pltpu.VMEM((n_col * slots, sibs, width, BLK), jnp.bfloat16),
            pltpu.VMEM((n_blocks, BLK, BLK), jnp.bfloat16),
            pltpu.VMEM((n_blocks, BLK, BLK), jnp.bfloat16),
            pltpu.VMEM((sibs, width, width), jnp.float32),
        ],
        compiler_params=pltpu.CompilerParams(vmem_limit_bytes=48 * 2**20),
    )(pattern, ids, diag_inverse, *operands)

    total = keep + xor_permute(send, "row", 1)
    bit = 2
    while bit < n_row:
        total = total + xor_permute(total, "row", bit)
        bit *= 2
    bit = 1
    while bit < n_col:
        total = total + xor_permute(total, "col", bit)
        bit *= 2
    other = xor_permute(total, "row", 1)
    first = jnp.where(core == 0, total, other)
    second = jnp.where(core == 0, other, total)
    both = jnp.concatenate([first[..., :width], first[..., width:], second[..., :width], second[..., width:]], axis=0)
    return panel, both


def solution(mesh):
    return jax.shard_map(
        per_device,
        mesh=mesh,
        in_specs=(
            P("wave", None, "col"),
            P("wave", None, None),
            P("row", ("col", "wave")),
            P("wave", None),
        ),
        out_specs=(P("wave", None, ("row", "col")), P("wave", None, None)),
        check_vma=False,
    )
```

time: 177 us -> 56.1 us (0.32)
  waiting for transfers between devices: 143 us -> 21.8 us
  starting transfers between devices: 3.12 us -> 24.5 us
  between operations: 13.8 us -> 0.73 us
  matrix products: 12.3 us -> 0 us
  Pallas kernels: 0 us -> 5.02 us
    psum x1 -> x0, waiting for transfers between devices: 89.5 us -> none  [per_device(): total_update = lax.psum(update, ('row', 'col'))]
    all_gather x1 -> x0, waiting for transfers between devices: 29.2 us -> none  [per_device(): gathered = lax.all_gather(normed, 'col', axis=2, tiled=True)]
    reduce_scatter x1 -> x0, waiting for transfers between devices: 24.3 us -> none  [per_device(): lax.psum_scatter(group_sums, 'col', scatter_dimension=1, tiled=True)]
    ppermute x1 -> x18, waiting for transfers between devices: 0.01 us -> 21.8 us  [xor_permute(): lax.ppermute(value, axis, [(i, i ^ distance) for i in range(lax.axis_size...]
    ppermute x1 -> x18, starting transfers between devices: 3 us -> 24.5 us  [xor_permute(): lax.ppermute(value, axis, [(i, i ^ distance) for i in range(lax.axis_size...]
    dot_general x8 -> x0, matrix products: 12.3 us -> none  [the longest x3 3.46 us: place_blocks(): jnp.einsum('sqk,swkb->swqb', onehot, packed, precision=lax.Precision.HIGH...]
    pallas_call x0 -> x1, Pallas kernels: none -> 5.02 us  [per_device(): pl.pallas_call(functools.partial(local_kernel, n_col, sibs, slots, nbk, c...]
    dynamic_slice x0 -> x2, local copies, waits for them, and re-layouts: none -> 2.1 us  [the longest x1 1.19 us: per_device(): lax.dynamic_slice_in_dim(ancestor_inverse, (col_id ^ step) * own_rows, ow...]
  transfers between devices with their start and end apart: 4 -> 18, of which waited for: 3 -> 11; matrix products, arithmetic and copies ran while one was open for 4% -> 2% of each run, Pallas kernels for 0% -> 0%
where the time goes in v1:
time: 56.1 us; the launch traced here: 55.9 us
  starting transfers between devices  24.5 us (44%)
  waiting for transfers between devices  21.8 us (39%)
  Pallas kernels  5.02 us (9%)
  local copies, waits for them, and re-layouts  3.04 us (5%)
  other arithmetic  0.78 us (1%)
  between operations  0.73 us (1%)
    ppermute x18, starting transfers between devices, xor_permute(): lax.ppermute(value, axis, [(i, i ^ distance) for i in range(lax.axis_size...  24.5 us
    ppermute x18, waiting for transfers between devices, xor_permute(): lax.ppermute(value, axis, [(i, i ^ distance) for i in range(lax.axis_size...  21.8 us
    pallas_call x1, Pallas kernels, per_device(): pl.pallas_call(functools.partial(local_kernel, n_col, sibs, slots, nbk, c...  5.02 us
    dynamic_slice x1, local copies, waits for them, and re-layouts, per_device(): lax.dynamic_slice_in_dim(ancestor_inverse, (col_id ^ step) * own_rows, ow...  1.19 us
  transfers between devices with their start and end apart: 18, of which 11 were waited for; matrix products, arithmetic and copies ran while one was open for 2% of the time, Pallas kernels for 0%

profile of v1, /device:TPU:0, one launch (start us, length us, event | category | flops | bytes accessed | tf_op | source)
XLA Modules:
  0.0 55.9 jit_solution(2248942773281509382)
XLA Ops:
  0.6 0.9 %constant_dynamic-slice_fusion.4 = f32[4,64,128]{2,1,0:T(8,128)S(1)} fusion(f32[8,64,128]{2,1,0:T(8,128)} %refs_0_.1, s32[]{:T(128)S(6)} %select_n.40), kind=kLoop, calls=%fused_computation.7 | loop fusion | bytes 262148 | tf_op jit(solution)/shard_map/dynamic_slice | solution.py:101
  1.6 4.1 %collective-permute-start.1 = (f32[4,64,128]{2,1,0:T(8,128)S(1)}, f32[4,64,128]{2,1,0:T(8,128)S(1)}, u32[]{:S(2)}, u32[]{:S(2)}) collective-permute-start(f32[4,64,128]{2,1,0:T(8,128)S(1)} %constant_dynamic-slice_fusion.4), channel_id=1, source_target_pairs={{0,4},{2,6},{4,0},{6,2},{1,5},{3,7},{5,1},{7,3},{8,12},{10,14},{12... | collective-permute-start | bytes 393224 | tf_op jit(solution)/shard_map/ppermute | solution.py:14
  5.7 1.6 %collective-permute-start = (f32[4,64,128]{2,1,0:T(8,128)S(1)}, f32[4,64,128]{2,1,0:T(8,128)S(1)}, u32[]{:S(2)}, u32[]{:S(2)}) collective-permute-start(f32[4,64,128]{2,1,0:T(8,128)S(1)} %constant_dynamic-slice_fusion.4), channel_id=1, source_target_pairs={{0,2},{2,0},{4,6},{6,4},{1,3},{3,1},{5,7},{7,5},{8,10},{10,8},{12,... | collective-permute-start | bytes 393224 | tf_op jit(solution)/shard_map/ppermute | solution.py:14
  7.3 1.2 %constant_dynamic-slice_fusion = (f32[128,256]{1,0:T(8,128)S(1)}, f32[128,256]{1,0:T(8,128)S(1)}, f32[128,256]{1,0:T(8,128)S(1)}, f32[128,256]{1,0:T(8,128)S(1)}) fusion(f32[512,256]{1,0:T(8,128)} %param.6, s32[]{:T(128)S(6)} %select_n.44, s32[]{:T(128)S(6)} %select_n.42, s32[]{:T(128)S(6)} %select_n.41, s32[]{:T(128)S(6)} %select_n.43), kind=kLoop, calls=%fused_computation.3 | loop fusion | bytes 1048592 | tf_op jit(solution)/shard_map/dynamic_slice | solution.py:111
  8.5 0.9 %collective-permute-start.6 = (f32[128,256]{1,0:T(8,128)S(1)}, f32[128,256]{1,0:T(8,128)S(1)}, u32[]{:S(2)}, u32[]{:S(2)}) collective-permute-start(f32[128,256]{1,0:T(8,128)S(1)} %get-tuple-element.9), channel_id=1, source_target_pairs={{0,2},{2,0},{4,6},{6,4},{1,3},{3,1},{5,7},{7,5},{8,10},{10,8},{12,... | collective-permute-start | bytes 393224 | tf_op jit(solution)/shard_map/ppermute | solution.py:14
  9.4 3.5 %collective-permute-start.7 = (f32[128,256]{1,0:T(8,128)S(1)}, f32[128,256]{1,0:T(8,128)S(1)}, u32[]{:S(2)}, u32[]{:S(2)}) collective-permute-start(f32[128,256]{1,0:T(8,128)S(1)} %get-tuple-element.11), channel_id=1, source_target_pairs={{0,4},{2,6},{4,0},{6,2},{1,5},{3,7},{5,1},{7,3},{8,12},{10,14},{12... | collective-permute-start | bytes 393224 | tf_op jit(solution)/shard_map/ppermute | solution.py:14
  13.4 2.1 %collective-permute-start.9 = (f32[128,256]{1,0:T(8,128)S(1)}, f32[128,256]{1,0:T(8,128)S(1)}, u32[]{:S(2)}, u32[]{:S(2)}) collective-permute-start(f32[128,256]{1,0:T(8,128)S(1)} %get-tuple-element.10.refs_7_), channel_id=1, source_target_pairs={{0,1},{1,0},{2,3},{3,2},{4,5},{5,4},{6,7},{7,6},{8,9},{9,8},{10,11... | collective-permute-start | bytes 393224 | tf_op jit(solution)/shard_map/ppermute | solution.py:14
  15.5 1.3 %collective-permute-done.8.refs_10_ = f32[128,256]{1,0:T(8,128)S(1)} collective-permute-done((f32[128,256]{1,0:T(8,128)S(1)}, f32[128,256]{1,0:T(8,128)S(1)}, u32[]{:S(2)}, u32[]{:S(2)}) %collective-permute-start.8) | collective-permute-done | bytes 131104 | tf_op jit(solution)/shard_map/ppermute | solution.py:14
  16.8 2.7 %collective-permute-start.2 = (f32[4,64,128]{2,1,0:T(8,128)S(1)}, f32[4,64,128]{2,1,0:T(8,128)S(1)}, u32[]{:S(2)}, u32[]{:S(2)}) collective-permute-start(f32[4,64,128]{2,1,0:T(8,128)S(1)} %collective-permute-done.1.refs_2_), channel_id=1, source_target_pairs={{0,2},{2,0},{4,6},{6,4},{1,3},{3,1},{5,7},{7,5},{8,10},{10,8},{12,... | collective-permute-start | bytes 393224 | tf_op jit(solution)/shard_map/ppermute | solution.py:14
  19.5 3.8 %collective-permute-done.7.refs_9_ = f32[128,256]{1,0:T(8,128)S(1)} collective-permute-done((f32[128,256]{1,0:T(8,128)S(1)}, f32[128,256]{1,0:T(8,128)S(1)}, u32[]{:S(2)}, u32[]{:S(2)}) %collective-permute-start.7) | collective-permute-done | bytes 131104 | tf_op jit(solution)/shard_map/ppermute | solution.py:14
  23.3 1.5 %collective-permute-start.12 = (f32[128,256]{1,0:T(8,128)S(1)}, f32[128,256]{1,0:T(8,128)S(1)}, u32[]{:S(2)}, u32[]{:S(2)}) collective-permute-start(f32[128,256]{1,0:T(8,128)S(1)} %collective-permute-done.8.refs_10_), channel_id=1, source_target_pairs={{0,1},{1,0},{2,3},{3,2},{4,5},{5,4},{6,7},{7,6},{8,9},{9,8},{10,11... | collective-permute-start | bytes 393224 | tf_op jit(solution)/shard_map/ppermute | solution.py:14
  25.4 1.5 %collective-permute-start.11 = (f32[128,256]{1,0:T(8,128)S(1)}, f32[128,256]{1,0:T(8,128)S(1)}, u32[]{:S(2)}, u32[]{:S(2)}) collective-permute-start(f32[128,256]{1,0:T(8,128)S(1)} %collective-permute-done.7.refs_9_), channel_id=1, source_target_pairs={{0,1},{1,0},{2,3},{3,2},{4,5},{5,4},{6,7},{7,6},{8,9},{9,8},{10,11... | collective-permute-start | bytes 393224 | tf_op jit(solution)/shard_map/ppermute | solution.py:14
  27.7 2.0 %collective-permute-done.12.refs_14_ = f32[128,256]{1,0:T(8,128)S(1)} collective-permute-done((f32[128,256]{1,0:T(8,128)S(1)}, f32[128,256]{1,0:T(8,128)S(1)}, u32[]{:S(2)}, u32[]{:S(2)}) %collective-permute-start.12) | collective-permute-done | bytes 131104 | tf_op jit(solution)/shard_map/ppermute | solution.py:14
  29.8 2.4 %collective-permute-done.10.refs_12_ = f32[128,256]{1,0:T(8,128)S(1)} collective-permute-done((f32[128,256]{1,0:T(8,128)S(1)}, f32[128,256]{1,0:T(8,128)S(1)}, u32[]{:S(2)}, u32[]{:S(2)}) %collective-permute-start.10) | collective-permute-done | bytes 131104 | tf_op jit(solution)/shard_map/ppermute | solution.py:14
  32.1 1.4 %collective-permute-done.11.refs_13_ = f32[128,256]{1,0:T(8,128)S(1)} collective-permute-done((f32[128,256]{1,0:T(8,128)S(1)}, f32[128,256]{1,0:T(8,128)S(1)}, u32[]{:S(2)}, u32[]{:S(2)}) %collective-permute-start.11) | collective-permute-done | bytes 131104 | tf_op jit(solution)/shard_map/ppermute | solution.py:14
  33.5 5.0 %shard_map.59 = (f32[8,64,128]{2,1,0:T(8,128)}, f32[2,64,128]{2,1,0:T(8,128)S(1)}, f32[2,64,128]{2,1,0:T(8,128)S(1)}) custom-call(s32[8,4]{1,0:T(8,128)S(1)} %copy.6.pattern, s32[5]{0:T(128)S(1)} %stack.23.ids, f32[8,64,64]{2,1,0:T(8,128)S(1)} %copy-done.1, f32[8,64,128]{2,1,0:T(8,128)S(1)} %copy-done, f32[4,64,128]{2,1,0:T(8,128)S(1)} %collective-permute-done.refs_1_, ...), custom_call_target="tpu_custom_call" | custom-call | tf_op jit(solution)/shard_map/pallas_call | solution.py:125
  38.5 1.3 %collective-permute-done.13 = f32[2,64,128]{2,1,0:T(8,128)S(1)} collective-permute-done((f32[2,64,128]{2,1,0:T(8,128)S(1)}, f32[2,64,128]{2,1,0:T(8,128)S(1)}, u32[]{:S(2)}, u32[]{:S(2)}) %collective-permute-start.13) | collective-permute-done | bytes 65568 | tf_op jit(solution)/shard_map/ppermute | solution.py:14
  39.8 1.3 %collective-permute-start.14 = (f32[2,64,128]{2,1,0:T(8,128)S(1)}, f32[2,64,128]{2,1,0:T(8,128)S(1)}, u32[]{:S(2)}, u32[]{:S(2)}) collective-permute-start(f32[2,64,128]{2,1,0:T(8,128)S(1)} %add.41), channel_id=1, source_target_pairs={{0,16},{8,24},{16,0},{24,8},{1,17},{9,25},{17,1},{25,9},{2,18},{10... | collective-permute-start | bytes 196616 | tf_op jit(solution)/shard_map/ppermute | solution.py:14
  41.2 3.0 %collective-permute-done.14 = f32[2,64,128]{2,1,0:T(8,128)S(1)} collective-permute-done((f32[2,64,128]{2,1,0:T(8,128)S(1)}, f32[2,64,128]{2,1,0:T(8,128)S(1)}, u32[]{:S(2)}, u32[]{:S(2)}) %collective-permute-start.14) | collective-permute-done | bytes 65568 | tf_op jit(solution)/shard_map/ppermute | solution.py:14
  44.2 1.6 %collective-permute-start.15 = (f32[2,64,128]{2,1,0:T(8,128)S(1)}, f32[2,64,128]{2,1,0:T(8,128)S(1)}, u32[]{:S(2)}, u32[]{:S(2)}) collective-permute-start(f32[2,64,128]{2,1,0:T(8,128)S(1)} %add.42), channel_id=1, source_target_pairs={{0,2},{2,0},{4,6},{6,4},{1,3},{3,1},{5,7},{7,5},{8,10},{10,8},{12,... | collective-permute-start | bytes 196616 | tf_op jit(solution)/shard_map/ppermute | solution.py:14
  45.8 2.7 %collective-permute-done.15 = f32[2,64,128]{2,1,0:T(8,128)S(1)} collective-permute-done((f32[2,64,128]{2,1,0:T(8,128)S(1)}, f32[2,64,128]{2,1,0:T(8,128)S(1)}, u32[]{:S(2)}, u32[]{:S(2)}) %collective-permute-start.15) | collective-permute-done | bytes 65568 | tf_op jit(solution)/shard_map/ppermute | solution.py:14
  48.5 3.0 %collective-permute-start.16 = (f32[2,64,128]{2,1,0:T(8,128)S(1)}, f32[2,64,128]{2,1,0:T(8,128)S(1)}, u32[]{:S(2)}, u32[]{:S(2)}) collective-permute-start(f32[2,64,128]{2,1,0:T(8,128)S(1)} %add.43), channel_id=1, source_target_pairs={{0,4},{2,6},{4,0},{6,2},{1,5},{3,7},{5,1},{7,3},{8,12},{10,14},{12... | collective-permute-start | bytes 196616 | tf_op jit(solution)/shard_map/ppermute | solution.py:14
  51.5 2.3 %collective-permute-done.16 = f32[2,64,128]{2,1,0:T(8,128)S(1)} collective-permute-done((f32[2,64,128]{2,1,0:T(8,128)S(1)}, f32[2,64,128]{2,1,0:T(8,128)S(1)}, u32[]{:S(2)}, u32[]{:S(2)}) %collective-permute-start.16) | collective-permute-done | bytes 65568 | tf_op jit(solution)/shard_map/ppermute | solution.py:14
  53.8 1.2 %collective-permute-done.17 = f32[2,64,128]{2,1,0:T(8,128)S(1)} collective-permute-done((f32[2,64,128]{2,1,0:T(8,128)S(1)}, f32[2,64,128]{2,1,0:T(8,128)S(1)}, u32[]{:S(2)}, u32[]{:S(2)}) %collective-permute-start.17) | collective-permute-done | bytes 65568 | tf_op jit(solution)/shard_map/ppermute | solution.py:14
  (30 shorter events, 2.9 us)
Async XLA Ops:
  1.6 11.8 %collective-permute-start.1 = (f32[4,64,128]{2,1,0:T(8,128)S(1)}, f32[4,64,128]{2,1,0:T(8,128)S(1)}, u32[]{:S(2)}, u32[]{:S(2)}) collective-permute-start(f32[4,64,128]{2,1,0:T(8,128)S(1)} %constant_dynamic-slice_fusion.4), channel_id=1, source_target_pairs={{0,4},{2,6},{4,0},{6,2},{1,5},{3,7},{5,1},{7,3},{8,12},{10,14},{12... | collective-permute-start | bytes 393224 | tf_op jit(solution)/shard_map/ppermute | solution.py:14
  5.7 9.8 %collective-permute-start = (f32[4,64,128]{2,1,0:T(8,128)S(1)}, f32[4,64,128]{2,1,0:T(8,128)S(1)}, u32[]{:S(2)}, u32[]{:S(2)}) collective-permute-start(f32[4,64,128]{2,1,0:T(8,128)S(1)} %constant_dynamic-slice_fusion.4), channel_id=1, source_target_pairs={{0,2},{2,0},{4,6},{6,4},{1,3},{3,1},{5,7},{7,5},{8,10},{10,8},{12,... | collective-permute-start | bytes 393224 | tf_op jit(solution)/shard_map/ppermute | solution.py:14
  7.2 26.3 %copy-start = (f32[8,64,128]{2,1,0:T(8,128)S(1)}, f32[8,64,128]{2,1,0:T(8,128)}, u32[]{:S(2)}) copy-start(f32[8,64,128]{2,1,0:T(8,128)} %refs_0_.1) | copy-start | bytes 786436
  7.2 26.3 %copy-start.1 = (f32[8,64,64]{2,1,0:T(8,128)S(1)}, f32[8,64,64]{2,1,0:T(8,128)}, u32[]{:S(2)}) copy-start(f32[8,64,64]{2,1,0:T(8,128)} %dinv.1) | copy-start | bytes 393220
  8.4 8.3 %collective-permute-start.8 = (f32[128,256]{1,0:T(8,128)S(1)}, f32[128,256]{1,0:T(8,128)S(1)}, u32[]{:S(2)}, u32[]{:S(2)}) collective-permute-start(f32[128,256]{1,0:T(8,128)S(1)} %get-tuple-element.8), channel_id=1, source_target_pairs={{0,6},{2,4},{4,2},{6,0},{1,7},{3,5},{5,3},{7,1},{8,14},{10,12},{12... | collective-permute-start | bytes 393224 | tf_op jit(solution)/shard_map/ppermute | solution.py:14
  8.5 11.0 %collective-permute-start.6 = (f32[128,256]{1,0:T(8,128)S(1)}, f32[128,256]{1,0:T(8,128)S(1)}, u32[]{:S(2)}, u32[]{:S(2)}) collective-permute-start(f32[128,256]{1,0:T(8,128)S(1)} %get-tuple-element.9), channel_id=1, source_target_pairs={{0,2},{2,0},{4,6},{6,4},{1,3},{3,1},{5,7},{7,5},{8,10},{10,8},{12,... | collective-permute-start | bytes 393224 | tf_op jit(solution)/shard_map/ppermute | solution.py:14
  9.4 13.9 %collective-permute-start.7 = (f32[128,256]{1,0:T(8,128)S(1)}, f32[128,256]{1,0:T(8,128)S(1)}, u32[]{:S(2)}, u32[]{:S(2)}) collective-permute-start(f32[128,256]{1,0:T(8,128)S(1)} %get-tuple-element.11), channel_id=1, source_target_pairs={{0,4},{2,6},{4,0},{6,2},{1,5},{3,7},{5,1},{7,3},{8,12},{10,14},{12... | collective-permute-start | bytes 393224 | tf_op jit(solution)/shard_map/ppermute | solution.py:14
  13.4 11.5 %collective-permute-start.9 = (f32[128,256]{1,0:T(8,128)S(1)}, f32[128,256]{1,0:T(8,128)S(1)}, u32[]{:S(2)}, u32[]{:S(2)}) collective-permute-start(f32[128,256]{1,0:T(8,128)S(1)} %get-tuple-element.10.refs_7_), channel_id=1, source_target_pairs={{0,1},{1,0},{2,3},{3,2},{4,5},{5,4},{6,7},{7,6},{8,9},{9,8},{10,11... | collective-permute-start | bytes 393224 | tf_op jit(solution)/shard_map/ppermute | solution.py:14
  15.5 9.9 %collective-permute-start.4 = (f32[4,64,128]{2,1,0:T(8,128)S(1)}, f32[4,64,128]{2,1,0:T(8,128)S(1)}, u32[]{:S(2)}, u32[]{:S(2)}) collective-permute-start(f32[4,64,128]{2,1,0:T(8,128)S(1)} %collective-permute-done.1.refs_2_), channel_id=1, source_target_pairs={{0,8},{8,0},{16,24},{24,16},{1,9},{9,1},{17,25},{25,17},{2,10},{10... | collective-permute-start | bytes 393224 | tf_op jit(solution)/shard_map/ppermute | solution.py:14
  16.8 10.1 %collective-permute-start.2 = (f32[4,64,128]{2,1,0:T(8,128)S(1)}, f32[4,64,128]{2,1,0:T(8,128)S(1)}, u32[]{:S(2)}, u32[]{:S(2)}) collective-permute-start(f32[4,64,128]{2,1,0:T(8,128)S(1)} %collective-permute-done.1.refs_2_), channel_id=1, source_target_pairs={{0,2},{2,0},{4,6},{6,4},{1,3},{3,1},{5,7},{7,5},{8,10},{10,8},{12,... | collective-permute-start | bytes 393224 | tf_op jit(solution)/shard_map/ppermute | solution.py:14
  19.5 8.2 %collective-permute-start.3 = (f32[4,64,128]{2,1,0:T(8,128)S(1)}, f32[4,64,128]{2,1,0:T(8,128)S(1)}, u32[]{:S(2)}, u32[]{:S(2)}) collective-permute-start(f32[4,64,128]{2,1,0:T(8,128)S(1)} %collective-permute-done.refs_1_), channel_id=1, source_target_pairs={{0,8},{8,0},{16,24},{24,16},{1,9},{9,1},{17,25},{25,17},{2,10},{10... | collective-permute-start | bytes 393224 | tf_op jit(solution)/shard_map/ppermute | solution.py:14
  23.3 6.4 %collective-permute-start.12 = (f32[128,256]{1,0:T(8,128)S(1)}, f32[128,256]{1,0:T(8,128)S(1)}, u32[]{:S(2)}, u32[]{:S(2)}) collective-permute-start(f32[128,256]{1,0:T(8,128)S(1)} %collective-permute-done.8.refs_10_), channel_id=1, source_target_pairs={{0,1},{1,0},{2,3},{3,2},{4,5},{5,4},{6,7},{7,6},{8,9},{9,8},{10,11... | collective-permute-start | bytes 393224 | tf_op jit(solution)/shard_map/ppermute | solution.py:14
  24.9 7.2 %collective-permute-start.10 = (f32[128,256]{1,0:T(8,128)S(1)}, f32[128,256]{1,0:T(8,128)S(1)}, u32[]{:S(2)}, u32[]{:S(2)}) collective-permute-start(f32[128,256]{1,0:T(8,128)S(1)} %collective-permute-done.6.refs_8_), channel_id=1, source_target_pairs={{0,1},{1,0},{2,3},{3,2},{4,5},{5,4},{6,7},{7,6},{8,9},{9,8},{10,11... | collective-permute-start | bytes 393224 | tf_op jit(solution)/shard_map/ppermute | solution.py:14
  25.4 8.2 %collective-permute-start.11 = (f32[128,256]{1,0:T(8,128)S(1)}, f32[128,256]{1,0:T(8,128)S(1)}, u32[]{:S(2)}, u32[]{:S(2)}) collective-permute-start(f32[128,256]{1,0:T(8,128)S(1)} %collective-permute-done.7.refs_9_), channel_id=1, source_target_pairs={{0,1},{1,0},{2,3},{3,2},{4,5},{5,4},{6,7},{7,6},{8,9},{9,8},{10,11... | collective-permute-start | bytes 393224 | tf_op jit(solution)/shard_map/ppermute | solution.py:14
  26.9 6.6 %collective-permute-start.5 = (f32[4,64,128]{2,1,0:T(8,128)S(1)}, f32[4,64,128]{2,1,0:T(8,128)S(1)}, u32[]{:S(2)}, u32[]{:S(2)}) collective-permute-start(f32[4,64,128]{2,1,0:T(8,128)S(1)} %collective-permute-done.2.refs_3_), channel_id=1, source_target_pairs={{0,8},{8,0},{16,24},{24,16},{1,9},{9,1},{17,25},{25,17},{2,10},{10... | collective-permute-start | bytes 393224 | tf_op jit(solution)/shard_map/ppermute | solution.py:14
  26.9 0.7 %copy-start.2 = (s32[8,4]{0,1:T(4,128)S(1)}, s32[8,4]{0,1:T(4,128)}, u32[]{:S(2)}) copy-start(s32[8,4]{0,1:T(4,128)} %param.7) | copy-start | bytes 388
  38.5 1.3 %collective-permute-start.13 = (f32[2,64,128]{2,1,0:T(8,128)S(1)}, f32[2,64,128]{2,1,0:T(8,128)S(1)}, u32[]{:S(2)}, u32[]{:S(2)}) collective-permute-start(f32[2,64,128]{2,1,0:T(8,128)S(1)} %get-tuple-element.7), channel_id=1, source_target_pairs={{0,8},{8,0},{16,24},{24,16},{1,9},{9,1},{17,25},{25,17},{2,10},{10... | collective-permute-start | bytes 196616 | tf_op jit(solution)/shard_map/ppermute | solution.py:14
  39.8 4.3 %collective-permute-start.14 = (f32[2,64,128]{2,1,0:T(8,128)S(1)}, f32[2,64,128]{2,1,0:T(8,128)S(1)}, u32[]{:S(2)}, u32[]{:S(2)}) collective-permute-start(f32[2,64,128]{2,1,0:T(8,128)S(1)} %add.41), channel_id=1, source_target_pairs={{0,16},{8,24},{16,0},{24,8},{1,17},{9,25},{17,1},{25,9},{2,18},{10... | collective-permute-start | bytes 196616 | tf_op jit(solution)/shard_map/ppermute | solution.py:14
  44.2 4.3 %collective-permute-start.15 = (f32[2,64,128]{2,1,0:T(8,128)S(1)}, f32[2,64,128]{2,1,0:T(8,128)S(1)}, u32[]{:S(2)}, u32[]{:S(2)}) collective-permute-start(f32[2,64,128]{2,1,0:T(8,128)S(1)} %add.42), channel_id=1, source_target_pairs={{0,2},{2,0},{4,6},{6,4},{1,3},{3,1},{5,7},{7,5},{8,10},{10,8},{12,... | collective-permute-start | bytes 196616 | tf_op jit(solution)/shard_map/ppermute | solution.py:14
  48.5 5.2 %collective-permute-start.16 = (f32[2,64,128]{2,1,0:T(8,128)S(1)}, f32[2,64,128]{2,1,0:T(8,128)S(1)}, u32[]{:S(2)}, u32[]{:S(2)}) collective-permute-start(f32[2,64,128]{2,1,0:T(8,128)S(1)} %add.43), channel_id=1, source_target_pairs={{0,4},{2,6},{4,0},{6,2},{1,5},{3,7},{5,1},{7,3},{8,12},{10,14},{12... | collective-permute-start | bytes 196616 | tf_op jit(solution)/shard_map/ppermute | solution.py:14
  53.7 1.3 %collective-permute-start.17 = (f32[2,64,128]{2,1,0:T(8,128)S(1)}, f32[2,64,128]{2,1,0:T(8,128)S(1)}, u32[]{:S(2)}, u32[]{:S(2)}) collective-permute-start(f32[2,64,128]{2,1,0:T(8,128)S(1)} %add.44), channel_id=1, source_target_pairs={{0,8},{8,0},{16,24},{24,16},{1,9},{9,1},{17,25},{25,17},{2,10},{10... | collective-permute-start | bytes 196616 | tf_op jit(solution)/shard_map/ppermute | solution.py:14

commit v2 on v1

v2 whole, which is shorter than its diff:
```python
import functools

import jax
import jax.numpy as jnp
from jax import lax
from jax.experimental import pallas as pl
from jax.experimental.pallas import tpu as pltpu
from jax.sharding import PartitionSpec as P

BLK = 128
CONTRACT_LAST = ((1,), (1,))
CONTRACT_FIRST = ((0,), (0,))


DONE = {'core_own': 1, 'mine0': 5, 'mine1': 4, 'mine2': 4, 'normed_other': 4, 'panel': 6, 'theirs0': 4, 'theirs1': None, 'theirs2': None}
GATE = {'mine2': False, 'scalars': True}
SPLIT = True
COST = [100000000000, 1000000000, 100000000000]


def xor_permute(value, axis, distance):
    return lax.ppermute(value, axis, [(i, i ^ distance) for i in range(lax.axis_size(axis))])


def split(value):
    high = value.astype(jnp.bfloat16)
    return high, (value - high.astype(jnp.float32)).astype(jnp.bfloat16)


def product(left, right, dims):
    dot = functools.partial(lax.dot_general, dimension_numbers=(dims, ((), ())), preferred_element_type=jnp.float32)
    return dot(left[0], right[0]) + (dot(left[0], right[1]) + dot(left[1], right[0]))


def update_kernel(n_col, slots, col_blocks, rows_blocks, scalars, dinv, *refs):
    halves, (own, partner, core_own, core_partner) = refs[:n_col], refs[n_col : n_col + 4]
    out, normed_out, r_high, r_low, c_high, c_low = refs[n_col + 4 :]
    nbk = n_col * slots
    col_id, wave_id, core, row_id = scalars[scalars.shape[0] - 5 + 0], scalars[scalars.shape[0] - 5 + 1], scalars[scalars.shape[0] - 5 + 2], scalars[scalars.shape[0] - 5 + 3]
    half, width = halves[0].shape[0], halves[0].shape[1]
    row_first = (row_id - core) * rows_blocks
    col_first = col_id * 2 * col_blocks
    n_rows, n_cols = 2 * rows_blocks, 2 * col_blocks
    for ref in (r_high, r_low, c_high, c_low):
        ref[...] = jnp.zeros_like(ref)
    for s in range(half):
        lower = jnp.concatenate([halves[step][s] for step in range(n_col)], axis=1)
        normed = product(split(dinv[core * half + s]), split(lower), CONTRACT_FIRST)
        for step in range(n_col):
            for slot in range(slots):
                first = (step * slots + slot) * BLK
                here = normed[:, first : first + BLK]
                number = (col_id ^ step) * slots + slot
                normed_out[number, s] = here
                high, low = split(here)
                place = scalars[(core * half + s) * nbk + number]
                for first, count, to_high, to_low in ((row_first, n_rows, r_high, r_low), (col_first, n_cols, c_high, c_low)):
                    inside = jnp.logical_and(place >= first, place < first + count)
                    target = jnp.where(inside, place - first, count)
                    to_high[target, s * width : (s + 1) * width] = high
                    to_low[target, s * width : (s + 1) * width] = low

    def columns(ref):
        mine = [ref[wave_id * col_blocks + part] for part in range(col_blocks)]
        theirs = [ref[(1 - wave_id) * col_blocks + part] for part in range(col_blocks)]
        return jnp.concatenate(mine + theirs, axis=1)

    left = columns(c_high), columns(c_low)
    total = jnp.zeros((half * width, half * width), jnp.float32)
    group = 2
    for who, mine, theirs in ((core, own, partner), (1 - core, core_own, core_partner)):
        for first in range(0, rows_blocks, group):
            rows = slice(first * BLK, (first + group) * BLK)
            block = split(jnp.concatenate([mine[rows, :], theirs[rows, :]], axis=1))
            part = product(left, block, CONTRACT_LAST)
            place = who * rows_blocks + first
            right = tuple(jnp.concatenate([ref[place + i] for i in range(group)], axis=1) for ref in (r_high, r_low))
            total = total + product(right, split(part), CONTRACT_LAST)
    blocks = [total[s * width : (s + 1) * width, s * width : (s + 1) * width] for s in range(half)]
    for i in range(half // 2):
        out[i] = jnp.concatenate([blocks[i], blocks[i + half // 2]], axis=1)


def add_products(total, left, r_high, r_low, blocks):
    for place, rows in blocks:
        part = product(left, split(rows), CONTRACT_LAST)
        right = tuple(jnp.concatenate([ref[place], ref[place + 1]], axis=1) for ref in (r_high, r_low))
        total = total + product(right, split(part), CONTRACT_LAST)
    return total


def row_pairs(core, rows_blocks, own, other):
    for who, ref in ((core, own), (1 - core, other)):
        for first in range(0, rows_blocks, 2):
            yield who * rows_blocks + first, ref[first * BLK : (first + 2) * BLK, :]


def columns(ref, first, count):
    return jnp.concatenate([ref[first + part] for part in range(count)], axis=1)


def first_kernel(n_col, slots, col_blocks, rows_blocks, scalars, dinv, *refs):
    halves, own, core_own = refs[:n_col], refs[n_col], refs[n_col + 1]
    total_out, normed_out, r_high, r_low, c_high, c_low = refs[n_col + 2 :]
    nbk = n_col * slots
    col_id, wave_id, core, row_id = scalars[scalars.shape[0] - 5 + 0], scalars[scalars.shape[0] - 5 + 1], scalars[scalars.shape[0] - 5 + 2], scalars[scalars.shape[0] - 5 + 3]
    half, width = halves[0].shape[0], halves[0].shape[1]
    row_first = (row_id - core) * rows_blocks
    col_first = col_id * 2 * col_blocks
    n_rows, n_cols = 2 * rows_blocks, 2 * col_blocks
    for ref in (r_high, r_low, c_high, c_low):
        ref[...] = jnp.zeros_like(ref)
    for s in range(half):
        lower = jnp.concatenate([halves[step][s] for step in range(n_col)], axis=1)
        normed = product(split(dinv[core * half + s]), split(lower), CONTRACT_FIRST)
        for step in range(n_col):
            for slot in range(slots):
                first = (step * slots + slot) * BLK
                here = normed[:, first : first + BLK]
                number = (col_id ^ step) * slots + slot
                normed_out[number, s] = here
                high, low = split(here)
                place = scalars[(core * half + s) * nbk + number]
                for first, count, to_high, to_low in ((row_first, n_rows, r_high, r_low), (col_first, n_cols, c_high, c_low)):
                    inside = jnp.logical_and(place >= first, place < first + count)
                    target = jnp.where(inside, place - first, count)
                    to_high[target, s * width : (s + 1) * width] = high
                    to_low[target, s * width : (s + 1) * width] = low
    left = tuple(columns(ref, wave_id * col_blocks, col_blocks) for ref in (c_high, c_low))
    total = jnp.zeros((half * width, half * width), jnp.float32)
    total_out[...] = add_products(total, left, r_high, r_low, row_pairs(core, rows_blocks, own, core_own))


def second_kernel(half, width, col_blocks, rows_blocks, scalars, total, r_high, r_low, c_high, c_low, partner, core_partner, out):
    wave_id, core = scalars[scalars.shape[0] - 5 + 1], scalars[scalars.shape[0] - 5 + 2]
    left = tuple(columns(ref, (1 - wave_id) * col_blocks, col_blocks) for ref in (c_high, c_low))
    total = add_products(total[...], left, r_high, r_low, row_pairs(core, rows_blocks, partner, core_partner))
    blocks = [total[s * width : (s + 1) * width, s * width : (s + 1) * width] for s in range(half)]
    for i in range(half // 2):
        out[i] = jnp.concatenate([blocks[i], blocks[i + half // 2]], axis=1)


def panel_kernel(n_col, sibs, nbk, col_blocks, scalars, dinv, *refs):
    normed, own, partner = refs[:2], refs[2], refs[3]
    mine, theirs = refs[4 : 3 + n_col], refs[3 + n_col : 2 + 2 * n_col]
    panel_out, base_out, n_high, n_low, a_high, a_low = refs[2 + 2 * n_col :]
    col_id, wave_id, core, block = scalars[scalars.shape[0] - 5 + 0], scalars[scalars.shape[0] - 5 + 1], scalars[scalars.shape[0] - 5 + 2], scalars[scalars.shape[0] - 5 + 4]
    half = sibs // 2
    for ref, who in zip(normed, (core, 1 - core)):
        for slot in range(nbk):
            high, low = split(ref[slot])
            n_high[slot, pl.ds(who * half, half)] = high
            n_low[slot, pl.ds(who * half, half)] = low
    here = pl.ds(pl.multiple_of(col_id * BLK, BLK), BLK)
    for step in range(n_col):
        for group, first, pieces in ((wave_id, own, mine), (1 - wave_id, partner, theirs)):
            for part in range(col_blocks):
                columns = slice(part * BLK, (part + 1) * BLK)
                high, low = split(pieces[step - 1][:, columns] if step else first[here, columns])
                place = ((col_id ^ step) * 2 + group) * col_blocks + part
                a_high[place] = high
                a_low[place] = low

    def sibling(s, carry):
        total = jnp.zeros((dinv.shape[1], BLK), jnp.float32)
        found = False
        width = min(4, nbk)
        for first in range(0, nbk, width):
            places = [scalars[(s) * nbk + first + k] for k in range(width)]
            left = tuple(jnp.concatenate([ref[first + k, s] for k in range(width)], axis=1) for ref in (n_high, n_low))
            right = tuple(jnp.concatenate([ref[place] for place in places], axis=1) for ref in (a_high, a_low))
            total = total + product(left, right, CONTRACT_LAST)
            for place in places:
                found = jnp.logical_or(found, place == block)
        panel_out[s] = total * jnp.where(found, -1.0, 0.0)
        return carry

    if sibs * nbk <= 64:
        for s in range(sibs):
            sibling(s, 0)
    else:
        lax.fori_loop(0, sibs, sibling, 0)
    bases = []
    for s in range(sibs):
        factor = split(dinv[s])
        bases.append(product(factor, factor, CONTRACT_FIRST))
    for i in range(half // 2):
        for first in (0, half):
            base_out[first // 2 + i] = jnp.concatenate([bases[first + i], bases[first + half // 2 + i]], axis=1)


def per_device(lower_panel, diag_inverse, ancestor_inverse, pattern):
    sibs, width, packed = lower_panel.shape
    rows_here, cols_here = ancestor_inverse.shape
    n_row, n_col = lax.axis_size("row"), lax.axis_size("col")
    row_id, col_id, wave_id = (lax.axis_index(axis) for axis in ("row", "col", "wave"))
    core = row_id % 2
    own_rows = rows_here // n_col
    slots, col_blocks, nbk = packed // BLK, cols_here // BLK, pattern.shape[1]
    rows_blocks = rows_here // BLK
    half, quarter = sibs // 2, sibs // 4
    n_blocks = n_col * 2 * col_blocks
    f32, bf16 = jnp.float32, jnp.bfloat16
    smem = pl.BlockSpec(memory_space=pltpu.SMEM)
    vmem = pl.BlockSpec(memory_space=pltpu.VMEM)
    mib = 2**20
    size = rows_here * cols_here * 4 // mib + 1
    params = pltpu.CompilerParams(vmem_limit_bytes=min(60, 12 + 12 * size) * mib)
    ids = jnp.stack([col_id, wave_id, core, row_id, row_id * n_col + col_id]).astype(jnp.int32)

    def call(kernel, out_shape, operands, scratch, flops):
        moved = sum(x.size * 4 for x in operands)
        return pl.pallas_call(
            kernel,
            out_shape=out_shape,
            in_specs=[smem] + [vmem] * len(operands),
            out_specs=jax.tree.map(lambda _: vmem, out_shape),
            scratch_shapes=scratch,
            compiler_params=params,
            cost_estimate=pl.CostEstimate(flops=flops, bytes_accessed=(moved if flops > 10 else 1), transcendentals=0),
        )(scalars, *operands)

    def tie(point, value):
        names = [name for name in late if due(name) == point]
        if names:
            value, *tied = lax.optimization_barrier((value, *[late[name] for name in names]))
            late.update(zip(names, tied))
        return value

    def due(name):
        if name[-1].isdigit():
            stem = name.rstrip("0123456789")
            return DONE.get(stem + str(min(int(name[len(stem) :]), 2)))
        return DONE.get(name)

    far = n_col // 2
    late = {}
    half_panel = lax.dynamic_slice_in_dim(lower_panel, core * half, half, 0)
    source = ancestor_inverse
    if GATE.get("wave"):
        source, half_panel = lax.optimization_barrier((source, half_panel))
    partner = xor_permute(source, "wave", 1)
    halves = {0: half_panel}
    halves[far] = xor_permute(halves[0], "col", far)
    chunks = [
        lax.dynamic_slice_in_dim(ancestor_inverse, (col_id ^ step) * own_rows, own_rows, 0) for step in range(1, n_col)
    ]
    if GATE.get("slices"):
        half_panel, *chunks = lax.optimization_barrier((half_panel, *chunks))
        halves[0] = half_panel
        halves[far] = xor_permute(half_panel, "col", far)
    gated = [i for i in range(n_col - 1) if GATE.get("mine" + str(min(i, 2)))]
    if gated:
        halves[far], *held = lax.optimization_barrier((halves[far], *[chunks[i] for i in gated]))
        for i, chunk in zip(gated, held):
            chunks[i] = chunk
    mine = [xor_permute(chunk, "col", step) for step, chunk in enumerate(chunks, 1)]
    late.update({"mine" + str(i): x for i, x in enumerate(mine)})
    late.update({"theirs" + str(i): xor_permute(x, "wave", 1) for i, x in enumerate(mine)})
    late["core_own"] = xor_permute(ancestor_inverse, "row", 1)
    scalars = jnp.concatenate([pattern.reshape(-1), ids])
    if GATE.get("scalars"):
        halves[far], scalars = lax.optimization_barrier((halves[far], scalars))
    halves[far] = tie(0, halves[far])
    bit = far // 2
    while bit:
        for step in list(halves):
            halves[step ^ bit] = xor_permute(halves[step], "col", bit)
        bit //= 2
    partner, *tied = lax.optimization_barrier((partner, *[halves[step] for step in range(n_col)]))
    halves = dict(enumerate(tied))
    partner = tie(1, partner)
    core_partner = xor_permute(partner, "row", 1)
    if SPLIT:
        square = half * width
        partial, normed, *placed = call(
            functools.partial(first_kernel, n_col, slots, col_blocks, rows_blocks),
            (
                jax.ShapeDtypeStruct((square, square), f32),
                jax.ShapeDtypeStruct((nbk, half, width, BLK), f32),
                jax.ShapeDtypeStruct((2 * rows_blocks + 1, square, BLK), bf16),
                jax.ShapeDtypeStruct((2 * rows_blocks + 1, square, BLK), bf16),
                jax.ShapeDtypeStruct((2 * col_blocks + 1, square, BLK), bf16),
                jax.ShapeDtypeStruct((2 * col_blocks + 1, square, BLK), bf16),
            ),
            [diag_inverse] + [halves[step] for step in range(n_col)] + [ancestor_inverse, late["core_own"]],
            [],
            COST[0],
        )
        late["normed_other"] = xor_permute(normed, "row", 1)
        core_partner = tie(2, core_partner)
        total = call(
            functools.partial(second_kernel, half, width, col_blocks, rows_blocks),
            jax.ShapeDtypeStruct((quarter, width, 2 * width), f32),
            [partial, *placed, partner, core_partner],
            [],
            COST[2],
        )
    else:
        core_partner = tie(2, core_partner)
        total, normed = call(
            functools.partial(update_kernel, n_col, slots, col_blocks, rows_blocks),
            (
                jax.ShapeDtypeStruct((quarter, width, 2 * width), f32),
                jax.ShapeDtypeStruct((nbk, half, width, BLK), f32),
            ),
            [diag_inverse] + [halves[step] for step in range(n_col)]
            + [ancestor_inverse, partner, late["core_own"], core_partner],
            [pltpu.VMEM((2 * rows_blocks + 1, half * width, BLK), bf16)] * 2
            + [pltpu.VMEM((2 * col_blocks + 1, half * width, BLK), bf16)] * 2,
            COST[0],
        )
        late["normed_other"] = xor_permute(normed, "row", 1)
    total = tie(3, total)
    bit = 2
    while bit < n_row:
        total = total + xor_permute(total, "row", bit)
        bit *= 2
    total = tie(4, total)
    bit = 1
    while bit < n_col:
        total = total + xor_permute(total, "col", bit)
        bit *= 2
        if bit < n_col:
            total = tie(5, total)
    total = tie(6, total)
    pieces = [late["mine" + str(i)] for i in range(n_col - 1)] + [late["theirs" + str(i)] for i in range(n_col - 1)]
    panel, base = call(
        functools.partial(panel_kernel, n_col, sibs, nbk, col_blocks),
        (
            jax.ShapeDtypeStruct((sibs, width, BLK), f32),
            jax.ShapeDtypeStruct((half, width, 2 * width), f32),
        ),
        [diag_inverse, normed, late["normed_other"], ancestor_inverse, partner] + pieces,
        [pltpu.VMEM((nbk, sibs, width, BLK), bf16)] * 2 + [pltpu.VMEM((n_blocks, BLK, BLK), bf16)] * 2,
        COST[1],
    )
    if DONE.get("panel") == 6:
        total, panel = lax.optimization_barrier((total, panel))
    other = xor_permute(total, "row", 1)
    if DONE.get("panel") == 7:
        other, panel = lax.optimization_barrier((other, panel))
    first = jnp.where(core == 0, total, other) + base[:quarter]
    second = jnp.where(core == 0, other, total) + base[quarter:]
    diag = jnp.concatenate([first[..., :width], first[..., width:], second[..., :width], second[..., width:]], axis=0)
    return panel, diag


def solution(mesh):
    return jax.shard_map(
        per_device,
        mesh=mesh,
        in_specs=(
            P("wave", None, "col"),
            P("wave", None, None),
            P("row", ("col", "wave")),
            P("wave", None),
        ),
        out_specs=(P("wave", None, ("row", "col")), P("wave", None, None)),
        check_vma=False,
    )
```

time: 56.1 us -> 43.8 us (0.78)
  waiting for transfers between devices: 21.8 us -> 12 us
  starting transfers between devices: 24.5 us -> 19.6 us
  Pallas kernels: 5.02 us -> 7.61 us
    ppermute x18 -> x17, waiting for transfers between devices: 21.8 us -> 12 us  [xor_permute(): lax.ppermute(value, axis, [(i, i ^ distance) for i in range(lax.axis_size...]
    ppermute x18 -> x17, starting transfers between devices: 24.5 us -> 19.6 us  [xor_permute(): lax.ppermute(value, axis, [(i, i ^ distance) for i in range(lax.axis_size...]
    pallas_call x1 -> x3, Pallas kernels: 5.02 us -> 7.61 us  [call(): pl.pallas_call(kernel, out_shape=out_shape, in_specs=[smem] + [vmem] * le...]
    dynamic_slice x1, local copies, waits for them, and re-layouts: 0.92 us -> 0.01 us  [per_device(): half_panel = lax.dynamic_slice_in_dim(lower_panel, core * half, half, 0)]
    dynamic_slice x1, local copies, waits for them, and re-layouts: 1.19 us -> 1.8 us  [per_device(): lax.dynamic_slice_in_dim(ancestor_inverse, (col_id ^ step) * own_rows, ow...]
  transfers between devices with their start and end apart: 18 -> 17, of which waited for: 11 -> 6; matrix products, arithmetic and copies ran while one was open for 2% -> 5% of each run, Pallas kernels for 0% -> 17%
where the time goes in v2:
time: 43.8 us; the launch traced here: 43.6 us
  starting transfers between devices  19.6 us (45%)
  waiting for transfers between devices  12 us (27%)
  Pallas kernels  7.61 us (17%)
  local copies, waits for them, and re-layouts  2.84 us (6%)
  other arithmetic  0.77 us (2%)
  between operations  0.75 us (2%)
    ppermute x17, starting transfers between devices, xor_permute(): lax.ppermute(value, axis, [(i, i ^ distance) for i in range(lax.axis_size...  19.6 us
    ppermute x17, waiting for transfers between devices, xor_permute(): lax.ppermute(value, axis, [(i, i ^ distance) for i in range(lax.axis_size...  12 us
    pallas_call x3, Pallas kernels, call(): pl.pallas_call(kernel, out_shape=out_shape, in_specs=[smem] + [vmem] * le...  7.61 us
    dynamic_slice x1, local copies, waits for them, and re-layouts, per_device(): lax.dynamic_slice_in_dim(ancestor_inverse, (col_id ^ step) * own_rows, ow...  1.8 us
  transfers between devices with their start and end apart: 17, of which 6 were waited for; matrix products, arithmetic and copies ran while one was open for 5% of the time, Pallas kernels for 17%

profile of v2, /device:TPU:0, one launch (start us, length us, event | category | flops | bytes accessed | tf_op | source)
XLA Modules:
  0.0 43.6 jit_solution(980980400191622227)
XLA Ops:
  0.6 3.0 %collective-permute-start.1 = (f32[512,256]{1,0:T(8,128)}, f32[512,256]{1,0:T(8,128)S(1)}, u32[]{:S(2)}, u32[]{:S(2)}) collective-permute-start(f32[512,256]{1,0:T(8,128)} %refs_2_.1), channel_id=1, source_target_pairs={{0,1},{1,0},{2,3},{3,2},{4,5},{5,4},{6,7},{7,6},{8,9},{9,8},{10,11... | collective-permute-start | bytes 1572872 | tf_op jit(solution)/shard_map/ppermute | solution.py:22
  3.7 2.7 %collective-permute-start = (f32[4,64,128]{2,1,0:T(8,128)S(1)}, f32[4,64,128]{2,1,0:T(8,128)S(1)}, u32[]{:S(2)}, u32[]{:S(2)}) collective-permute-start(f32[4,64,128]{2,1,0:T(8,128)S(1)} %constant_dynamic-slice_fusion.3.refs_0_), channel_id=1, source_target_pairs={{0,4},{2,6},{4,0},{6,2},{1,5},{3,7},{5,1},{7,3},{8,12},{10,14},{12... | collective-permute-start | bytes 393224 | tf_op jit(solution)/shard_map/ppermute | solution.py:22
  6.3 1.6 %collective-permute-start.2 = (f32[4,64,128]{2,1,0:T(8,128)S(1)}, f32[4,64,128]{2,1,0:T(8,128)S(1)}, u32[]{:S(2)}, u32[]{:S(2)}) collective-permute-start(f32[4,64,128]{2,1,0:T(8,128)S(1)} %constant_dynamic-slice_fusion.3.refs_0_), channel_id=1, source_target_pairs={{0,2},{2,0},{4,6},{6,4},{1,3},{3,1},{5,7},{7,5},{8,10},{10,8},{12,... | collective-permute-start | bytes 393224 | tf_op jit(solution)/shard_map/ppermute | solution.py:22
  7.9 1.8 %constant_dynamic-slice_fusion = (f32[128,256]{1,0:T(8,128)S(1)}, f32[128,256]{1,0:T(8,128)}, f32[128,256]{1,0:T(8,128)}) fusion(f32[512,256]{1,0:T(8,128)} %refs_2_.1, s32[]{:T(128)S(6)} %select_n.35, s32[]{:T(128)S(6)} %select_n.34, s32[]{:T(128)S(6)} %select_n.33), kind=kLoop, calls=%fused_computation.3 | loop fusion | bytes 786444 | tf_op jit(solution)/shard_map/dynamic_slice | solution.py:246
  9.7 0.4 %collective-permute-start.9 = (f32[128,256]{1,0:T(8,128)S(1)}, f32[128,256]{1,0:T(8,128)}, u32[]{:S(2)}, u32[]{:S(2)}) collective-permute-start(f32[128,256]{1,0:T(8,128)S(1)} %get-tuple-element.54), channel_id=1, source_target_pairs={{0,2},{2,0},{4,6},{6,4},{1,3},{3,1},{5,7},{7,5},{8,10},{10,8},{12,... | collective-permute-start | bytes 393224 | tf_op jit(solution)/shard_map/ppermute | solution.py:22
  10.2 0.7 %copy-done.3 = s32[8,4]{0,1:T(4,128)S(1)} copy-done((s32[8,4]{0,1:T(4,128)S(1)}, s32[8,4]{0,1:T(4,128)}, u32[]{:S(2)}) %copy-start.3) | copy-done | bytes 152
  11.1 2.4 %collective-permute-done.refs_2_ = f32[4,64,128]{2,1,0:T(8,128)S(1)} collective-permute-done((f32[4,64,128]{2,1,0:T(8,128)S(1)}, f32[4,64,128]{2,1,0:T(8,128)S(1)}, u32[]{:S(2)}, u32[]{:S(2)}) %collective-permute-start) | collective-permute-done | bytes 131104 | tf_op jit(solution)/shard_map/ppermute | solution.py:22
  13.5 0.6 %collective-permute-start.3 = (f32[4,64,128]{2,1,0:T(8,128)S(1)}, f32[4,64,128]{2,1,0:T(8,128)S(1)}, u32[]{:S(2)}, u32[]{:S(2)}) collective-permute-start(f32[4,64,128]{2,1,0:T(8,128)S(1)} %collective-permute-done.refs_2_), channel_id=1, source_target_pairs={{0,2},{2,0},{4,6},{6,4},{1,3},{3,1},{5,7},{7,5},{8,10},{10,8},{12,... | collective-permute-start | bytes 393224 | tf_op jit(solution)/shard_map/ppermute | solution.py:22
  14.1 3.4 %collective-permute-start.7 = (f32[128,256]{1,0:T(8,128)}, f32[128,256]{1,0:T(8,128)}, u32[]{:S(2)}, u32[]{:S(2)}) collective-permute-start(f32[128,256]{1,0:T(8,128)} %get-tuple-element.56), channel_id=1, source_target_pairs={{0,4},{2,6},{4,0},{6,2},{1,5},{3,7},{5,1},{7,3},{8,12},{10,14},{12... | collective-permute-start | bytes 393224 | tf_op jit(solution)/shard_map/ppermute | solution.py:22
  17.5 1.5 %collective-permute-start.8 = (f32[128,256]{1,0:T(8,128)}, f32[128,256]{1,0:T(8,128)}, u32[]{:S(2)}, u32[]{:S(2)}) collective-permute-start(f32[128,256]{1,0:T(8,128)} %get-tuple-element.55), channel_id=1, source_target_pairs={{0,6},{2,4},{4,2},{6,0},{1,7},{3,5},{5,3},{7,1},{8,14},{10,12},{12... | collective-permute-start | bytes 393224 | tf_op jit(solution)/shard_map/ppermute | solution.py:22
  19.0 2.3 %collective-permute-done.3.refs_3_ = f32[4,64,128]{2,1,0:T(8,128)S(1)} collective-permute-done((f32[4,64,128]{2,1,0:T(8,128)S(1)}, f32[4,64,128]{2,1,0:T(8,128)S(1)}, u32[]{:S(2)}, u32[]{:S(2)}) %collective-permute-start.3) | collective-permute-done | bytes 131104 | tf_op jit(solution)/shard_map/ppermute | solution.py:22
  21.9 2.5 %shard_map.59 = (f32[256,256]{1,0:T(8,128)S(1)}, f32[4,4,64,128]{3,2,1,0:T(8,128)S(1)}, bf16[9,256,128]{2,1,0:T(8,128)(2,1)S(1)}, bf16[9,256,128]{2,1,0:T(8,128)...) custom-call(s32[37]{0:T(128)S(1)} %concatenate.6.scalars, f32[8,64,64]{2,1,0:T(8,128)S(1)} %copy-done.2, ...), custom_call_target="tpu_custom_call" | custom-call | flops 99999997952 | bytes 1703936 | tf_op jit(solution)/shard_map/pallas_call | solution.py:213
  24.3 0.6 %collective-permute-start.11 = (f32[4,4,64,128]{3,2,1,0:T(8,128)S(1)}, f32[4,4,64,128]{3,2,1,0:T(8,128)S(1)}, u32[]{:S(2)}, u32[]{:S(2)}) collective-permute-start(f32[4,4,64,128]{3,2,1,0:T(8,128)S(1)} %get-tuple-element.42.refs_0_), channel_id=1, source_target_pairs={{0,8},{8,0},{16,24},{24,16},{1,9},{9,1},{17,25},{25,17},{2,10},{10... | collective-permute-start | bytes 1572872 | tf_op jit(solution)/shard_map/ppermute | solution.py:22
  24.9 1.9 %shard_map.60 = f32[2,64,128]{2,1,0:T(8,128)S(1)} custom-call(s32[37]{0:T(128)S(1)} %concatenate.6.scalars, f32[256,256]{1,0:T(8,128)S(1)} %get-tuple-element.36.total, bf16[9,256,128]{2,1,0:T(8,128)(2,1)S(1)} %get-tuple-element.37.r_high, bf16[9,256,128]{2,1,0:T(8,128)(2,1)S(1)} %get-tuple-element.38.r_low, ...), custom_call_target="tpu_custom_call" | custom-call | flops 99999997952 | bytes 4980736 | tf_op jit(solution)/shard_map/pallas_call | solution.py:213
  26.8 1.7 %collective-permute-start.6 = (f32[2,64,128]{2,1,0:T(8,128)S(1)}, f32[2,64,128]{2,1,0:T(8,128)S(1)}, u32[]{:S(2)}, u32[]{:S(2)}) collective-permute-start(f32[2,64,128]{2,1,0:T(8,128)S(1)} %shard_map.60), channel_id=1, source_target_pairs={{0,16},{8,24},{16,0},{24,8},{1,17},{9,25},{17,1},{25,9},{2,18},{10... | collective-permute-start | bytes 196616 | tf_op jit(solution)/shard_map/ppermute | solution.py:22
  28.5 1.5 %collective-permute-start.14 = (f32[128,256]{1,0:T(8,128)}, f32[128,256]{1,0:T(8,128)S(1)}, u32[]{:S(2)}, u32[]{:S(2)}) collective-permute-start(f32[128,256]{1,0:T(8,128)} %collective-permute-done.7.refs_5_), channel_id=1, source_target_pairs={{0,1},{1,0},{2,3},{3,2},{4,5},{5,4},{6,7},{7,6},{8,9},{9,8},{10,11... | collective-permute-start | bytes 393224 | tf_op jit(solution)/shard_map/ppermute | solution.py:22
  30.0 0.5 %collective-permute-start.15 = (f32[128,256]{1,0:T(8,128)}, f32[128,256]{1,0:T(8,128)S(1)}, u32[]{:S(2)}, u32[]{:S(2)}) collective-permute-start(f32[128,256]{1,0:T(8,128)} %collective-permute-done.8.refs_6_), channel_id=1, source_target_pairs={{0,1},{1,0},{2,3},{3,2},{4,5},{5,4},{6,7},{7,6},{8,9},{9,8},{10,11... | collective-permute-start | bytes 393224 | tf_op jit(solution)/shard_map/ppermute | solution.py:22
  30.5 0.6 %collective-permute-done.6 = f32[2,64,128]{2,1,0:T(8,128)S(1)} collective-permute-done((f32[2,64,128]{2,1,0:T(8,128)S(1)}, f32[2,64,128]{2,1,0:T(8,128)S(1)}, u32[]{:S(2)}, u32[]{:S(2)}) %collective-permute-start.6) | collective-permute-done | bytes 65568 | tf_op jit(solution)/shard_map/ppermute | solution.py:22
  31.3 4.2 %collective-permute-done.12 = f32[2,64,128]{2,1,0:T(8,128)S(1)} collective-permute-done((f32[2,64,128]{2,1,0:T(8,128)S(1)}, f32[2,64,128]{2,1,0:T(8,128)S(1)}, u32[]{:S(2)}, u32[]{:S(2)}) %collective-permute-start.12) | collective-permute-done | bytes 65568 | tf_op jit(solution)/shard_map/ppermute | solution.py:22
  35.5 1.5 %collective-permute-start.13 = (f32[2,64,128]{2,1,0:T(8,128)S(1)}, f32[2,64,128]{2,1,0:T(8,128)S(1)}, u32[]{:S(2)}, u32[]{:S(2)}) collective-permute-start(f32[2,64,128]{2,1,0:T(8,128)S(1)} %add.41), channel_id=1, source_target_pairs={{0,4},{2,6},{4,0},{6,2},{1,5},{3,7},{5,1},{7,3},{8,12},{10,14},{12... | collective-permute-start | bytes 196616 | tf_op jit(solution)/shard_map/ppermute | solution.py:22
  37.0 3.2 %shard_map.61 = (f32[8,64,128]{2,1,0:T(8,128)}, f32[4,64,128]{2,1,0:T(8,128)S(1)}) custom-call(s32[37]{0:T(128)S(1)} %concatenate.6.scalars, f32[8,64,64]{2,1,0:T(8,128)S(1)} %copy-done.2, f32[4,4,64,128]{3,2,1,0:T(8,128)S(1)} %get-tuple-element.42.refs_0_, f32[4,4,64,128]{3,2,1,0:T(8,128)S(1)} %collective-permute-done.11.refs_1_, f32[512,256]{1,0:T(8,128)S(1)} %copy-done.1, ...), custom_call_target="tpu_custom_call" | custom-call | flops 1000000000 | bytes 3014656 | tf_op jit(solution)/shard_map/pallas_call | solution.py:213
  40.2 1.2 %collective-permute-done.13 = f32[2,64,128]{2,1,0:T(8,128)S(1)} collective-permute-done((f32[2,64,128]{2,1,0:T(8,128)S(1)}, f32[2,64,128]{2,1,0:T(8,128)S(1)}, u32[]{:S(2)}, u32[]{:S(2)}) %collective-permute-start.13) | collective-permute-done | bytes 65568 | tf_op jit(solution)/shard_map/ppermute | solution.py:22
  41.5 1.2 %collective-permute-done.16 = f32[2,64,128]{2,1,0:T(8,128)S(1)} collective-permute-done((f32[2,64,128]{2,1,0:T(8,128)S(1)}, f32[2,64,128]{2,1,0:T(8,128)S(1)}, u32[]{:S(2)}, u32[]{:S(2)}) %collective-permute-start.16) | collective-permute-done | bytes 65568 | tf_op jit(solution)/shard_map/ppermute | solution.py:22
  42.8 0.7 %pad_maximum_fusion = f32[8,64,64]{2,1,0:T(8,128)} fusion(f32[2,64,64]{2,1,0:T(8,128)S(1)} %get-tuple-element.63, f32[2,64,64]{2,1,0:T(8,128)S(1)} %get-tuple-element.64, f32[2,64,64]{2,1,0:T(8,128)S(1)} %get-tuple-element.60, f32[2,64,64]{2,1,0:T(8,128)S(1)} %get-tuple-element.59), kind=kLoop, calls=%fused_computation | loop fusion | flops 98304 | bytes 262144 | tf_op jit(solution)/shard_map/concatenate | solution.py:345
  (32 shorter events, 1.1 us)
Async XLA Ops:
  0.6 3.0 %copy-start = (f32[8,64,128]{2,1,0:T(8,128)S(1)}, f32[8,64,128]{2,1,0:T(8,128)}, u32[]{:S(2)}) copy-start(f32[8,64,128]{2,1,0:T(8,128)} %param.4) | copy-start | bytes 786436
  0.6 21.2 %collective-permute-start.1 = (f32[512,256]{1,0:T(8,128)}, f32[512,256]{1,0:T(8,128)S(1)}, u32[]{:S(2)}, u32[]{:S(2)}) collective-permute-start(f32[512,256]{1,0:T(8,128)} %refs_2_.1), channel_id=1, source_target_pairs={{0,1},{1,0},{2,3},{3,2},{4,5},{5,4},{6,7},{7,6},{8,9},{9,8},{10,11... | collective-permute-start | bytes 1572872 | tf_op jit(solution)/shard_map/ppermute | solution.py:22
  3.6 18.2 %collective-permute-start.4 = (f32[512,256]{1,0:T(8,128)}, f32[512,256]{1,0:T(8,128)S(1)}, u32[]{:S(2)}, u32[]{:S(2)}) collective-permute-start(f32[512,256]{1,0:T(8,128)} %refs_2_.1), channel_id=1, source_target_pairs={{0,8},{8,0},{16,24},{24,16},{1,9},{9,1},{17,25},{25,17},{2,10},{10... | collective-permute-start | bytes 1572872 | tf_op jit(solution)/shard_map/ppermute | solution.py:22
  3.7 18.2 %copy-start.1 = (f32[512,256]{1,0:T(8,128)S(1)}, f32[512,256]{1,0:T(8,128)}, u32[]{:S(2)}) copy-start(f32[512,256]{1,0:T(8,128)} %refs_2_.1) | copy-start | bytes 1572868
  3.7 9.8 %collective-permute-start = (f32[4,64,128]{2,1,0:T(8,128)S(1)}, f32[4,64,128]{2,1,0:T(8,128)S(1)}, u32[]{:S(2)}, u32[]{:S(2)}) collective-permute-start(f32[4,64,128]{2,1,0:T(8,128)S(1)} %constant_dynamic-slice_fusion.3.refs_0_), channel_id=1, source_target_pairs={{0,4},{2,6},{4,0},{6,2},{1,5},{3,7},{5,1},{7,3},{8,12},{10,14},{12... | collective-permute-start | bytes 393224 | tf_op jit(solution)/shard_map/ppermute | solution.py:22
  6.3 7.8 %collective-permute-start.2 = (f32[4,64,128]{2,1,0:T(8,128)S(1)}, f32[4,64,128]{2,1,0:T(8,128)S(1)}, u32[]{:S(2)}, u32[]{:S(2)}) collective-permute-start(f32[4,64,128]{2,1,0:T(8,128)S(1)} %constant_dynamic-slice_fusion.3.refs_0_), channel_id=1, source_target_pairs={{0,2},{2,0},{4,6},{6,4},{1,3},{3,1},{5,7},{7,5},{8,10},{10,8},{12,... | collective-permute-start | bytes 393224 | tf_op jit(solution)/shard_map/ppermute | solution.py:22
  7.9 13.9 %copy-start.2 = (f32[8,64,64]{2,1,0:T(8,128)S(1)}, f32[8,64,64]{2,1,0:T(8,128)}, u32[]{:S(2)}) copy-start(f32[8,64,64]{2,1,0:T(8,128)} %dinv.3) | copy-start | bytes 393220
  9.7 7.8 %collective-permute-start.9 = (f32[128,256]{1,0:T(8,128)S(1)}, f32[128,256]{1,0:T(8,128)}, u32[]{:S(2)}, u32[]{:S(2)}) collective-permute-start(f32[128,256]{1,0:T(8,128)S(1)} %get-tuple-element.54), channel_id=1, source_target_pairs={{0,2},{2,0},{4,6},{6,4},{1,3},{3,1},{5,7},{7,5},{8,10},{10,8},{12,... | collective-permute-start | bytes 393224 | tf_op jit(solution)/shard_map/ppermute | solution.py:22
  10.2 0.7 %copy-start.3 = (s32[8,4]{0,1:T(4,128)S(1)}, s32[8,4]{0,1:T(4,128)}, u32[]{:S(2)}) copy-start(s32[8,4]{0,1:T(4,128)} %param.7) | copy-start | bytes 388
  13.5 7.9 %collective-permute-start.3 = (f32[4,64,128]{2,1,0:T(8,128)S(1)}, f32[4,64,128]{2,1,0:T(8,128)S(1)}, u32[]{:S(2)}, u32[]{:S(2)}) collective-permute-start(f32[4,64,128]{2,1,0:T(8,128)S(1)} %collective-permute-done.refs_2_), channel_id=1, source_target_pairs={{0,2},{2,0},{4,6},{6,4},{1,3},{3,1},{5,7},{7,5},{8,10},{10,8},{12,... | collective-permute-start | bytes 393224 | tf_op jit(solution)/shard_map/ppermute | solution.py:22
  14.1 14.4 %collective-permute-start.7 = (f32[128,256]{1,0:T(8,128)}, f32[128,256]{1,0:T(8,128)}, u32[]{:S(2)}, u32[]{:S(2)}) collective-permute-start(f32[128,256]{1,0:T(8,128)} %get-tuple-element.56), channel_id=1, source_target_pairs={{0,4},{2,6},{4,0},{6,2},{1,5},{3,7},{5,1},{7,3},{8,12},{10,14},{12... | collective-permute-start | bytes 393224 | tf_op jit(solution)/shard_map/ppermute | solution.py:22
  17.5 12.5 %collective-permute-start.8 = (f32[128,256]{1,0:T(8,128)}, f32[128,256]{1,0:T(8,128)}, u32[]{:S(2)}, u32[]{:S(2)}) collective-permute-start(f32[128,256]{1,0:T(8,128)} %get-tuple-element.55), channel_id=1, source_target_pairs={{0,6},{2,4},{4,2},{6,0},{1,7},{3,5},{5,3},{7,1},{8,14},{10,12},{12... | collective-permute-start | bytes 393224 | tf_op jit(solution)/shard_map/ppermute | solution.py:22
  21.4 9.8 %collective-permute-start.10 = (f32[128,256]{1,0:T(8,128)}, f32[128,256]{1,0:T(8,128)}, u32[]{:S(2)}, u32[]{:S(2)}) collective-permute-start(f32[128,256]{1,0:T(8,128)} %collective-permute-done.9.refs_4_), channel_id=1, source_target_pairs={{0,1},{1,0},{2,3},{3,2},{4,5},{5,4},{6,7},{7,6},{8,9},{9,8},{10,11... | collective-permute-start | bytes 393224 | tf_op jit(solution)/shard_map/ppermute | solution.py:22
  21.8 3.1 %collective-permute-start.5 = (f32[512,256]{1,0:T(8,128)S(1)}, f32[512,256]{1,0:T(8,128)S(1)}, u32[]{:S(2)}, u32[]{:S(2)}) collective-permute-start(f32[512,256]{1,0:T(8,128)S(1)} %collective-permute-done.1.partner.refs_3_), channel_id=1, source_target_pairs={{0,8},{8,0},{16,24},{24,16},{1,9},{9,1},{17,25},{25,17},{2,10},{10... | collective-permute-start | bytes 1572872 | tf_op jit(solution)/shard_map/ppermute | solution.py:22
  24.3 6.8 %collective-permute-start.11 = (f32[4,4,64,128]{3,2,1,0:T(8,128)S(1)}, f32[4,4,64,128]{3,2,1,0:T(8,128)S(1)}, u32[]{:S(2)}, u32[]{:S(2)}) collective-permute-start(f32[4,4,64,128]{3,2,1,0:T(8,128)S(1)} %get-tuple-element.42.refs_0_), channel_id=1, source_target_pairs={{0,8},{8,0},{16,24},{24,16},{1,9},{9,1},{17,25},{25,17},{2,10},{10... | collective-permute-start | bytes 1572872 | tf_op jit(solution)/shard_map/ppermute | solution.py:22
  26.8 4.3 %collective-permute-start.6 = (f32[2,64,128]{2,1,0:T(8,128)S(1)}, f32[2,64,128]{2,1,0:T(8,128)S(1)}, u32[]{:S(2)}, u32[]{:S(2)}) collective-permute-start(f32[2,64,128]{2,1,0:T(8,128)S(1)} %shard_map.60), channel_id=1, source_target_pairs={{0,16},{8,24},{16,0},{24,8},{1,17},{9,25},{17,1},{25,9},{2,18},{10... | collective-permute-start | bytes 196616 | tf_op jit(solution)/shard_map/ppermute | solution.py:22
  28.5 8.5 %collective-permute-start.14 = (f32[128,256]{1,0:T(8,128)}, f32[128,256]{1,0:T(8,128)S(1)}, u32[]{:S(2)}, u32[]{:S(2)}) collective-permute-start(f32[128,256]{1,0:T(8,128)} %collective-permute-done.7.refs_5_), channel_id=1, source_target_pairs={{0,1},{1,0},{2,3},{3,2},{4,5},{5,4},{6,7},{7,6},{8,9},{9,8},{10,11... | collective-permute-start | bytes 393224 | tf_op jit(solution)/shard_map/ppermute | solution.py:22
  30.0 7.0 %collective-permute-start.15 = (f32[128,256]{1,0:T(8,128)}, f32[128,256]{1,0:T(8,128)S(1)}, u32[]{:S(2)}, u32[]{:S(2)}) collective-permute-start(f32[128,256]{1,0:T(8,128)} %collective-permute-done.8.refs_6_), channel_id=1, source_target_pairs={{0,1},{1,0},{2,3},{3,2},{4,5},{5,4},{6,7},{7,6},{8,9},{9,8},{10,11... | collective-permute-start | bytes 393224 | tf_op jit(solution)/shard_map/ppermute | solution.py:22
  31.2 4.3 %collective-permute-start.12 = (f32[2,64,128]{2,1,0:T(8,128)S(1)}, f32[2,64,128]{2,1,0:T(8,128)S(1)}, u32[]{:S(2)}, u32[]{:S(2)}) collective-permute-start(f32[2,64,128]{2,1,0:T(8,128)S(1)} %add.37), channel_id=1, source_target_pairs={{0,2},{2,0},{4,6},{6,4},{1,3},{3,1},{5,7},{7,5},{8,10},{10,8},{12,... | collective-permute-start | bytes 196616 | tf_op jit(solution)/shard_map/ppermute | solution.py:22
  35.5 5.9 %collective-permute-start.13 = (f32[2,64,128]{2,1,0:T(8,128)S(1)}, f32[2,64,128]{2,1,0:T(8,128)S(1)}, u32[]{:S(2)}, u32[]{:S(2)}) collective-permute-start(f32[2,64,128]{2,1,0:T(8,128)S(1)} %add.41), channel_id=1, source_target_pairs={{0,4},{2,6},{4,0},{6,2},{1,5},{3,7},{5,1},{7,3},{8,12},{10,14},{12... | collective-permute-start | bytes 196616 | tf_op jit(solution)/shard_map/ppermute | solution.py:22
  41.4 1.3 %collective-permute-start.16 = (f32[2,64,128]{2,1,0:T(8,128)S(1)}, f32[2,64,128]{2,1,0:T(8,128)S(1)}, u32[]{:S(2)}, u32[]{:S(2)}) collective-permute-start(f32[2,64,128]{2,1,0:T(8,128)S(1)} %add.42), channel_id=1, source_target_pairs={{0,8},{8,0},{16,24},{24,16},{1,9},{9,1},{17,25},{25,17},{2,10},{10... | collective-permute-start | bytes 196616 | tf_op jit(solution)/shard_map/ppermute | solution.py:22

commit v3 on v2

--- a/solution.py
+++ b/solution.py
@@ -12,10 +12,13 @@
 CONTRACT_FIRST = ((0,), (0,))
 
 
-DONE = {'core_own': 1, 'mine0': 5, 'mine1': 4, 'mine2': 4, 'normed_other': 4, 'panel': 6, 'theirs0': 4, 'theirs1': None, 'theirs2': None}
-GATE = {'mine2': False, 'scalars': True}
+DONE = {'core_own': 2, 'mine0': 2, 'mine1': 4, 'mine2': 3, 'normed_other': 4, 'panel': 6, 'prep': 5, 'theirs0': 5, 'theirs1': None, 'theirs2': None}
+GATE = {'mine0': 0, 'mine2': False, 'scalars': True}
 SPLIT = True
-COST = [100000000000, 1000000000, 100000000000]
+RADIX = False
+MIX = False
+TIED = False
+COST = [100000000000, 100000000000, 100000000000]
 
 
 def xor_permute(value, axis, distance):
@@ -30,6 +33,25 @@
 def product(left, right, dims):
     dot = functools.partial(lax.dot_general, dimension_numbers=(dims, ((), ())), preferred_element_type=jnp.float32)
     return dot(left[0], right[0]) + (dot(left[0], right[1]) + dot(left[1], right[0]))
+
+
+def norm_kernel(scalars, dinv, lower, out):
+    half = out.shape[0]
+    core = scalars[scalars.shape[0] - 3]
+    for s in range(half):
+        out[s] = packed_product(split(dinv[core * half + s]), split(lower[s]), CONTRACT_FIRST)
+
+
+def packed_product(left, right, dims):
+    axis = 1 - dims[0][0]
+    rows, columns = left[0].shape[axis], right[0].shape[axis]
+    both = lax.dot_general(
+        jnp.concatenate(left, axis=axis),
+        jnp.concatenate(right, axis=axis),
+        (dims, ((), ())),
+        preferred_element_type=jnp.float32,
+    )
+    return both[:rows, :columns] + (both[:rows, columns:] + both[rows:, :columns])
 
 
 def update_kernel(n_col, slots, col_blocks, rows_blocks, scalars, dinv, *refs):
@@ -44,8 +66,10 @@
     for ref in (r_high, r_low, c_high, c_low):
         ref[...] = jnp.zeros_like(ref)
     for s in range(half):
-        lower = jnp.concatenate([halves[step][s] for step in range(n_col)], axis=1)
-        normed = product(split(dinv[core * half + s]), split(lower), CONTRACT_FIRST)
+        far = n_col // 2
+        lower = jnp.concatenate([halves[step][s] for step in range(far)], axis=1)
+        normed = packed_product(split(dinv[core * half + s]), split(lower), CONTRACT_FIRST)
+        normed = jnp.concatenate([normed] + [halves[step][s] for step in range(far, n_col)], axis=1)
         for step in range(n_col):
             for slot in range(slots):
                 first = (step * slots + slot) * BLK
@@ -111,8 +135,10 @@
     for ref in (r_high, r_low, c_high, c_low):
         ref[...] = jnp.zeros_like(ref)
     for s in range(half):
-        lower = jnp.concatenate([halves[step][s] for step in range(n_col)], axis=1)
-        normed = product(split(dinv[core * half + s]), split(lower), CONTRACT_FIRST)
+        far = n_col // 2
+        lower = jnp.concatenate([halves[step][s] for step in range(far)], axis=1)
+        normed = packed_product(split(dinv[core * half + s]), split(lower), CONTRACT_FIRST)
+        normed = jnp.concatenate([normed] + [halves[step][s] for step in range(far, n_col)], axis=1)
         for step in range(n_col):
             for slot in range(slots):
                 first = (step * slots + slot) * BLK
@@ -140,11 +166,21 @@
         out[i] = jnp.concatenate([blocks[i], blocks[i + half // 2]], axis=1)
 
 
-def panel_kernel(n_col, sibs, nbk, col_blocks, scalars, dinv, *refs):
+def put_rows(step, places, sources, col_blocks, a_high, a_low, rows=None):
+    for place, source in zip(places, sources):
+        for part in range(col_blocks):
+            inside = slice(part * BLK, (part + 1) * BLK)
+            high, low = split(source[:, inside] if rows is None else source[rows, inside])
+            a_high[place * col_blocks + part] = high
+            a_low[place * col_blocks + part] = low
+
+
+def prepare_kernel(n_col, sibs, nbk, col_blocks, scalars, dinv, *refs):
+    far = n_col // 2
     normed, own, partner = refs[:2], refs[2], refs[3]
-    mine, theirs = refs[4 : 3 + n_col], refs[3 + n_col : 2 + 2 * n_col]
-    panel_out, base_out, n_high, n_low, a_high, a_low = refs[2 + 2 * n_col :]
-    col_id, wave_id, core, block = scalars[scalars.shape[0] - 5 + 0], scalars[scalars.shape[0] - 5 + 1], scalars[scalars.shape[0] - 5 + 2], scalars[scalars.shape[0] - 5 + 4]
+    mine, theirs = refs[4 : 3 + far], refs[3 + far : 2 + 2 * far]
+    n_high, n_low, a_high, a_low, base_out = refs[2 + 2 * far :]
+    col_id, wave_id, core = scalars[scalars.shape[0] - 5 + 0], scalars[scalars.shape[0] - 5 + 1], scalars[scalars.shape[0] - 5 + 2]
     half = sibs // 2
     for ref, who in zip(normed, (core, 1 - core)):
         for slot in range(nbk):
@@ -152,27 +188,48 @@
             n_high[slot, pl.ds(who * half, half)] = high
             n_low[slot, pl.ds(who * half, half)] = low
     here = pl.ds(pl.multiple_of(col_id * BLK, BLK), BLK)
-    for step in range(n_col):
-        for group, first, pieces in ((wave_id, own, mine), (1 - wave_id, partner, theirs)):
-            for part in range(col_blocks):
-                columns = slice(part * BLK, (part + 1) * BLK)
-                high, low = split(pieces[step - 1][:, columns] if step else first[here, columns])
-                place = ((col_id ^ step) * 2 + group) * col_blocks + part
-                a_high[place] = high
-                a_low[place] = low
+    for step in range(far):
+        places = [step * 2 + wave_id, step * 2 + 1 - wave_id]
+        if step:
+            put_rows(step, places, (mine[step - 1], theirs[step - 1]), col_blocks, a_high, a_low)
+        else:
+            put_rows(step, places, (own, partner), col_blocks, a_high, a_low, here)
+    bases = []
+    for s in range(sibs):
+        factor = split(dinv[s])
+        bases.append(packed_product(factor, factor, CONTRACT_FIRST))
+    for i in range(half // 2):
+        for first in (0, half):
+            base_out[first // 2 + i] = jnp.concatenate([bases[first + i], bases[first + half // 2 + i]], axis=1)
+
+
+def panel_kernel(n_col, sibs, nbk, col_blocks, scalars, n_high, n_low, early_high, early_low, *refs):
+    far = n_col // 2
+    mine, theirs = refs[: n_col - far], refs[n_col - far : 2 * (n_col - far)]
+    panel_out, a_high, a_low, held, sems = refs[2 * (n_col - far) :]
+    col_id, wave_id, core, block = scalars[scalars.shape[0] - 5 + 0], scalars[scalars.shape[0] - 5 + 1], scalars[scalars.shape[0] - 5 + 2], scalars[scalars.shape[0] - 5 + 4]
+    group = 2 * col_blocks
+    for step in range(far):
+        for part in range(group):
+            a_high[(col_id ^ step) * group + part] = early_high[step * group + part]
+            a_low[(col_id ^ step) * group + part] = early_low[step * group + part]
+    for i, step in enumerate(range(far, n_col)):
+        places = [(col_id ^ step) * 2 + wave_id, (col_id ^ step) * 2 + 1 - wave_id]
+        put_rows(step, places, (mine[i], theirs[i]), col_blocks, a_high, a_low)
 
     def sibling(s, carry):
-        total = jnp.zeros((dinv.shape[1], BLK), jnp.float32)
+        total = jnp.zeros((n_high.shape[2], BLK), jnp.float32)
         found = False
         width = min(4, nbk)
         for first in range(0, nbk, width):
             places = [scalars[(s) * nbk + first + k] for k in range(width)]
             left = tuple(jnp.concatenate([ref[first + k, s] for k in range(width)], axis=1) for ref in (n_high, n_low))
             right = tuple(jnp.concatenate([ref[place] for place in places], axis=1) for ref in (a_high, a_low))
-            total = total + product(left, right, CONTRACT_LAST)
+            total = total + packed_product(left, right, CONTRACT_LAST)
             for place in places:
                 found = jnp.logical_or(found, place == block)
-        panel_out[s] = total * jnp.where(found, -1.0, 0.0)
+        held[s] = total * jnp.where(found, -1.0, 0.0)
+        pltpu.make_async_copy(held.at[s], panel_out.at[s], sems.at[s]).start()
         return carry
 
     if sibs * nbk <= 64:
@@ -180,13 +237,8 @@
             sibling(s, 0)
     else:
         lax.fori_loop(0, sibs, sibling, 0)
-    bases = []
     for s in range(sibs):
-        factor = split(dinv[s])
-        bases.append(product(factor, factor, CONTRACT_FIRST))
-    for i in range(half // 2):
-        for first in (0, half):
-            base_out[first // 2 + i] = jnp.concatenate([bases[first + i], bases[first + half // 2 + i]], axis=1)
+        pltpu.make_async_copy(held.at[s], panel_out.at[s], sems.at[s]).wait()
 
 
 def per_device(lower_panel, diag_inverse, ancestor_inverse, pattern):
@@ -208,13 +260,13 @@
     params = pltpu.CompilerParams(vmem_limit_bytes=min(60, 12 + 12 * size) * mib)
     ids = jnp.stack([col_id, wave_id, core, row_id, row_id * n_col + col_id]).astype(jnp.int32)
 
-    def call(kernel, out_shape, operands, scratch, flops):
+    def call(kernel, out_shape, operands, scratch, flops, out_space=vmem):
         moved = sum(x.size * 4 for x in operands)
         return pl.pallas_call(
             kernel,
             out_shape=out_shape,
             in_specs=[smem] + [vmem] * len(operands),
-            out_specs=jax.tree.map(lambda _: vmem, out_shape),
+            out_specs=jax.tree.map(lambda _: out_space, out_shape),
             scratch_shapes=scratch,
             compiler_params=params,
             cost_estimate=pl.CostEstimate(flops=flops, bytes_accessed=(moved if flops > 10 else 1), transcendentals=0),
@@ -228,6 +280,8 @@
         return value
 
     def due(name):
+        if name.startswith("prep"):
+            return DONE.get("prep")
         if name[-1].isdigit():
             stem = name.rstrip("0123456789")
             return DONE.get(stem + str(min(int(name[len(stem) :]), 2)))
@@ -249,24 +303,42 @@
         half_panel, *chunks = lax.optimization_barrier((half_panel, *chunks))
         halves[0] = half_panel
         halves[far] = xor_permute(half_panel, "col", far)
-    gated = [i for i in range(n_col - 1) if GATE.get("mine" + str(min(i, 2)))]
+    gated = [i for i in range(n_col - 1) if GATE.get("mine" + str(min(i, 2))) == 1]
     if gated:
         halves[far], *held = lax.optimization_barrier((halves[far], *[chunks[i] for i in gated]))
         for i, chunk in zip(gated, held):
             chunks[i] = chunk
-    mine = [xor_permute(chunk, "col", step) for step, chunk in enumerate(chunks, 1)]
-    late.update({"mine" + str(i): x for i, x in enumerate(mine)})
-    late.update({"theirs" + str(i): xor_permute(x, "wave", 1) for i, x in enumerate(mine)})
+    held_back = [i for i in range(n_col - 1) if GATE.get("mine" + str(min(i, 2))) == 2]
+    for i in range(n_col - 1):
+        if i not in held_back:
+            late["mine" + str(i)] = xor_permute(chunks[i], "col", i + 1)
+            if not TIED:
+                late["theirs" + str(i)] = xor_permute(late["mine" + str(i)], "wave", 1)
     late["core_own"] = xor_permute(ancestor_inverse, "row", 1)
     scalars = jnp.concatenate([pattern.reshape(-1), ids])
     if GATE.get("scalars"):
         halves[far], scalars = lax.optimization_barrier((halves[far], scalars))
     halves[far] = tie(0, halves[far])
+    halves[far] = call(norm_kernel, jax.ShapeDtypeStruct(half_panel.shape, f32), [diag_inverse, halves[far]], [], 100000000000)
+    halves[far] = tie(8, halves[far])
+    near = halves[0]
+    if GATE.get("near") == 1:
+        halves[far], near = lax.optimization_barrier((halves[far], near))
+    if GATE.get("near") == 2:
+        near, *_ = lax.optimization_barrier((near, *chunks))
+    if GATE.get("near") == 3:
+        near, late["core_own"] = lax.optimization_barrier((near, late["core_own"]))
     bit = far // 2
     while bit:
         for step in list(halves):
-            halves[step ^ bit] = xor_permute(halves[step], "col", bit)
+            halves[step ^ bit] = xor_permute(halves[step] if step else near, "col", bit)
         bit //= 2
+    if held_back:
+        halves[n_col - 1], *held = lax.optimization_barrier((halves[n_col - 1], *[chunks[i] for i in held_back]))
+        for i, chunk in zip(held_back, held):
+            late["mine" + str(i)] = xor_permute(chunk, "col", i + 1)
+            if not TIED:
+                late["theirs" + str(i)] = xor_permute(late["mine" + str(i)], "wave", 1)
     partner, *tied = lax.optimization_barrier((partner, *[halves[step] for step in range(n_col)]))
     halves = dict(enumerate(tied))
     partner = tie(1, partner)
@@ -312,29 +384,64 @@
         )
         late["normed_other"] = xor_permute(normed, "row", 1)
     total = tie(3, total)
-    bit = 2
-    while bit < n_row:
+    bits = [2**i for i in range(1, n_row.bit_length() - 1)]
+    if RADIX:
+        last = bits.pop()
+    for bit in bits:
         total = total + xor_permute(total, "row", bit)
-        bit *= 2
     total = tie(4, total)
-    bit = 1
-    while bit < n_col:
-        total = total + xor_permute(total, "col", bit)
-        bit *= 2
-        if bit < n_col:
+    early = [diag_inverse, normed, late["normed_other"], ancestor_inverse, partner]
+    early += [late[name + str(i)] for name in ("mine", "theirs") for i in range(far - 1)]
+    prepared = call(
+        functools.partial(prepare_kernel, n_col, sibs, nbk, col_blocks),
+        (
+            jax.ShapeDtypeStruct((nbk, sibs, width, BLK), bf16),
+            jax.ShapeDtypeStruct((nbk, sibs, width, BLK), bf16),
+            jax.ShapeDtypeStruct((n_blocks // 2, BLK, BLK), bf16),
+            jax.ShapeDtypeStruct((n_blocks // 2, BLK, BLK), bf16),
+            jax.ShapeDtypeStruct((half, width, 2 * width), f32),
+        ),
+        early,
+        [],
+        COST[3] if len(COST) > 3 else 10**7,
+    )
+    late.update({"prep" + str(i): x for i, x in enumerate(prepared)})
+    bits = [2**i for i in range(n_col.bit_length() - 1)]
+    if RADIX:
+        first = bits.pop(0)
+        both = [(r * n_col + c, (r ^ last) * n_col + (c ^ first)) for r in range(n_row) for c in range(n_col)]
+        steps = [
+            xor_permute(total, "row", last),
+            xor_permute(total, "col", first),
+            lax.ppermute(total, ("row", "col"), both),
+        ]
+        total = (total + steps[0]) + (steps[1] + steps[2])
+        total = tie(5, total)
+    for i, bit in enumerate(bits):
+        if MIX:
+            turn = (bit, bits[len(bits) - 1 - i])
+            pairs = [(r * n_col + c, r * n_col + (c ^ turn[r % 2])) for r in range(n_row) for c in range(n_col)]
+            total = total + lax.ppermute(total, ("row", "col"), pairs)
+        else:
+            total = total + xor_permute(total, "col", bit)
+        if i == 0 and not RADIX:
             total = tie(5, total)
     total = tie(6, total)
-    pieces = [late["mine" + str(i)] for i in range(n_col - 1)] + [late["theirs" + str(i)] for i in range(n_col - 1)]
-    panel, base = call(
+    panel = call(
         functools.partial(panel_kernel, n_col, sibs, nbk, col_blocks),
-        (
-            jax.ShapeDtypeStruct((sibs, width, BLK), f32),
-            jax.ShapeDtypeStruct((half, width, 2 * width), f32),
-        ),
-        [diag_inverse, normed, late["normed_other"], ancestor_inverse, partner] + pieces,
-        [pltpu.VMEM((nbk, sibs, width, BLK), bf16)] * 2 + [pltpu.VMEM((n_blocks, BLK, BLK), bf16)] * 2,
+        jax.ShapeDtypeStruct((sibs, width, BLK), f32),
+        [late["prep" + str(i)] for i in range(4)]
+        + [late[name + str(i)] for name in ("mine", "theirs") for i in range(far - 1, n_col - 1)],
+        [
+            pltpu.VMEM((n_blocks, BLK, BLK), bf16),
+            pltpu.VMEM((n_blocks, BLK, BLK), bf16),
+            pltpu.VMEM((sibs, width, BLK), f32),
+            pltpu.SemaphoreType.DMA((sibs,)),
+        ],
         COST[1],
+        pl.BlockSpec(memory_space=pl.ANY),
     )
+    base = late["prep4"]
     if DONE.get("panel") == 6:
         total, panel = lax.optimization_barrier((total, panel))
     other = xor_permute(total, "row", 1)

time: 43.8 us -> 43.2 us (0.986)
  waiting for transfers between devices: 12 us -> 8.31 us
  Pallas kernels: 7.61 us -> 9.5 us
  local copies, waits for them, and re-layouts: 2.84 us -> 3.76 us
    ppermute x17, waiting for transfers between devices: 12 us -> 8.31 us  [xor_permute(): lax.ppermute(value, axis, [(i, i ^ distance) for i in range(lax.axis_size...]
    pallas_call x3 -> x5, Pallas kernels: 7.61 us -> 9.5 us  [call(): pl.pallas_call(kernel, out_shape=out_shape, in_specs=[smem] + [vmem] * le...]
    unnamed x9, local copies, waits for them, and re-layouts: 0.78 us -> 1.7 us
  transfers between devices with their start and end apart: 17 -> 17, of which waited for: 6 -> 8; matrix products, arithmetic and copies ran while one was open for 5% -> 5% of each run, Pallas kernels for 17% -> 22%
where the time goes in v3:
time: 43.2 us; the launch traced here: 43 us
  starting transfers between devices  19.9 us (46%)
  Pallas kernels  9.5 us (22%)
  waiting for transfers between devices  8.31 us (19%)
  local copies, waits for them, and re-layouts  3.76 us (9%)
  other arithmetic  0.77 us (2%)
  between operations  0.77 us (2%)
    ppermute x17, starting transfers between devices, xor_permute(): lax.ppermute(value, axis, [(i, i ^ distance) for i in range(lax.axis_size...  19.9 us
    pallas_call x5, Pallas kernels, call(): pl.pallas_call(kernel, out_shape=out_shape, in_specs=[smem] + [vmem] * le...  9.5 us
    ppermute x17, waiting for transfers between devices, xor_permute(): lax.ppermute(value, axis, [(i, i ^ distance) for i in range(lax.axis_size...  8.31 us
    dynamic_slice x1, local copies, waits for them, and re-layouts, per_device(): lax.dynamic_slice_in_dim(ancestor_inverse, (col_id ^ step) * own_rows, ow...  1.8 us
    unnamed x9, local copies, waits for them, and re-layouts  1.7 us
  transfers between devices with their start and end apart: 17, of which 8 were waited for; matrix products, arithmetic and copies ran while one was open for 5% of the time, Pallas kernels for 22%

profile of v3, /device:TPU:0, one launch (start us, length us, event | category | flops | bytes accessed | tf_op | source)
XLA Modules:
  0.0 43.0 jit_solution(17933209282302060491)
XLA Ops:
  0.7 0.9 %copy-done = f32[8,64,128]{2,1,0:T(8,128)S(1)} copy-done((f32[8,64,128]{2,1,0:T(8,128)S(1)}, f32[8,64,128]{2,1,0:T(8,128)}, u32[]{:S(2)}) %copy-start) | copy-done | bytes 262168
  1.6 4.1 %collective-permute-start = (f32[4,64,128]{2,1,0:T(8,128)S(1)}, f32[4,64,128]{2,1,0:T(8,128)S(1)}, u32[]{:S(2)}, u32[]{:S(2)}) collective-permute-start(f32[4,64,128]{2,1,0:T(8,128)S(1)} %constant_dynamic-slice_fusion.3.refs_0_), channel_id=1, source_target_pairs={{0,4},{2,6},{4,0},{6,2},{1,5},{3,7},{5,1},{7,3},{8,12},{10,14},{12... | collective-permute-start | bytes 393224 | tf_op jit(solution)/shard_map/ppermute | solution.py:25
  5.7 1.6 %collective-permute-start.2 = (f32[4,64,128]{2,1,0:T(8,128)S(1)}, f32[4,64,128]{2,1,0:T(8,128)S(1)}, u32[]{:S(2)}, u32[]{:S(2)}) collective-permute-start(f32[4,64,128]{2,1,0:T(8,128)S(1)} %constant_dynamic-slice_fusion.3.refs_0_), channel_id=1, source_target_pairs={{0,2},{2,0},{4,6},{6,4},{1,3},{3,1},{5,7},{7,5},{8,10},{10,8},{12,... | collective-permute-start | bytes 393224 | tf_op jit(solution)/shard_map/ppermute | solution.py:25
  7.3 1.5 %collective-permute-start.1 = (f32[512,256]{1,0:T(8,128)}, f32[512,256]{1,0:T(8,128)S(1)}, u32[]{:S(2)}, u32[]{:S(2)}) collective-permute-start(f32[512,256]{1,0:T(8,128)} %refs_2_.1), channel_id=1, source_target_pairs={{0,1},{1,0},{2,3},{3,2},{4,5},{5,4},{6,7},{7,6},{8,9},{9,8},{10,11... | collective-permute-start | bytes 1572872 | tf_op jit(solution)/shard_map/ppermute | solution.py:25
  8.8 1.8 %constant_dynamic-slice_fusion = (f32[128,256]{1,0:T(8,128)}, f32[128,256]{1,0:T(8,128)}, f32[128,256]{1,0:T(8,128)S(1)}) fusion(f32[512,256]{1,0:T(8,128)} %refs_2_.1, s32[]{:T(128)S(6)} %select_n.35, s32[]{:T(128)S(6)} %select_n.34, s32[]{:T(128)S(6)} %select_n.33), kind=kLoop, calls=%fused_computation.3 | loop fusion | bytes 786444 | tf_op jit(solution)/shard_map/dynamic_slice | solution.py:300
  11.0 0.7 %copy-done.3 = s32[8,4]{0,1:T(4,128)S(1)} copy-done((s32[8,4]{0,1:T(4,128)S(1)}, s32[8,4]{0,1:T(4,128)}, u32[]{:S(2)}) %copy-start.3) | copy-done | bytes 152
  12.1 0.9 %shard_map.59.refs_2_ = f32[4,64,128]{2,1,0:T(8,128)S(1)} custom-call(s32[37]{0:T(128)S(1)} %concatenate.6.scalars, f32[8,64,64]{2,1,0:T(8,128)S(1)} %copy-done.2, f32[4,64,128]{2,1,0:T(8,128)S(1)} %collective-permute-done.lower), custom_call_target="tpu_custom_call" | custom-call | flops 99999997952 | bytes 262144 | tf_op jit(solution)/shard_map/pallas_call | solution.py:265
  13.0 1.5 %collective-permute-start.3 = (f32[4,64,128]{2,1,0:T(8,128)S(1)}, f32[4,64,128]{2,1,0:T(8,128)S(1)}, u32[]{:S(2)}, u32[]{:S(2)}) collective-permute-start(f32[4,64,128]{2,1,0:T(8,128)S(1)} %shard_map.59.refs_2_), channel_id=1, source_target_pairs={{0,2},{2,0},{4,6},{6,4},{1,3},{3,1},{5,7},{7,5},{8,10},{10,8},{12,... | collective-permute-start | bytes 393224 | tf_op jit(solution)/shard_map/ppermute | solution.py:25
  14.5 2.2 %collective-permute-start.7 = (f32[128,256]{1,0:T(8,128)}, f32[128,256]{1,0:T(8,128)}, u32[]{:S(2)}, u32[]{:S(2)}) collective-permute-start(f32[128,256]{1,0:T(8,128)} %get-tuple-element.69), channel_id=1, source_target_pairs={{0,6},{2,4},{4,2},{6,0},{1,7},{3,5},{5,3},{7,1},{8,14},{10,12},{12... | collective-permute-start | bytes 393224 | tf_op jit(solution)/shard_map/ppermute | solution.py:25
  17.2 2.1 %collective-permute-done.3.refs_3_ = f32[4,64,128]{2,1,0:T(8,128)S(1)} collective-permute-done((f32[4,64,128]{2,1,0:T(8,128)S(1)}, f32[4,64,128]{2,1,0:T(8,128)S(1)}, u32[]{:S(2)}, u32[]{:S(2)}) %collective-permute-start.3) | collective-permute-done | bytes 131104 | tf_op jit(solution)/shard_map/ppermute | solution.py:25
  19.8 0.8 %collective-permute-done.1.partner.refs_3_ = f32[512,256]{1,0:T(8,128)S(1)} collective-permute-done((f32[512,256]{1,0:T(8,128)}, f32[512,256]{1,0:T(8,128)S(1)}, u32[]{:S(2)}, u32[]{:S(2)}) %collective-permute-start.1) | collective-permute-done | bytes 524320 | tf_op jit(solution)/shard_map/ppermute | solution.py:25
  20.6 2.4 %shard_map.60 = (f32[256,256]{1,0:T(8,128)S(1)}, f32[4,4,64,128]{3,2,1,0:T(8,128)S(1)}, bf16[9,256,128]{2,1,0:T(8,128)(2,1)S(1)}, bf16[9,256,128]{2,1,0:T(8,128)...) custom-call(s32[37]{0:T(128)S(1)} %concatenate.6.scalars, f32[8,64,64]{2,1,0:T(8,128)S(1)} %copy-done.2, ...), custom_call_target="tpu_custom_call" | custom-call | flops 99999997952 | bytes 1703936 | tf_op jit(solution)/shard_map/pallas_call | solution.py:265
  23.0 0.6 %collective-permute-start.10 = (f32[4,4,64,128]{3,2,1,0:T(8,128)S(1)}, f32[4,4,64,128]{3,2,1,0:T(8,128)S(1)}, u32[]{:S(2)}, u32[]{:S(2)}) collective-permute-start(f32[4,4,64,128]{3,2,1,0:T(8,128)S(1)} %get-tuple-element.49.refs_0_), channel_id=1, source_target_pairs={{0,8},{8,0},{16,24},{24,16},{1,9},{9,1},{17,25},{25,17},{2,10},{10... | collective-permute-start | bytes 1572872 | tf_op jit(solution)/shard_map/ppermute | solution.py:25
  23.6 1.9 %shard_map.61 = f32[2,64,128]{2,1,0:T(8,128)S(1)} custom-call(s32[37]{0:T(128)S(1)} %concatenate.6.scalars, f32[256,256]{1,0:T(8,128)S(1)} %get-tuple-element.41.total, bf16[9,256,128]{2,1,0:T(8,128)(2,1)S(1)} %get-tuple-element.42.r_high, bf16[9,256,128]{2,1,0:T(8,128)(2,1)S(1)} %get-tuple-element.43.r_low, ...), custom_call_target="tpu_custom_call" | custom-call | flops 99999997952 | bytes 4980736 | tf_op jit(solution)/shard_map/pallas_call | solution.py:265
  25.5 1.6 %collective-permute-start.8 = (f32[2,64,128]{2,1,0:T(8,128)S(1)}, f32[2,64,128]{2,1,0:T(8,128)S(1)}, u32[]{:S(2)}, u32[]{:S(2)}) collective-permute-start(f32[2,64,128]{2,1,0:T(8,128)S(1)} %shard_map.61), channel_id=1, source_target_pairs={{0,16},{8,24},{16,0},{24,8},{1,17},{9,25},{17,1},{25,9},{2,18},{10... | collective-permute-start | bytes 196616 | tf_op jit(solution)/shard_map/ppermute | solution.py:25
  27.1 2.1 %collective-permute-done.9.refs_0_ = f32[128,256]{1,0:T(8,128)} collective-permute-done((f32[128,256]{1,0:T(8,128)}, f32[128,256]{1,0:T(8,128)}, u32[]{:S(2)}, u32[]{:S(2)}) %collective-permute-start.9) | collective-permute-done | bytes 131104 | tf_op jit(solution)/shard_map/ppermute | solution.py:25
  29.2 1.5 %collective-permute-start.14 = (f32[128,256]{1,0:T(8,128)}, f32[128,256]{1,0:T(8,128)S(1)}, u32[]{:S(2)}, u32[]{:S(2)}) collective-permute-start(f32[128,256]{1,0:T(8,128)} %collective-permute-done.9.refs_0_), channel_id=1, source_target_pairs={{0,1},{1,0},{2,3},{3,2},{4,5},{5,4},{6,7},{7,6},{8,9},{9,8},{10,11... | collective-permute-start | bytes 393224 | tf_op jit(solution)/shard_map/ppermute | solution.py:25
  31.3 1.0 %collective-permute-start.11 = (f32[2,64,128]{2,1,0:T(8,128)S(1)}, f32[2,64,128]{2,1,0:T(8,128)S(1)}, u32[]{:S(2)}, u32[]{:S(2)}) collective-permute-start(f32[2,64,128]{2,1,0:T(8,128)S(1)} %add.39), channel_id=1, source_target_pairs={{0,2},{2,0},{4,6},{6,4},{1,3},{3,1},{5,7},{7,5},{8,10},{10,8},{12,... | collective-permute-start | bytes 196616 | tf_op jit(solution)/shard_map/ppermute | solution.py:25
  32.2 1.7 %shard_map.62 = (bf16[4,8,64,128]{3,2,1,0:T(8,128)(2,1)S(1)}, bf16[4,8,64,128]{3,2,1,0:T(8,128)(2,1)S(1)}, bf16[8,128,128]{2,1,0:T(8,128)(2,1)S(1)}, bf16[8,128,128]{2,1,0:T(8,128)(2,1)S(1)}, f32[4,64,128]{2,1,0:T(8,128)S(1)}) custom-call(s32[37]{0:T(128)S(1)} %concatenate.6.scalars, f32[8,64,64]{2,1,0:T(8,128)S(1)} %copy-done.2, ...), custom_call_target="tpu_custom_call" | custom-call | flops 10000000 | bytes 2490368 | tf_op jit(solution)/shard_map/pallas_call | solution.py:265
  33.9 1.6 %collective-permute-done.11 = f32[2,64,128]{2,1,0:T(8,128)S(1)} collective-permute-done((f32[2,64,128]{2,1,0:T(8,128)S(1)}, f32[2,64,128]{2,1,0:T(8,128)S(1)}, u32[]{:S(2)}, u32[]{:S(2)}) %collective-permute-start.11) | collective-permute-done | bytes 65568 | tf_op jit(solution)/shard_map/ppermute | solution.py:25
  35.6 2.6 %collective-permute-start.13 = (f32[2,64,128]{2,1,0:T(8,128)S(1)}, f32[2,64,128]{2,1,0:T(8,128)S(1)}, u32[]{:S(2)}, u32[]{:S(2)}) collective-permute-start(f32[2,64,128]{2,1,0:T(8,128)S(1)} %add.41), channel_id=1, source_target_pairs={{0,4},{2,6},{4,0},{6,2},{1,5},{3,7},{5,1},{7,3},{8,12},{10,14},{12... | collective-permute-start | bytes 196616 | tf_op jit(solution)/shard_map/ppermute | solution.py:25
  38.2 2.6 %shard_map.63 = f32[8,64,128]{2,1,0:T(8,128)} custom-call(s32[37]{0:T(128)S(1)} %concatenate.6.scalars, bf16[4,8,64,128]{3,2,1,0:T(8,128)(2,1)S(1)} %get-tuple-element.59.n_high, bf16[4,8,64,128]{3,2,1,0:T(8,128)(2,1)S(1)} %get-tuple-element.60.n_low, bf16[8,128,128]{2,1,0:T(8,128)(2,1)S(1)} %get-tuple-element.61.early_high, ...), custom_call_target="tpu_custom_call" | custom-call | flops 99999997952 | bytes 3670016 | tf_op jit(solution)/shard_map/pallas_call | solution.py:265
  40.9 1.2 %collective-permute-done.16 = f32[2,64,128]{2,1,0:T(8,128)S(1)} collective-permute-done((f32[2,64,128]{2,1,0:T(8,128)S(1)}, f32[2,64,128]{2,1,0:T(8,128)S(1)}, u32[]{:S(2)}, u32[]{:S(2)}) %collective-permute-start.16) | collective-permute-done | bytes 65568 | tf_op jit(solution)/shard_map/ppermute | solution.py:25
  42.3 0.7 %pad_maximum_fusion = f32[8,64,64]{2,1,0:T(8,128)} fusion(f32[2,64,64]{2,1,0:T(8,128)S(1)} %get-tuple-element.77, f32[2,64,64]{2,1,0:T(8,128)S(1)} %get-tuple-element.78, f32[2,64,64]{2,1,0:T(8,128)S(1)} %get-tuple-element.74, f32[2,64,64]{2,1,0:T(8,128)S(1)} %get-tuple-element.73), kind=kLoop, calls=%fused_computation | loop fusion | flops 98304 | bytes 262144 | tf_op jit(solution)/shard_map/concatenate | solution.py:452
  (34 shorter events, 2.8 us)
Async XLA Ops:
  0.6 1.0 %copy-start = (f32[8,64,128]{2,1,0:T(8,128)S(1)}, f32[8,64,128]{2,1,0:T(8,128)}, u32[]{:S(2)}) copy-start(f32[8,64,128]{2,1,0:T(8,128)} %param.4) | copy-start | bytes 786436
  1.6 10.5 %collective-permute-start = (f32[4,64,128]{2,1,0:T(8,128)S(1)}, f32[4,64,128]{2,1,0:T(8,128)S(1)}, u32[]{:S(2)}, u32[]{:S(2)}) collective-permute-start(f32[4,64,128]{2,1,0:T(8,128)S(1)} %constant_dynamic-slice_fusion.3.refs_0_), channel_id=1, source_target_pairs={{0,4},{2,6},{4,0},{6,2},{1,5},{3,7},{5,1},{7,3},{8,12},{10,14},{12... | collective-permute-start | bytes 393224 | tf_op jit(solution)/shard_map/ppermute | solution.py:25
  5.7 8.8 %collective-permute-start.2 = (f32[4,64,128]{2,1,0:T(8,128)S(1)}, f32[4,64,128]{2,1,0:T(8,128)S(1)}, u32[]{:S(2)}, u32[]{:S(2)}) collective-permute-start(f32[4,64,128]{2,1,0:T(8,128)S(1)} %constant_dynamic-slice_fusion.3.refs_0_), channel_id=1, source_target_pairs={{0,2},{2,0},{4,6},{6,4},{1,3},{3,1},{5,7},{7,5},{8,10},{10,8},{12,... | collective-permute-start | bytes 393224 | tf_op jit(solution)/shard_map/ppermute | solution.py:25
  7.3 13.3 %collective-permute-start.1 = (f32[512,256]{1,0:T(8,128)}, f32[512,256]{1,0:T(8,128)S(1)}, u32[]{:S(2)}, u32[]{:S(2)}) collective-permute-start(f32[512,256]{1,0:T(8,128)} %refs_2_.1), channel_id=1, source_target_pairs={{0,1},{1,0},{2,3},{3,2},{4,5},{5,4},{6,7},{7,6},{8,9},{9,8},{10,11... | collective-permute-start | bytes 1572872 | tf_op jit(solution)/shard_map/ppermute | solution.py:25
  8.8 11.8 %collective-permute-start.4 = (f32[512,256]{1,0:T(8,128)}, f32[512,256]{1,0:T(8,128)S(1)}, u32[]{:S(2)}, u32[]{:S(2)}) collective-permute-start(f32[512,256]{1,0:T(8,128)} %refs_2_.1), channel_id=1, source_target_pairs={{0,8},{8,0},{16,24},{24,16},{1,9},{9,1},{17,25},{25,17},{2,10},{10... | collective-permute-start | bytes 1572872 | tf_op jit(solution)/shard_map/ppermute | solution.py:25
  8.8 3.3 %copy-start.2 = (f32[8,64,64]{2,1,0:T(8,128)S(1)}, f32[8,64,64]{2,1,0:T(8,128)}, u32[]{:S(2)}) copy-start(f32[8,64,64]{2,1,0:T(8,128)} %dinv.5) | copy-start | bytes 393220
  10.6 6.4 %collective-permute-start.6 = (f32[128,256]{1,0:T(8,128)S(1)}, f32[128,256]{1,0:T(8,128)}, u32[]{:S(2)}, u32[]{:S(2)}) collective-permute-start(f32[128,256]{1,0:T(8,128)S(1)} %get-tuple-element.70), channel_id=1, source_target_pairs={{0,2},{2,0},{4,6},{6,4},{1,3},{3,1},{5,7},{7,5},{8,10},{10,8},{12,... | collective-permute-start | bytes 393224 | tf_op jit(solution)/shard_map/ppermute | solution.py:25
  11.0 0.7 %copy-start.3 = (s32[8,4]{0,1:T(4,128)S(1)}, s32[8,4]{0,1:T(4,128)}, u32[]{:S(2)}) copy-start(s32[8,4]{0,1:T(4,128)} %param.7) | copy-start | bytes 388
  12.0 8.6 %copy-start.1 = (f32[512,256]{1,0:T(8,128)S(1)}, f32[512,256]{1,0:T(8,128)}, u32[]{:S(2)}) copy-start(f32[512,256]{1,0:T(8,128)} %refs_2_.1) | copy-start | bytes 1572868
  13.0 6.3 %collective-permute-start.3 = (f32[4,64,128]{2,1,0:T(8,128)S(1)}, f32[4,64,128]{2,1,0:T(8,128)S(1)}, u32[]{:S(2)}, u32[]{:S(2)}) collective-permute-start(f32[4,64,128]{2,1,0:T(8,128)S(1)} %shard_map.59.refs_2_), channel_id=1, source_target_pairs={{0,2},{2,0},{4,6},{6,4},{1,3},{3,1},{5,7},{7,5},{8,10},{10,8},{12,... | collective-permute-start | bytes 393224 | tf_op jit(solution)/shard_map/ppermute | solution.py:25
  14.5 11.0 %collective-permute-start.7 = (f32[128,256]{1,0:T(8,128)}, f32[128,256]{1,0:T(8,128)}, u32[]{:S(2)}, u32[]{:S(2)}) collective-permute-start(f32[128,256]{1,0:T(8,128)} %get-tuple-element.69), channel_id=1, source_target_pairs={{0,6},{2,4},{4,2},{6,0},{1,7},{3,5},{5,3},{7,1},{8,14},{10,12},{12... | collective-permute-start | bytes 393224 | tf_op jit(solution)/shard_map/ppermute | solution.py:25
  17.0 12.2 %collective-permute-start.9 = (f32[128,256]{1,0:T(8,128)}, f32[128,256]{1,0:T(8,128)}, u32[]{:S(2)}, u32[]{:S(2)}) collective-permute-start(f32[128,256]{1,0:T(8,128)} %get-tuple-element.68), channel_id=1, source_target_pairs={{0,4},{2,6},{4,0},{6,2},{1,5},{3,7},{5,1},{7,3},{8,12},{10,14},{12... | collective-permute-start | bytes 393224 | tf_op jit(solution)/shard_map/ppermute | solution.py:25
  19.3 12.9 %collective-permute-start.12 = (f32[128,256]{1,0:T(8,128)}, f32[128,256]{1,0:T(8,128)}, u32[]{:S(2)}, u32[]{:S(2)}) collective-permute-start(f32[128,256]{1,0:T(8,128)} %collective-permute-done.6.refs_4_), channel_id=1, source_target_pairs={{0,1},{1,0},{2,3},{3,2},{4,5},{5,4},{6,7},{7,6},{8,9},{9,8},{10,11... | collective-permute-start | bytes 393224 | tf_op jit(solution)/shard_map/ppermute | solution.py:25
  20.6 3.0 %collective-permute-start.5 = (f32[512,256]{1,0:T(8,128)S(1)}, f32[512,256]{1,0:T(8,128)S(1)}, u32[]{:S(2)}, u32[]{:S(2)}) collective-permute-start(f32[512,256]{1,0:T(8,128)S(1)} %collective-permute-done.1.partner.refs_3_), channel_id=1, source_target_pairs={{0,8},{8,0},{16,24},{24,16},{1,9},{9,1},{17,25},{25,17},{2,10},{10... | collective-permute-start | bytes 1572872 | tf_op jit(solution)/shard_map/ppermute | solution.py:25
  23.0 8.2 %collective-permute-start.10 = (f32[4,4,64,128]{3,2,1,0:T(8,128)S(1)}, f32[4,4,64,128]{3,2,1,0:T(8,128)S(1)}, u32[]{:S(2)}, u32[]{:S(2)}) collective-permute-start(f32[4,4,64,128]{3,2,1,0:T(8,128)S(1)} %get-tuple-element.49.refs_0_), channel_id=1, source_target_pairs={{0,8},{8,0},{16,24},{24,16},{1,9},{9,1},{17,25},{25,17},{2,10},{10... | collective-permute-start | bytes 1572872 | tf_op jit(solution)/shard_map/ppermute | solution.py:25
  25.5 5.7 %collective-permute-start.8 = (f32[2,64,128]{2,1,0:T(8,128)S(1)}, f32[2,64,128]{2,1,0:T(8,128)S(1)}, u32[]{:S(2)}, u32[]{:S(2)}) collective-permute-start(f32[2,64,128]{2,1,0:T(8,128)S(1)} %shard_map.61), channel_id=1, source_target_pairs={{0,16},{8,24},{16,0},{24,8},{1,17},{9,25},{17,1},{25,9},{2,18},{10... | collective-permute-start | bytes 196616 | tf_op jit(solution)/shard_map/ppermute | solution.py:25
  29.2 9.0 %collective-permute-start.14 = (f32[128,256]{1,0:T(8,128)}, f32[128,256]{1,0:T(8,128)S(1)}, u32[]{:S(2)}, u32[]{:S(2)}) collective-permute-start(f32[128,256]{1,0:T(8,128)} %collective-permute-done.9.refs_0_), channel_id=1, source_target_pairs={{0,1},{1,0},{2,3},{3,2},{4,5},{5,4},{6,7},{7,6},{8,9},{9,8},{10,11... | collective-permute-start | bytes 393224 | tf_op jit(solution)/shard_map/ppermute | solution.py:25
  30.7 7.4 %collective-permute-start.15 = (f32[128,256]{1,0:T(8,128)}, f32[128,256]{1,0:T(8,128)S(1)}, u32[]{:S(2)}, u32[]{:S(2)}) collective-permute-start(f32[128,256]{1,0:T(8,128)} %collective-permute-done.7.refs_1_), channel_id=1, source_target_pairs={{0,1},{1,0},{2,3},{3,2},{4,5},{5,4},{6,7},{7,6},{8,9},{9,8},{10,11... | collective-permute-start | bytes 393224 | tf_op jit(solution)/shard_map/ppermute | solution.py:25
  31.3 4.3 %collective-permute-start.11 = (f32[2,64,128]{2,1,0:T(8,128)S(1)}, f32[2,64,128]{2,1,0:T(8,128)S(1)}, u32[]{:S(2)}, u32[]{:S(2)}) collective-permute-start(f32[2,64,128]{2,1,0:T(8,128)S(1)} %add.39), channel_id=1, source_target_pairs={{0,2},{2,0},{4,6},{6,4},{1,3},{3,1},{5,7},{7,5},{8,10},{10,8},{12,... | collective-permute-start | bytes 196616 | tf_op jit(solution)/shard_map/ppermute | solution.py:25
  35.6 5.2 %collective-permute-start.13 = (f32[2,64,128]{2,1,0:T(8,128)S(1)}, f32[2,64,128]{2,1,0:T(8,128)S(1)}, u32[]{:S(2)}, u32[]{:S(2)}) collective-permute-start(f32[2,64,128]{2,1,0:T(8,128)S(1)} %add.41), channel_id=1, source_target_pairs={{0,4},{2,6},{4,0},{6,2},{1,5},{3,7},{5,1},{7,3},{8,12},{10,14},{12... | collective-permute-start | bytes 196616 | tf_op jit(solution)/shard_map/ppermute | solution.py:25
  40.8 1.3 %collective-permute-start.16 = (f32[2,64,128]{2,1,0:T(8,128)S(1)}, f32[2,64,128]{2,1,0:T(8,128)S(1)}, u32[]{:S(2)}, u32[]{:S(2)}) collective-permute-start(f32[2,64,128]{2,1,0:T(8,128)S(1)} %add.42), channel_id=1, source_target_pairs={{0,8},{8,0},{16,24},{24,16},{1,9},{9,1},{17,25},{25,17},{2,10},{10... | collective-permute-start | bytes 196616 | tf_op jit(solution)/shard_map/ppermute | solution.py:25

commit v4 on v3

--- a/solution.py
+++ b/solution.py
@@ -12,7 +12,7 @@
 CONTRACT_FIRST = ((0,), (0,))
 
 
-DONE = {'core_own': 2, 'mine0': 2, 'mine1': 4, 'mine2': 3, 'normed_other': 4, 'panel': 6, 'prep': 5, 'theirs0': 5, 'theirs1': None, 'theirs2': None}
+DONE = {'core_own': 2, 'mine0': 2, 'mine1': 5, 'mine2': 3, 'normed_other': 4, 'panel': 6, 'prep': None, 'theirs0': 5, 'theirs1': None, 'theirs2': None}
 GATE = {'mine0': 0, 'mine2': False, 'scalars': True}
 SPLIT = True
 RADIX = False

time: 43.2 us -> 43.2 us (level)
  no operation moved by 1% of the time
where the time goes in v4:
time: 43.2 us; the launch traced here: 43 us
  starting transfers between devices  19.9 us (46%)
  Pallas kernels  9.5 us (22%)
  waiting for transfers between devices  8.31 us (19%)
  local copies, waits for them, and re-layouts  3.76 us (9%)
  other arithmetic  0.77 us (2%)
  between operations  0.77 us (2%)
    ppermute x17, starting transfers between devices, xor_permute(): lax.ppermute(value, axis, [(i, i ^ distance) for i in range(lax.axis_size...  19.9 us
    pallas_call x5, Pallas kernels, call(): pl.pallas_call(kernel, out_shape=out_shape, in_specs=[smem] + [vmem] * le...  9.5 us
    ppermute x17, waiting for transfers between devices, xor_permute(): lax.ppermute(value, axis, [(i, i ^ distance) for i in range(lax.axis_size...  8.31 us
    dynamic_slice x1, local copies, waits for them, and re-layouts, per_device(): lax.dynamic_slice_in_dim(ancestor_inverse, (col_id ^ step) * own_rows, ow...  1.8 us
    unnamed x9, local copies, waits for them, and re-layouts  1.7 us
  transfers between devices with their start and end apart: 17, of which 8 were waited for; matrix products, arithmetic and copies ran while one was open for 5% of the time, Pallas kernels for 22%

profile of v4, /device:TPU:0, one launch (start us, length us, event | category | flops | bytes accessed | tf_op | source)
XLA Modules:
  0.0 43.0 jit_solution(13787743190868829746)
XLA Ops:
  0.7 0.9 %copy-done = f32[8,64,128]{2,1,0:T(8,128)S(1)} copy-done((f32[8,64,128]{2,1,0:T(8,128)S(1)}, f32[8,64,128]{2,1,0:T(8,128)}, u32[]{:S(2)}) %copy-start) | copy-done | bytes 262168
  1.6 4.1 %collective-permute-start = (f32[4,64,128]{2,1,0:T(8,128)S(1)}, f32[4,64,128]{2,1,0:T(8,128)S(1)}, u32[]{:S(2)}, u32[]{:S(2)}) collective-permute-start(f32[4,64,128]{2,1,0:T(8,128)S(1)} %constant_dynamic-slice_fusion.3.refs_0_), channel_id=1, source_target_pairs={{0,4},{2,6},{4,0},{6,2},{1,5},{3,7},{5,1},{7,3},{8,12},{10,14},{12... | collective-permute-start | bytes 393224 | tf_op jit(solution)/shard_map/ppermute | solution.py:25
  5.7 1.6 %collective-permute-start.2 = (f32[4,64,128]{2,1,0:T(8,128)S(1)}, f32[4,64,128]{2,1,0:T(8,128)S(1)}, u32[]{:S(2)}, u32[]{:S(2)}) collective-permute-start(f32[4,64,128]{2,1,0:T(8,128)S(1)} %constant_dynamic-slice_fusion.3.refs_0_), channel_id=1, source_target_pairs={{0,2},{2,0},{4,6},{6,4},{1,3},{3,1},{5,7},{7,5},{8,10},{10,8},{12,... | collective-permute-start | bytes 393224 | tf_op jit(solution)/shard_map/ppermute | solution.py:25
  7.3 1.5 %collective-permute-start.1 = (f32[512,256]{1,0:T(8,128)}, f32[512,256]{1,0:T(8,128)S(1)}, u32[]{:S(2)}, u32[]{:S(2)}) collective-permute-start(f32[512,256]{1,0:T(8,128)} %refs_2_.1), channel_id=1, source_target_pairs={{0,1},{1,0},{2,3},{3,2},{4,5},{5,4},{6,7},{7,6},{8,9},{9,8},{10,11... | collective-permute-start | bytes 1572872 | tf_op jit(solution)/shard_map/ppermute | solution.py:25
  8.8 1.8 %constant_dynamic-slice_fusion = (f32[128,256]{1,0:T(8,128)}, f32[128,256]{1,0:T(8,128)}, f32[128,256]{1,0:T(8,128)S(1)}) fusion(f32[512,256]{1,0:T(8,128)} %refs_2_.1, s32[]{:T(128)S(6)} %select_n.35, s32[]{:T(128)S(6)} %select_n.34, s32[]{:T(128)S(6)} %select_n.33), kind=kLoop, calls=%fused_computation.3 | loop fusion | bytes 786444 | tf_op jit(solution)/shard_map/dynamic_slice | solution.py:300
  11.0 0.7 %copy-done.3 = s32[8,4]{0,1:T(4,128)S(1)} copy-done((s32[8,4]{0,1:T(4,128)S(1)}, s32[8,4]{0,1:T(4,128)}, u32[]{:S(2)}) %copy-start.3) | copy-done | bytes 152
  12.1 0.9 %shard_map.59.refs_2_ = f32[4,64,128]{2,1,0:T(8,128)S(1)} custom-call(s32[37]{0:T(128)S(1)} %concatenate.6.scalars, f32[8,64,64]{2,1,0:T(8,128)S(1)} %copy-done.2, f32[4,64,128]{2,1,0:T(8,128)S(1)} %collective-permute-done.lower), custom_call_target="tpu_custom_call" | custom-call | flops 99999997952 | bytes 262144 | tf_op jit(solution)/shard_map/pallas_call | solution.py:265
  13.0 1.5 %collective-permute-start.3 = (f32[4,64,128]{2,1,0:T(8,128)S(1)}, f32[4,64,128]{2,1,0:T(8,128)S(1)}, u32[]{:S(2)}, u32[]{:S(2)}) collective-permute-start(f32[4,64,128]{2,1,0:T(8,128)S(1)} %shard_map.59.refs_2_), channel_id=1, source_target_pairs={{0,2},{2,0},{4,6},{6,4},{1,3},{3,1},{5,7},{7,5},{8,10},{10,8},{12,... | collective-permute-start | bytes 393224 | tf_op jit(solution)/shard_map/ppermute | solution.py:25
  14.5 2.2 %collective-permute-start.7 = (f32[128,256]{1,0:T(8,128)}, f32[128,256]{1,0:T(8,128)}, u32[]{:S(2)}, u32[]{:S(2)}) collective-permute-start(f32[128,256]{1,0:T(8,128)} %get-tuple-element.59), channel_id=1, source_target_pairs={{0,6},{2,4},{4,2},{6,0},{1,7},{3,5},{5,3},{7,1},{8,14},{10,12},{12... | collective-permute-start | bytes 393224 | tf_op jit(solution)/shard_map/ppermute | solution.py:25
  17.2 2.1 %collective-permute-done.3.refs_3_ = f32[4,64,128]{2,1,0:T(8,128)S(1)} collective-permute-done((f32[4,64,128]{2,1,0:T(8,128)S(1)}, f32[4,64,128]{2,1,0:T(8,128)S(1)}, u32[]{:S(2)}, u32[]{:S(2)}) %collective-permute-start.3) | collective-permute-done | bytes 131104 | tf_op jit(solution)/shard_map/ppermute | solution.py:25
  19.8 0.8 %collective-permute-done.1.partner.refs_3_ = f32[512,256]{1,0:T(8,128)S(1)} collective-permute-done((f32[512,256]{1,0:T(8,128)}, f32[512,256]{1,0:T(8,128)S(1)}, u32[]{:S(2)}, u32[]{:S(2)}) %collective-permute-start.1) | collective-permute-done | bytes 524320 | tf_op jit(solution)/shard_map/ppermute | solution.py:25
  20.6 2.4 %shard_map.60 = (f32[256,256]{1,0:T(8,128)S(1)}, f32[4,4,64,128]{3,2,1,0:T(8,128)S(1)}, bf16[9,256,128]{2,1,0:T(8,128)(2,1)S(1)}, bf16[9,256,128]{2,1,0:T(8,128)...) custom-call(s32[37]{0:T(128)S(1)} %concatenate.6.scalars, f32[8,64,64]{2,1,0:T(8,128)S(1)} %copy-done.2, ...), custom_call_target="tpu_custom_call" | custom-call | flops 99999997952 | bytes 1703936 | tf_op jit(solution)/shard_map/pallas_call | solution.py:265
  23.0 0.6 %collective-permute-start.9 = (f32[4,4,64,128]{3,2,1,0:T(8,128)S(1)}, f32[4,4,64,128]{3,2,1,0:T(8,128)S(1)}, u32[]{:S(2)}, u32[]{:S(2)}) collective-permute-start(f32[4,4,64,128]{3,2,1,0:T(8,128)S(1)} %get-tuple-element.44.refs_0_), channel_id=1, source_target_pairs={{0,8},{8,0},{16,24},{24,16},{1,9},{9,1},{17,25},{25,17},{2,10},{10... | collective-permute-start | bytes 1572872 | tf_op jit(solution)/shard_map/ppermute | solution.py:25
  23.6 1.9 %shard_map.61 = f32[2,64,128]{2,1,0:T(8,128)S(1)} custom-call(s32[37]{0:T(128)S(1)} %concatenate.6.scalars, f32[256,256]{1,0:T(8,128)S(1)} %get-tuple-element.36.total, bf16[9,256,128]{2,1,0:T(8,128)(2,1)S(1)} %get-tuple-element.37.r_high, bf16[9,256,128]{2,1,0:T(8,128)(2,1)S(1)} %get-tuple-element.38.r_low, ...), custom_call_target="tpu_custom_call" | custom-call | flops 99999997952 | bytes 4980736 | tf_op jit(solution)/shard_map/pallas_call | solution.py:265
  25.5 1.6 %collective-permute-start.8 = (f32[2,64,128]{2,1,0:T(8,128)S(1)}, f32[2,64,128]{2,1,0:T(8,128)S(1)}, u32[]{:S(2)}, u32[]{:S(2)}) collective-permute-start(f32[2,64,128]{2,1,0:T(8,128)S(1)} %shard_map.61), channel_id=1, source_target_pairs={{0,16},{8,24},{16,0},{24,8},{1,17},{9,25},{17,1},{25,9},{2,18},{10... | collective-permute-start | bytes 196616 | tf_op jit(solution)/shard_map/ppermute | solution.py:25
  27.1 2.1 %collective-permute-done.12.refs_0_ = f32[128,256]{1,0:T(8,128)} collective-permute-done((f32[128,256]{1,0:T(8,128)}, f32[128,256]{1,0:T(8,128)}, u32[]{:S(2)}, u32[]{:S(2)}) %collective-permute-start.12) | collective-permute-done | bytes 131104 | tf_op jit(solution)/shard_map/ppermute | solution.py:25
  29.2 1.5 %collective-permute-start.14 = (f32[128,256]{1,0:T(8,128)}, f32[128,256]{1,0:T(8,128)S(1)}, u32[]{:S(2)}, u32[]{:S(2)}) collective-permute-start(f32[128,256]{1,0:T(8,128)} %collective-permute-done.12.refs_0_), channel_id=1, source_target_pairs={{0,1},{1,0},{2,3},{3,2},{4,5},{5,4},{6,7},{7,6},{8,9},{9,8},{10,11... | collective-permute-start | bytes 393224 | tf_op jit(solution)/shard_map/ppermute | solution.py:25
  31.3 1.0 %collective-permute-start.10 = (f32[2,64,128]{2,1,0:T(8,128)S(1)}, f32[2,64,128]{2,1,0:T(8,128)S(1)}, u32[]{:S(2)}, u32[]{:S(2)}) collective-permute-start(f32[2,64,128]{2,1,0:T(8,128)S(1)} %add.39), channel_id=1, source_target_pairs={{0,2},{2,0},{4,6},{6,4},{1,3},{3,1},{5,7},{7,5},{8,10},{10,8},{12,... | collective-permute-start | bytes 196616 | tf_op jit(solution)/shard_map/ppermute | solution.py:25
  32.2 1.7 %shard_map.62 = (bf16[4,8,64,128]{3,2,1,0:T(8,128)(2,1)S(1)}, bf16[4,8,64,128]{3,2,1,0:T(8,128)(2,1)S(1)}, bf16[8,128,128]{2,1,0:T(8,128)(2,1)S(1)}, bf16[8,128,128]{2,1,0:T(8,128)(2,1)S(1)}, f32[4,64,128]{2,1,0:T(8,128)S(1)}) custom-call(s32[37]{0:T(128)S(1)} %concatenate.6.scalars, f32[8,64,64]{2,1,0:T(8,128)S(1)} %copy-done.2, ...), custom_call_target="tpu_custom_call" | custom-call | flops 10000000 | bytes 2490368 | tf_op jit(solution)/shard_map/pallas_call | solution.py:265
  33.9 1.6 %collective-permute-done.10 = f32[2,64,128]{2,1,0:T(8,128)S(1)} collective-permute-done((f32[2,64,128]{2,1,0:T(8,128)S(1)}, f32[2,64,128]{2,1,0:T(8,128)S(1)}, u32[]{:S(2)}, u32[]{:S(2)}) %collective-permute-start.10) | collective-permute-done | bytes 65568 | tf_op jit(solution)/shard_map/ppermute | solution.py:25
  35.6 2.6 %collective-permute-start.13 = (f32[2,64,128]{2,1,0:T(8,128)S(1)}, f32[2,64,128]{2,1,0:T(8,128)S(1)}, u32[]{:S(2)}, u32[]{:S(2)}) collective-permute-start(f32[2,64,128]{2,1,0:T(8,128)S(1)} %add.40), channel_id=1, source_target_pairs={{0,4},{2,6},{4,0},{6,2},{1,5},{3,7},{5,1},{7,3},{8,12},{10,14},{12... | collective-permute-start | bytes 196616 | tf_op jit(solution)/shard_map/ppermute | solution.py:25
  38.2 2.6 %shard_map.63 = f32[8,64,128]{2,1,0:T(8,128)} custom-call(s32[37]{0:T(128)S(1)} %concatenate.6.scalars, bf16[4,8,64,128]{3,2,1,0:T(8,128)(2,1)S(1)} %get-tuple-element.49.n_high, bf16[4,8,64,128]{3,2,1,0:T(8,128)(2,1)S(1)} %get-tuple-element.50.n_low, bf16[8,128,128]{2,1,0:T(8,128)(2,1)S(1)} %get-tuple-element.51.early_high, ...), custom_call_target="tpu_custom_call" | custom-call | flops 99999997952 | bytes 3670016 | tf_op jit(solution)/shard_map/pallas_call | solution.py:265
  40.9 1.2 %collective-permute-done.16 = f32[2,64,128]{2,1,0:T(8,128)S(1)} collective-permute-done((f32[2,64,128]{2,1,0:T(8,128)S(1)}, f32[2,64,128]{2,1,0:T(8,128)S(1)}, u32[]{:S(2)}, u32[]{:S(2)}) %collective-permute-start.16) | collective-permute-done | bytes 65568 | tf_op jit(solution)/shard_map/ppermute | solution.py:25
  42.3 0.7 %pad_maximum_fusion = f32[8,64,64]{2,1,0:T(8,128)} fusion(f32[2,64,64]{2,1,0:T(8,128)S(1)} %get-tuple-element.67, f32[2,64,64]{2,1,0:T(8,128)S(1)} %get-tuple-element.68, f32[2,64,64]{2,1,0:T(8,128)S(1)} %get-tuple-element.64, f32[2,64,64]{2,1,0:T(8,128)S(1)} %get-tuple-element.63), kind=kLoop, calls=%fused_computation | loop fusion | flops 98304 | bytes 262144 | tf_op jit(solution)/shard_map/concatenate | solution.py:452
  (34 shorter events, 2.8 us)
Async XLA Ops:
  0.6 1.0 %copy-start = (f32[8,64,128]{2,1,0:T(8,128)S(1)}, f32[8,64,128]{2,1,0:T(8,128)}, u32[]{:S(2)}) copy-start(f32[8,64,128]{2,1,0:T(8,128)} %param.4) | copy-start | bytes 786436
  1.6 10.5 %collective-permute-start = (f32[4,64,128]{2,1,0:T(8,128)S(1)}, f32[4,64,128]{2,1,0:T(8,128)S(1)}, u32[]{:S(2)}, u32[]{:S(2)}) collective-permute-start(f32[4,64,128]{2,1,0:T(8,128)S(1)} %constant_dynamic-slice_fusion.3.refs_0_), channel_id=1, source_target_pairs={{0,4},{2,6},{4,0},{6,2},{1,5},{3,7},{5,1},{7,3},{8,12},{10,14},{12... | collective-permute-start | bytes 393224 | tf_op jit(solution)/shard_map/ppermute | solution.py:25
  5.7 8.8 %collective-permute-start.2 = (f32[4,64,128]{2,1,0:T(8,128)S(1)}, f32[4,64,128]{2,1,0:T(8,128)S(1)}, u32[]{:S(2)}, u32[]{:S(2)}) collective-permute-start(f32[4,64,128]{2,1,0:T(8,128)S(1)} %constant_dynamic-slice_fusion.3.refs_0_), channel_id=1, source_target_pairs={{0,2},{2,0},{4,6},{6,4},{1,3},{3,1},{5,7},{7,5},{8,10},{10,8},{12,... | collective-permute-start | bytes 393224 | tf_op jit(solution)/shard_map/ppermute | solution.py:25
  7.3 13.3 %collective-permute-start.1 = (f32[512,256]{1,0:T(8,128)}, f32[512,256]{1,0:T(8,128)S(1)}, u32[]{:S(2)}, u32[]{:S(2)}) collective-permute-start(f32[512,256]{1,0:T(8,128)} %refs_2_.1), channel_id=1, source_target_pairs={{0,1},{1,0},{2,3},{3,2},{4,5},{5,4},{6,7},{7,6},{8,9},{9,8},{10,11... | collective-permute-start | bytes 1572872 | tf_op jit(solution)/shard_map/ppermute | solution.py:25
  8.8 11.8 %collective-permute-start.4 = (f32[512,256]{1,0:T(8,128)}, f32[512,256]{1,0:T(8,128)S(1)}, u32[]{:S(2)}, u32[]{:S(2)}) collective-permute-start(f32[512,256]{1,0:T(8,128)} %refs_2_.1), channel_id=1, source_target_pairs={{0,8},{8,0},{16,24},{24,16},{1,9},{9,1},{17,25},{25,17},{2,10},{10... | collective-permute-start | bytes 1572872 | tf_op jit(solution)/shard_map/ppermute | solution.py:25
  8.8 3.3 %copy-start.2 = (f32[8,64,64]{2,1,0:T(8,128)S(1)}, f32[8,64,64]{2,1,0:T(8,128)}, u32[]{:S(2)}) copy-start(f32[8,64,64]{2,1,0:T(8,128)} %dinv.5) | copy-start | bytes 393220
  10.6 6.4 %collective-permute-start.6 = (f32[128,256]{1,0:T(8,128)S(1)}, f32[128,256]{1,0:T(8,128)}, u32[]{:S(2)}, u32[]{:S(2)}) collective-permute-start(f32[128,256]{1,0:T(8,128)S(1)} %get-tuple-element.60), channel_id=1, source_target_pairs={{0,2},{2,0},{4,6},{6,4},{1,3},{3,1},{5,7},{7,5},{8,10},{10,8},{12,... | collective-permute-start | bytes 393224 | tf_op jit(solution)/shard_map/ppermute | solution.py:25
  11.0 0.7 %copy-start.3 = (s32[8,4]{0,1:T(4,128)S(1)}, s32[8,4]{0,1:T(4,128)}, u32[]{:S(2)}) copy-start(s32[8,4]{0,1:T(4,128)} %param.7) | copy-start | bytes 388
  12.0 8.6 %copy-start.1 = (f32[512,256]{1,0:T(8,128)S(1)}, f32[512,256]{1,0:T(8,128)}, u32[]{:S(2)}) copy-start(f32[512,256]{1,0:T(8,128)} %refs_2_.1) | copy-start | bytes 1572868
  13.0 6.3 %collective-permute-start.3 = (f32[4,64,128]{2,1,0:T(8,128)S(1)}, f32[4,64,128]{2,1,0:T(8,128)S(1)}, u32[]{:S(2)}, u32[]{:S(2)}) collective-permute-start(f32[4,64,128]{2,1,0:T(8,128)S(1)} %shard_map.59.refs_2_), channel_id=1, source_target_pairs={{0,2},{2,0},{4,6},{6,4},{1,3},{3,1},{5,7},{7,5},{8,10},{10,8},{12,... | collective-permute-start | bytes 393224 | tf_op jit(solution)/shard_map/ppermute | solution.py:25
  14.5 11.0 %collective-permute-start.7 = (f32[128,256]{1,0:T(8,128)}, f32[128,256]{1,0:T(8,128)}, u32[]{:S(2)}, u32[]{:S(2)}) collective-permute-start(f32[128,256]{1,0:T(8,128)} %get-tuple-element.59), channel_id=1, source_target_pairs={{0,6},{2,4},{4,2},{6,0},{1,7},{3,5},{5,3},{7,1},{8,14},{10,12},{12... | collective-permute-start | bytes 393224 | tf_op jit(solution)/shard_map/ppermute | solution.py:25
  17.0 12.2 %collective-permute-start.12 = (f32[128,256]{1,0:T(8,128)}, f32[128,256]{1,0:T(8,128)}, u32[]{:S(2)}, u32[]{:S(2)}) collective-permute-start(f32[128,256]{1,0:T(8,128)} %get-tuple-element.58), channel_id=1, source_target_pairs={{0,4},{2,6},{4,0},{6,2},{1,5},{3,7},{5,1},{7,3},{8,12},{10,14},{12... | collective-permute-start | bytes 393224 | tf_op jit(solution)/shard_map/ppermute | solution.py:25
  19.3 12.9 %collective-permute-start.11 = (f32[128,256]{1,0:T(8,128)}, f32[128,256]{1,0:T(8,128)}, u32[]{:S(2)}, u32[]{:S(2)}) collective-permute-start(f32[128,256]{1,0:T(8,128)} %collective-permute-done.6.refs_4_), channel_id=1, source_target_pairs={{0,1},{1,0},{2,3},{3,2},{4,5},{5,4},{6,7},{7,6},{8,9},{9,8},{10,11... | collective-permute-start | bytes 393224 | tf_op jit(solution)/shard_map/ppermute | solution.py:25
  20.6 3.0 %collective-permute-start.5 = (f32[512,256]{1,0:T(8,128)S(1)}, f32[512,256]{1,0:T(8,128)S(1)}, u32[]{:S(2)}, u32[]{:S(2)}) collective-permute-start(f32[512,256]{1,0:T(8,128)S(1)} %collective-permute-done.1.partner.refs_3_), channel_id=1, source_target_pairs={{0,8},{8,0},{16,24},{24,16},{1,9},{9,1},{17,25},{25,17},{2,10},{10... | collective-permute-start | bytes 1572872 | tf_op jit(solution)/shard_map/ppermute | solution.py:25
  23.0 8.2 %collective-permute-start.9 = (f32[4,4,64,128]{3,2,1,0:T(8,128)S(1)}, f32[4,4,64,128]{3,2,1,0:T(8,128)S(1)}, u32[]{:S(2)}, u32[]{:S(2)}) collective-permute-start(f32[4,4,64,128]{3,2,1,0:T(8,128)S(1)} %get-tuple-element.44.refs_0_), channel_id=1, source_target_pairs={{0,8},{8,0},{16,24},{24,16},{1,9},{9,1},{17,25},{25,17},{2,10},{10... | collective-permute-start | bytes 1572872 | tf_op jit(solution)/shard_map/ppermute | solution.py:25
  25.5 5.7 %collective-permute-start.8 = (f32[2,64,128]{2,1,0:T(8,128)S(1)}, f32[2,64,128]{2,1,0:T(8,128)S(1)}, u32[]{:S(2)}, u32[]{:S(2)}) collective-permute-start(f32[2,64,128]{2,1,0:T(8,128)S(1)} %shard_map.61), channel_id=1, source_target_pairs={{0,16},{8,24},{16,0},{24,8},{1,17},{9,25},{17,1},{25,9},{2,18},{10... | collective-permute-start | bytes 196616 | tf_op jit(solution)/shard_map/ppermute | solution.py:25
  29.2 9.0 %collective-permute-start.14 = (f32[128,256]{1,0:T(8,128)}, f32[128,256]{1,0:T(8,128)S(1)}, u32[]{:S(2)}, u32[]{:S(2)}) collective-permute-start(f32[128,256]{1,0:T(8,128)} %collective-permute-done.12.refs_0_), channel_id=1, source_target_pairs={{0,1},{1,0},{2,3},{3,2},{4,5},{5,4},{6,7},{7,6},{8,9},{9,8},{10,11... | collective-permute-start | bytes 393224 | tf_op jit(solution)/shard_map/ppermute | solution.py:25
  30.7 7.4 %collective-permute-start.15 = (f32[128,256]{1,0:T(8,128)}, f32[128,256]{1,0:T(8,128)S(1)}, u32[]{:S(2)}, u32[]{:S(2)}) collective-permute-start(f32[128,256]{1,0:T(8,128)} %collective-permute-done.7.refs_1_), channel_id=1, source_target_pairs={{0,1},{1,0},{2,3},{3,2},{4,5},{5,4},{6,7},{7,6},{8,9},{9,8},{10,11... | collective-permute-start | bytes 393224 | tf_op jit(solution)/shard_map/ppermute | solution.py:25
  31.3 4.3 %collective-permute-start.10 = (f32[2,64,128]{2,1,0:T(8,128)S(1)}, f32[2,64,128]{2,1,0:T(8,128)S(1)}, u32[]{:S(2)}, u32[]{:S(2)}) collective-permute-start(f32[2,64,128]{2,1,0:T(8,128)S(1)} %add.39), channel_id=1, source_target_pairs={{0,2},{2,0},{4,6},{6,4},{1,3},{3,1},{5,7},{7,5},{8,10},{10,8},{12,... | collective-permute-start | bytes 196616 | tf_op jit(solution)/shard_map/ppermute | solution.py:25
  35.6 5.2 %collective-permute-start.13 = (f32[2,64,128]{2,1,0:T(8,128)S(1)}, f32[2,64,128]{2,1,0:T(8,128)S(1)}, u32[]{:S(2)}, u32[]{:S(2)}) collective-permute-start(f32[2,64,128]{2,1,0:T(8,128)S(1)} %add.40), channel_id=1, source_target_pairs={{0,4},{2,6},{4,0},{6,2},{1,5},{3,7},{5,1},{7,3},{8,12},{10,14},{12... | collective-permute-start | bytes 196616 | tf_op jit(solution)/shard_map/ppermute | solution.py:25
  40.8 1.3 %collective-permute-start.16 = (f32[2,64,128]{2,1,0:T(8,128)S(1)}, f32[2,64,128]{2,1,0:T(8,128)S(1)}, u32[]{:S(2)}, u32[]{:S(2)}) collective-permute-start(f32[2,64,128]{2,1,0:T(8,128)S(1)} %add.42), channel_id=1, source_target_pairs={{0,8},{8,0},{16,24},{24,16},{1,9},{9,1},{17,25},{25,17},{2,10},{10... | collective-permute-start | bytes 196616 | tf_op jit(solution)/shard_map/ppermute | solution.py:25

commit v5 on v4

--- a/solution.py
+++ b/solution.py
@@ -12,10 +12,10 @@
 CONTRACT_FIRST = ((0,), (0,))
 
 
-DONE = {'core_own': 2, 'mine0': 2, 'mine1': 5, 'mine2': 3, 'normed_other': 4, 'panel': 6, 'prep': None, 'theirs0': 5, 'theirs1': None, 'theirs2': None}
+DONE = {'core_own': 2, 'mine0': 2, 'mine1': 5, 'mine2': 3, 'normed_other': 4, 'panel': 6, 'prep': 4, 'theirs0': 5, 'theirs1': None, 'theirs2': None}
 GATE = {'mine0': 0, 'mine2': False, 'scalars': True}
 SPLIT = True
-RADIX = False
+RADIX = True
 MIX = False
 TIED = False
 COST = [100000000000, 100000000000, 100000000000]

time: 43.2 us -> 43.2 us (level)
  waiting for transfers between devices: 8.31 us -> 5.67 us
  starting transfers between devices: 19.9 us -> 22.5 us
    ppermute x17, waiting for transfers between devices: 8.31 us -> 5.66 us  [xor_permute(): lax.ppermute(value, axis, [(i, i ^ distance) for i in range(lax.axis_size...]
    ppermute x17, starting transfers between devices: 19.9 us -> 21.5 us  [xor_permute(): lax.ppermute(value, axis, [(i, i ^ distance) for i in range(lax.axis_size...]
    ppermute x0 -> x1, starting transfers between devices: none -> 0.95 us  [per_device(): lax.ppermute(total, ('row', 'col'), both)]
  transfers between devices with their start and end apart: 17 -> 18, of which waited for: 8 -> 7; matrix products, arithmetic and copies ran while one was open for 5% -> 5% of each run, Pallas kernels for 22% -> 22%
where the time goes in v5:
time: 43.2 us; the launch traced here: 42.9 us
  starting transfers between devices  22.5 us (52%)
  Pallas kernels  9.5 us (22%)
  waiting for transfers between devices  5.67 us (13%)
  local copies, waits for them, and re-layouts  3.76 us (9%)
  between operations  0.78 us (2%)
  other arithmetic  0.77 us (2%)
    ppermute x17, starting transfers between devices, xor_permute(): lax.ppermute(value, axis, [(i, i ^ distance) for i in range(lax.axis_size...  21.5 us
    pallas_call x5, Pallas kernels, call(): pl.pallas_call(kernel, out_shape=out_shape, in_specs=[smem] + [vmem] * le...  9.5 us
    ppermute x17, waiting for transfers between devices, xor_permute(): lax.ppermute(value, axis, [(i, i ^ distance) for i in range(lax.axis_size...  5.66 us
    dynamic_slice x1, local copies, waits for them, and re-layouts, per_device(): lax.dynamic_slice_in_dim(ancestor_inverse, (col_id ^ step) * own_rows, ow...  1.8 us
    unnamed x9, local copies, waits for them, and re-layouts  1.7 us
    ppermute x1, starting transfers between devices, per_device(): lax.ppermute(total, ('row', 'col'), both)  0.95 us
  transfers between devices with their start and end apart: 18, of which 7 were waited for; matrix products, arithmetic and copies ran while one was open for 5% of the time, Pallas kernels for 22%

profile of v5, /device:TPU:0, one launch (start us, length us, event | category | flops | bytes accessed | tf_op | source)
XLA Modules:
  0.0 42.9 jit_solution(4432268702810750326)
XLA Ops:
  0.7 0.9 %copy-done = f32[8,64,128]{2,1,0:T(8,128)S(1)} copy-done((f32[8,64,128]{2,1,0:T(8,128)S(1)}, f32[8,64,128]{2,1,0:T(8,128)}, u32[]{:S(2)}) %copy-start) | copy-done | bytes 262168
  1.6 4.1 %collective-permute-start = (f32[4,64,128]{2,1,0:T(8,128)S(1)}, f32[4,64,128]{2,1,0:T(8,128)S(1)}, u32[]{:S(2)}, u32[]{:S(2)}) collective-permute-start(f32[4,64,128]{2,1,0:T(8,128)S(1)} %constant_dynamic-slice_fusion.3.refs_0_), channel_id=1, source_target_pairs={{0,4},{2,6},{4,0},{6,2},{1,5},{3,7},{5,1},{7,3},{8,12},{10,14},{12... | collective-permute-start | bytes 393224 | tf_op jit(solution)/shard_map/ppermute | solution.py:25
  5.7 1.6 %collective-permute-start.2 = (f32[4,64,128]{2,1,0:T(8,128)S(1)}, f32[4,64,128]{2,1,0:T(8,128)S(1)}, u32[]{:S(2)}, u32[]{:S(2)}) collective-permute-start(f32[4,64,128]{2,1,0:T(8,128)S(1)} %constant_dynamic-slice_fusion.3.refs_0_), channel_id=1, source_target_pairs={{0,2},{2,0},{4,6},{6,4},{1,3},{3,1},{5,7},{7,5},{8,10},{10,8},{12,... | collective-permute-start | bytes 393224 | tf_op jit(solution)/shard_map/ppermute | solution.py:25
  7.3 1.5 %collective-permute-start.1 = (f32[512,256]{1,0:T(8,128)}, f32[512,256]{1,0:T(8,128)S(1)}, u32[]{:S(2)}, u32[]{:S(2)}) collective-permute-start(f32[512,256]{1,0:T(8,128)} %refs_2_.1), channel_id=1, source_target_pairs={{0,1},{1,0},{2,3},{3,2},{4,5},{5,4},{6,7},{7,6},{8,9},{9,8},{10,11... | collective-permute-start | bytes 1572872 | tf_op jit(solution)/shard_map/ppermute | solution.py:25
  8.8 1.8 %constant_dynamic-slice_fusion = (f32[128,256]{1,0:T(8,128)}, f32[128,256]{1,0:T(8,128)}, f32[128,256]{1,0:T(8,128)S(1)}) fusion(f32[512,256]{1,0:T(8,128)} %refs_2_.1, s32[]{:T(128)S(6)} %select_n.35, s32[]{:T(128)S(6)} %select_n.34, s32[]{:T(128)S(6)} %select_n.33), kind=kLoop, calls=%fused_computation.4 | loop fusion | bytes 786444 | tf_op jit(solution)/shard_map/dynamic_slice | solution.py:300
  11.0 0.7 %copy-done.3 = s32[8,4]{0,1:T(4,128)S(1)} copy-done((s32[8,4]{0,1:T(4,128)S(1)}, s32[8,4]{0,1:T(4,128)}, u32[]{:S(2)}) %copy-start.3) | copy-done | bytes 152
  12.1 0.9 %shard_map.59.refs_2_ = f32[4,64,128]{2,1,0:T(8,128)S(1)} custom-call(s32[37]{0:T(128)S(1)} %concatenate.6.scalars, f32[8,64,64]{2,1,0:T(8,128)S(1)} %copy-done.2, f32[4,64,128]{2,1,0:T(8,128)S(1)} %collective-permute-done.lower), custom_call_target="tpu_custom_call" | custom-call | flops 99999997952 | bytes 262144 | tf_op jit(solution)/shard_map/pallas_call | solution.py:265
  13.0 1.5 %collective-permute-start.3 = (f32[4,64,128]{2,1,0:T(8,128)S(1)}, f32[4,64,128]{2,1,0:T(8,128)S(1)}, u32[]{:S(2)}, u32[]{:S(2)}) collective-permute-start(f32[4,64,128]{2,1,0:T(8,128)S(1)} %shard_map.59.refs_2_), channel_id=1, source_target_pairs={{0,2},{2,0},{4,6},{6,4},{1,3},{3,1},{5,7},{7,5},{8,10},{10,8},{12,... | collective-permute-start | bytes 393224 | tf_op jit(solution)/shard_map/ppermute | solution.py:25
  14.5 2.2 %collective-permute-start.7 = (f32[128,256]{1,0:T(8,128)}, f32[128,256]{1,0:T(8,128)}, u32[]{:S(2)}, u32[]{:S(2)}) collective-permute-start(f32[128,256]{1,0:T(8,128)} %get-tuple-element.59), channel_id=1, source_target_pairs={{0,6},{2,4},{4,2},{6,0},{1,7},{3,5},{5,3},{7,1},{8,14},{10,12},{12... | collective-permute-start | bytes 393224 | tf_op jit(solution)/shard_map/ppermute | solution.py:25
  17.2 2.1 %collective-permute-done.3.refs_3_ = f32[4,64,128]{2,1,0:T(8,128)S(1)} collective-permute-done((f32[4,64,128]{2,1,0:T(8,128)S(1)}, f32[4,64,128]{2,1,0:T(8,128)S(1)}, u32[]{:S(2)}, u32[]{:S(2)}) %collective-permute-start.3) | collective-permute-done | bytes 131104 | tf_op jit(solution)/shard_map/ppermute | solution.py:25
  19.8 0.8 %collective-permute-done.1.partner.refs_3_ = f32[512,256]{1,0:T(8,128)S(1)} collective-permute-done((f32[512,256]{1,0:T(8,128)}, f32[512,256]{1,0:T(8,128)S(1)}, u32[]{:S(2)}, u32[]{:S(2)}) %collective-permute-start.1) | collective-permute-done | bytes 524320 | tf_op jit(solution)/shard_map/ppermute | solution.py:25
  20.6 2.4 %shard_map.60 = (f32[256,256]{1,0:T(8,128)S(1)}, f32[4,4,64,128]{3,2,1,0:T(8,128)S(1)}, bf16[9,256,128]{2,1,0:T(8,128)(2,1)S(1)}, bf16[9,256,128]{2,1,0:T(8,128)...) custom-call(s32[37]{0:T(128)S(1)} %concatenate.6.scalars, f32[8,64,64]{2,1,0:T(8,128)S(1)} %copy-done.2, ...), custom_call_target="tpu_custom_call" | custom-call | flops 99999997952 | bytes 1703936 | tf_op jit(solution)/shard_map/pallas_call | solution.py:265
  23.0 0.6 %collective-permute-start.8 = (f32[4,4,64,128]{3,2,1,0:T(8,128)S(1)}, f32[4,4,64,128]{3,2,1,0:T(8,128)S(1)}, u32[]{:S(2)}, u32[]{:S(2)}) collective-permute-start(f32[4,4,64,128]{3,2,1,0:T(8,128)S(1)} %get-tuple-element.44.refs_0_), channel_id=1, source_target_pairs={{0,8},{8,0},{16,24},{24,16},{1,9},{9,1},{17,25},{25,17},{2,10},{10... | collective-permute-start | bytes 1572872 | tf_op jit(solution)/shard_map/ppermute | solution.py:25
  23.6 1.9 %shard_map.61 = f32[2,64,128]{2,1,0:T(8,128)S(1)} custom-call(s32[37]{0:T(128)S(1)} %concatenate.6.scalars, f32[256,256]{1,0:T(8,128)S(1)} %get-tuple-element.36.total, bf16[9,256,128]{2,1,0:T(8,128)(2,1)S(1)} %get-tuple-element.37.r_high, bf16[9,256,128]{2,1,0:T(8,128)(2,1)S(1)} %get-tuple-element.38.r_low, ...), custom_call_target="tpu_custom_call" | custom-call | flops 99999997952 | bytes 4980736 | tf_op jit(solution)/shard_map/pallas_call | solution.py:265
  25.6 2.3 %collective-permute-start.10 = (f32[2,64,128]{2,1,0:T(8,128)S(1)}, f32[2,64,128]{2,1,0:T(8,128)S(1)}, u32[]{:S(2)}, u32[]{:S(2)}) collective-permute-start(f32[2,64,128]{2,1,0:T(8,128)S(1)} %shard_map.61), channel_id=1, source_target_pairs={{0,2},{2,0},{4,6},{6,4},{1,3},{3,1},{5,7},{7,5},{8,10},{10,8},{12,... | collective-permute-start | bytes 196616 | tf_op jit(solution)/shard_map/ppermute | solution.py:25
  27.9 1.0 %collective-permute-start.11 = (f32[2,64,128]{2,1,0:T(8,128)S(1)}, f32[2,64,128]{2,1,0:T(8,128)S(1)}, u32[]{:S(2)}, u32[]{:S(2)}) collective-permute-start(f32[2,64,128]{2,1,0:T(8,128)S(1)} %shard_map.61), channel_id=1, source_target_pairs={{0,18},{2,16},{4,22},{6,20},{8,26},{10,24},{12,30},{14,28},{16,2},... | collective-permute-start | bytes 196616 | tf_op jit(solution)/shard_map/ppermute | solution.py:416
  28.8 0.6 %collective-permute-start.9 = (f32[2,64,128]{2,1,0:T(8,128)S(1)}, f32[2,64,128]{2,1,0:T(8,128)S(1)}, u32[]{:S(2)}, u32[]{:S(2)}) collective-permute-start(f32[2,64,128]{2,1,0:T(8,128)S(1)} %shard_map.61), channel_id=1, source_target_pairs={{0,16},{8,24},{16,0},{24,8},{1,17},{9,25},{17,1},{25,9},{2,18},{10... | collective-permute-start | bytes 196616 | tf_op jit(solution)/shard_map/ppermute | solution.py:25
  29.4 1.5 %collective-permute-start.16 = (f32[128,256]{1,0:T(8,128)}, f32[128,256]{1,0:T(8,128)S(1)}, u32[]{:S(2)}, u32[]{:S(2)}) collective-permute-start(f32[128,256]{1,0:T(8,128)} %collective-permute-done.7.refs_1_), channel_id=1, source_target_pairs={{0,1},{1,0},{2,3},{3,2},{4,5},{5,4},{6,7},{7,6},{8,9},{9,8},{10,11... | collective-permute-start | bytes 393224 | tf_op jit(solution)/shard_map/ppermute | solution.py:25
  31.4 1.7 %shard_map.62 = (bf16[4,8,64,128]{3,2,1,0:T(8,128)(2,1)S(1)}, bf16[4,8,64,128]{3,2,1,0:T(8,128)(2,1)S(1)}, bf16[8,128,128]{2,1,0:T(8,128)(2,1)S(1)}, bf16[8,128,128]{2,1,0:T(8,128)(2,1)S(1)}, f32[4,64,128]{2,1,0:T(8,128)S(1)}) custom-call(s32[37]{0:T(128)S(1)} %concatenate.6.scalars, f32[8,64,64]{2,1,0:T(8,128)S(1)} %copy-done.2, ...), custom_call_target="tpu_custom_call" | custom-call | flops 10000000 | bytes 2490368 | tf_op jit(solution)/shard_map/pallas_call | solution.py:265
  33.2 0.6 %collective-permute-done.9 = f32[2,64,128]{2,1,0:T(8,128)S(1)} collective-permute-done((f32[2,64,128]{2,1,0:T(8,128)S(1)}, f32[2,64,128]{2,1,0:T(8,128)S(1)}, u32[]{:S(2)}, u32[]{:S(2)}) %collective-permute-start.9) | collective-permute-done | bytes 65568 | tf_op jit(solution)/shard_map/ppermute | solution.py:25
  33.8 3.8 %collective-permute-start.14 = (f32[2,64,128]{2,1,0:T(8,128)S(1)}, f32[2,64,128]{2,1,0:T(8,128)S(1)}, u32[]{:S(2)}, u32[]{:S(2)}) collective-permute-start(f32[2,64,128]{2,1,0:T(8,128)S(1)} %add_add_fusion), channel_id=1, source_target_pairs={{0,4},{2,6},{4,0},{6,2},{1,5},{3,7},{5,1},{7,3},{8,12},{10,14},{12... | collective-permute-start | bytes 196616 | tf_op jit(solution)/shard_map/ppermute | solution.py:25
  37.6 2.6 %shard_map.63 = f32[8,64,128]{2,1,0:T(8,128)} custom-call(s32[37]{0:T(128)S(1)} %concatenate.6.scalars, bf16[4,8,64,128]{3,2,1,0:T(8,128)(2,1)S(1)} %get-tuple-element.49.n_high, bf16[4,8,64,128]{3,2,1,0:T(8,128)(2,1)S(1)} %get-tuple-element.50.n_low, bf16[8,128,128]{2,1,0:T(8,128)(2,1)S(1)} %get-tuple-element.51.early_high, ...), custom_call_target="tpu_custom_call" | custom-call | flops 99999997952 | bytes 3670016 | tf_op jit(solution)/shard_map/pallas_call | solution.py:265
  40.9 1.2 %collective-permute-done.17 = f32[2,64,128]{2,1,0:T(8,128)S(1)} collective-permute-done((f32[2,64,128]{2,1,0:T(8,128)S(1)}, f32[2,64,128]{2,1,0:T(8,128)S(1)}, u32[]{:S(2)}, u32[]{:S(2)}) %collective-permute-start.17) | collective-permute-done | bytes 65568 | tf_op jit(solution)/shard_map/ppermute | solution.py:25
  42.2 0.7 %pad_maximum_fusion = f32[8,64,64]{2,1,0:T(8,128)} fusion(f32[2,64,64]{2,1,0:T(8,128)S(1)} %get-tuple-element.67, f32[2,64,64]{2,1,0:T(8,128)S(1)} %get-tuple-element.68, f32[2,64,64]{2,1,0:T(8,128)S(1)} %get-tuple-element.64, f32[2,64,64]{2,1,0:T(8,128)S(1)} %get-tuple-element.63), kind=kLoop, calls=%fused_computation | loop fusion | flops 98304 | bytes 262144 | tf_op jit(solution)/shard_map/concatenate | solution.py:452
  (35 shorter events, 3.3 us)
Async XLA Ops:
  0.6 1.0 %copy-start = (f32[8,64,128]{2,1,0:T(8,128)S(1)}, f32[8,64,128]{2,1,0:T(8,128)}, u32[]{:S(2)}) copy-start(f32[8,64,128]{2,1,0:T(8,128)} %param.4) | copy-start | bytes 786436
  1.6 10.5 %collective-permute-start = (f32[4,64,128]{2,1,0:T(8,128)S(1)}, f32[4,64,128]{2,1,0:T(8,128)S(1)}, u32[]{:S(2)}, u32[]{:S(2)}) collective-permute-start(f32[4,64,128]{2,1,0:T(8,128)S(1)} %constant_dynamic-slice_fusion.3.refs_0_), channel_id=1, source_target_pairs={{0,4},{2,6},{4,0},{6,2},{1,5},{3,7},{5,1},{7,3},{8,12},{10,14},{12... | collective-permute-start | bytes 393224 | tf_op jit(solution)/shard_map/ppermute | solution.py:25
  5.7 8.8 %collective-permute-start.2 = (f32[4,64,128]{2,1,0:T(8,128)S(1)}, f32[4,64,128]{2,1,0:T(8,128)S(1)}, u32[]{:S(2)}, u32[]{:S(2)}) collective-permute-start(f32[4,64,128]{2,1,0:T(8,128)S(1)} %constant_dynamic-slice_fusion.3.refs_0_), channel_id=1, source_target_pairs={{0,2},{2,0},{4,6},{6,4},{1,3},{3,1},{5,7},{7,5},{8,10},{10,8},{12,... | collective-permute-start | bytes 393224 | tf_op jit(solution)/shard_map/ppermute | solution.py:25
  7.3 13.3 %collective-permute-start.1 = (f32[512,256]{1,0:T(8,128)}, f32[512,256]{1,0:T(8,128)S(1)}, u32[]{:S(2)}, u32[]{:S(2)}) collective-permute-start(f32[512,256]{1,0:T(8,128)} %refs_2_.1), channel_id=1, source_target_pairs={{0,1},{1,0},{2,3},{3,2},{4,5},{5,4},{6,7},{7,6},{8,9},{9,8},{10,11... | collective-permute-start | bytes 1572872 | tf_op jit(solution)/shard_map/ppermute | solution.py:25
  8.8 11.8 %collective-permute-start.4 = (f32[512,256]{1,0:T(8,128)}, f32[512,256]{1,0:T(8,128)S(1)}, u32[]{:S(2)}, u32[]{:S(2)}) collective-permute-start(f32[512,256]{1,0:T(8,128)} %refs_2_.1), channel_id=1, source_target_pairs={{0,8},{8,0},{16,24},{24,16},{1,9},{9,1},{17,25},{25,17},{2,10},{10... | collective-permute-start | bytes 1572872 | tf_op jit(solution)/shard_map/ppermute | solution.py:25
  8.8 3.3 %copy-start.2 = (f32[8,64,64]{2,1,0:T(8,128)S(1)}, f32[8,64,64]{2,1,0:T(8,128)}, u32[]{:S(2)}) copy-start(f32[8,64,64]{2,1,0:T(8,128)} %dinv.5) | copy-start | bytes 393220
  10.6 6.4 %collective-permute-start.6 = (f32[128,256]{1,0:T(8,128)S(1)}, f32[128,256]{1,0:T(8,128)}, u32[]{:S(2)}, u32[]{:S(2)}) collective-permute-start(f32[128,256]{1,0:T(8,128)S(1)} %get-tuple-element.60), channel_id=1, source_target_pairs={{0,2},{2,0},{4,6},{6,4},{1,3},{3,1},{5,7},{7,5},{8,10},{10,8},{12,... | collective-permute-start | bytes 393224 | tf_op jit(solution)/shard_map/ppermute | solution.py:25
  11.0 0.7 %copy-start.3 = (s32[8,4]{0,1:T(4,128)S(1)}, s32[8,4]{0,1:T(4,128)}, u32[]{:S(2)}) copy-start(s32[8,4]{0,1:T(4,128)} %param.7) | copy-start | bytes 388
  12.0 8.6 %copy-start.1 = (f32[512,256]{1,0:T(8,128)S(1)}, f32[512,256]{1,0:T(8,128)}, u32[]{:S(2)}) copy-start(f32[512,256]{1,0:T(8,128)} %refs_2_.1) | copy-start | bytes 1572868
  13.0 6.3 %collective-permute-start.3 = (f32[4,64,128]{2,1,0:T(8,128)S(1)}, f32[4,64,128]{2,1,0:T(8,128)S(1)}, u32[]{:S(2)}, u32[]{:S(2)}) collective-permute-start(f32[4,64,128]{2,1,0:T(8,128)S(1)} %shard_map.59.refs_2_), channel_id=1, source_target_pairs={{0,2},{2,0},{4,6},{6,4},{1,3},{3,1},{5,7},{7,5},{8,10},{10,8},{12,... | collective-permute-start | bytes 393224 | tf_op jit(solution)/shard_map/ppermute | solution.py:25
  14.5 11.0 %collective-permute-start.7 = (f32[128,256]{1,0:T(8,128)}, f32[128,256]{1,0:T(8,128)}, u32[]{:S(2)}, u32[]{:S(2)}) collective-permute-start(f32[128,256]{1,0:T(8,128)} %get-tuple-element.59), channel_id=1, source_target_pairs={{0,6},{2,4},{4,2},{6,0},{1,7},{3,5},{5,3},{7,1},{8,14},{10,12},{12... | collective-permute-start | bytes 393224 | tf_op jit(solution)/shard_map/ppermute | solution.py:25
  17.0 12.4 %collective-permute-start.13 = (f32[128,256]{1,0:T(8,128)}, f32[128,256]{1,0:T(8,128)}, u32[]{:S(2)}, u32[]{:S(2)}) collective-permute-start(f32[128,256]{1,0:T(8,128)} %get-tuple-element.58), channel_id=1, source_target_pairs={{0,4},{2,6},{4,0},{6,2},{1,5},{3,7},{5,1},{7,3},{8,12},{10,14},{12... | collective-permute-start | bytes 393224 | tf_op jit(solution)/shard_map/ppermute | solution.py:25
  19.3 11.6 %collective-permute-start.12 = (f32[128,256]{1,0:T(8,128)}, f32[128,256]{1,0:T(8,128)}, u32[]{:S(2)}, u32[]{:S(2)}) collective-permute-start(f32[128,256]{1,0:T(8,128)} %collective-permute-done.6.refs_4_), channel_id=1, source_target_pairs={{0,1},{1,0},{2,3},{3,2},{4,5},{5,4},{6,7},{7,6},{8,9},{9,8},{10,11... | collective-permute-start | bytes 393224 | tf_op jit(solution)/shard_map/ppermute | solution.py:25
  20.6 3.0 %collective-permute-start.5 = (f32[512,256]{1,0:T(8,128)S(1)}, f32[512,256]{1,0:T(8,128)S(1)}, u32[]{:S(2)}, u32[]{:S(2)}) collective-permute-start(f32[512,256]{1,0:T(8,128)S(1)} %collective-permute-done.1.partner.refs_3_), channel_id=1, source_target_pairs={{0,8},{8,0},{16,24},{24,16},{1,9},{9,1},{17,25},{25,17},{2,10},{10... | collective-permute-start | bytes 1572872 | tf_op jit(solution)/shard_map/ppermute | solution.py:25
  23.0 2.5 %collective-permute-start.8 = (f32[4,4,64,128]{3,2,1,0:T(8,128)S(1)}, f32[4,4,64,128]{3,2,1,0:T(8,128)S(1)}, u32[]{:S(2)}, u32[]{:S(2)}) collective-permute-start(f32[4,4,64,128]{3,2,1,0:T(8,128)S(1)} %get-tuple-element.44.refs_0_), channel_id=1, source_target_pairs={{0,8},{8,0},{16,24},{24,16},{1,9},{9,1},{17,25},{25,17},{2,10},{10... | collective-permute-start | bytes 1572872 | tf_op jit(solution)/shard_map/ppermute | solution.py:25
  25.6 7.6 %collective-permute-start.10 = (f32[2,64,128]{2,1,0:T(8,128)S(1)}, f32[2,64,128]{2,1,0:T(8,128)S(1)}, u32[]{:S(2)}, u32[]{:S(2)}) collective-permute-start(f32[2,64,128]{2,1,0:T(8,128)S(1)} %shard_map.61), channel_id=1, source_target_pairs={{0,2},{2,0},{4,6},{6,4},{1,3},{3,1},{5,7},{7,5},{8,10},{10,8},{12,... | collective-permute-start | bytes 196616 | tf_op jit(solution)/shard_map/ppermute | solution.py:25
  27.9 5.3 %collective-permute-start.11 = (f32[2,64,128]{2,1,0:T(8,128)S(1)}, f32[2,64,128]{2,1,0:T(8,128)S(1)}, u32[]{:S(2)}, u32[]{:S(2)}) collective-permute-start(f32[2,64,128]{2,1,0:T(8,128)S(1)} %shard_map.61), channel_id=1, source_target_pairs={{0,18},{2,16},{4,22},{6,20},{8,26},{10,24},{12,30},{14,28},{16,2},... | collective-permute-start | bytes 196616 | tf_op jit(solution)/shard_map/ppermute | solution.py:416
  28.8 4.9 %collective-permute-start.9 = (f32[2,64,128]{2,1,0:T(8,128)S(1)}, f32[2,64,128]{2,1,0:T(8,128)S(1)}, u32[]{:S(2)}, u32[]{:S(2)}) collective-permute-start(f32[2,64,128]{2,1,0:T(8,128)S(1)} %shard_map.61), channel_id=1, source_target_pairs={{0,16},{8,24},{16,0},{24,8},{1,17},{9,25},{17,1},{25,9},{2,18},{10... | collective-permute-start | bytes 196616 | tf_op jit(solution)/shard_map/ppermute | solution.py:25
  29.4 8.2 %collective-permute-start.16 = (f32[128,256]{1,0:T(8,128)}, f32[128,256]{1,0:T(8,128)S(1)}, u32[]{:S(2)}, u32[]{:S(2)}) collective-permute-start(f32[128,256]{1,0:T(8,128)} %collective-permute-done.7.refs_1_), channel_id=1, source_target_pairs={{0,1},{1,0},{2,3},{3,2},{4,5},{5,4},{6,7},{7,6},{8,9},{9,8},{10,11... | collective-permute-start | bytes 393224 | tf_op jit(solution)/shard_map/ppermute | solution.py:25
  30.9 6.7 %collective-permute-start.15 = (f32[128,256]{1,0:T(8,128)}, f32[128,256]{1,0:T(8,128)S(1)}, u32[]{:S(2)}, u32[]{:S(2)}) collective-permute-start(f32[128,256]{1,0:T(8,128)} %collective-permute-done.13.refs_0_), channel_id=1, source_target_pairs={{0,1},{1,0},{2,3},{3,2},{4,5},{5,4},{6,7},{7,6},{8,9},{9,8},{10,11... | collective-permute-start | bytes 393224 | tf_op jit(solution)/shard_map/ppermute | solution.py:25
  33.8 7.0 %collective-permute-start.14 = (f32[2,64,128]{2,1,0:T(8,128)S(1)}, f32[2,64,128]{2,1,0:T(8,128)S(1)}, u32[]{:S(2)}, u32[]{:S(2)}) collective-permute-start(f32[2,64,128]{2,1,0:T(8,128)S(1)} %add_add_fusion), channel_id=1, source_target_pairs={{0,4},{2,6},{4,0},{6,2},{1,5},{3,7},{5,1},{7,3},{8,12},{10,14},{12... | collective-permute-start | bytes 196616 | tf_op jit(solution)/shard_map/ppermute | solution.py:25
  40.8 1.3 %collective-permute-start.17 = (f32[2,64,128]{2,1,0:T(8,128)S(1)}, f32[2,64,128]{2,1,0:T(8,128)S(1)}, u32[]{:S(2)}, u32[]{:S(2)}) collective-permute-start(f32[2,64,128]{2,1,0:T(8,128)S(1)} %add.46), channel_id=1, source_target_pairs={{0,8},{8,0},{16,24},{24,16},{1,9},{9,1},{17,25},{25,17},{2,10},{10... | collective-permute-start | bytes 196616 | tf_op jit(solution)/shard_map/ppermute | solution.py:25

commit v6 on v5

--- a/solution.py
+++ b/solution.py
@@ -15,7 +15,7 @@
 DONE = {'core_own': 2, 'mine0': 2, 'mine1': 5, 'mine2': 3, 'normed_other': 4, 'panel': 6, 'prep': 4, 'theirs0': 5, 'theirs1': None, 'theirs2': None}
 GATE = {'mine0': 0, 'mine2': False, 'scalars': True}
 SPLIT = True
-RADIX = True
+RADIX = False
 MIX = False
 TIED = False
 COST = [100000000000, 100000000000, 100000000000]
@@ -39,7 +39,7 @@
     half = out.shape[0]
     core = scalars[scalars.shape[0] - 3]
     for s in range(half):
-        out[s] = packed_product(split(dinv[core * half + s]), split(lower[s]), CONTRACT_FIRST)
+        out[s] = product(split(dinv[core * half + s]), split(lower[s]), CONTRACT_FIRST)
 
 
 def packed_product(left, right, dims):

time: 43.2 us -> 43.1 us (level)
  waiting for transfers between devices: 5.67 us -> 8.54 us
  starting transfers between devices: 22.5 us -> 19.7 us
    ppermute x17, waiting for transfers between devices: 5.66 us -> 8.54 us  [xor_permute(): lax.ppermute(value, axis, [(i, i ^ distance) for i in range(lax.axis_size...]
    ppermute x17, starting transfers between devices: 21.5 us -> 19.7 us  [xor_permute(): lax.ppermute(value, axis, [(i, i ^ distance) for i in range(lax.axis_size...]
    ppermute x1 -> x0, starting transfers between devices: 0.95 us -> none  [per_device(): lax.ppermute(total, ('row', 'col'), both)]
  transfers between devices with their start and end apart: 18 -> 17, of which waited for: 7 -> 8; matrix products, arithmetic and copies ran while one was open for 5% -> 5% of each run, Pallas kernels for 22% -> 22%
where the time goes in v6:
time: 43.1 us; the launch traced here: 42.9 us
  starting transfers between devices  19.7 us (46%)
  Pallas kernels  9.41 us (22%)
  waiting for transfers between devices  8.54 us (20%)
  local copies, waits for them, and re-layouts  3.76 us (9%)
  other arithmetic  0.77 us (2%)
  between operations  0.76 us (2%)
    ppermute x17, starting transfers between devices, xor_permute(): lax.ppermute(value, axis, [(i, i ^ distance) for i in range(lax.axis_size...  19.7 us
    pallas_call x5, Pallas kernels, call(): pl.pallas_call(kernel, out_shape=out_shape, in_specs=[smem] + [vmem] * le...  9.41 us
    ppermute x17, waiting for transfers between devices, xor_permute(): lax.ppermute(value, axis, [(i, i ^ distance) for i in range(lax.axis_size...  8.54 us
    dynamic_slice x1, local copies, waits for them, and re-layouts, per_device(): lax.dynamic_slice_in_dim(ancestor_inverse, (col_id ^ step) * own_rows, ow...  1.8 us
    unnamed x9, local copies, waits for them, and re-layouts  1.7 us
  transfers between devices with their start and end apart: 17, of which 8 were waited for; matrix products, arithmetic and copies ran while one was open for 5% of the time, Pallas kernels for 22%

profile of v6, /device:TPU:0, one launch (start us, length us, event | category | flops | bytes accessed | tf_op | source)
XLA Modules:
  0.0 42.9 jit_solution(16683650218021333521)
XLA Ops:
  0.7 0.9 %copy-done = f32[8,64,128]{2,1,0:T(8,128)S(1)} copy-done((f32[8,64,128]{2,1,0:T(8,128)S(1)}, f32[8,64,128]{2,1,0:T(8,128)}, u32[]{:S(2)}) %copy-start) | copy-done | bytes 262168
  1.6 4.1 %collective-permute-start = (f32[4,64,128]{2,1,0:T(8,128)S(1)}, f32[4,64,128]{2,1,0:T(8,128)S(1)}, u32[]{:S(2)}, u32[]{:S(2)}) collective-permute-start(f32[4,64,128]{2,1,0:T(8,128)S(1)} %constant_dynamic-slice_fusion.3.refs_0_), channel_id=1, source_target_pairs={{0,4},{2,6},{4,0},{6,2},{1,5},{3,7},{5,1},{7,3},{8,12},{10,14},{12... | collective-permute-start | bytes 393224 | tf_op jit(solution)/shard_map/ppermute | solution.py:25
  5.7 1.6 %collective-permute-start.2 = (f32[4,64,128]{2,1,0:T(8,128)S(1)}, f32[4,64,128]{2,1,0:T(8,128)S(1)}, u32[]{:S(2)}, u32[]{:S(2)}) collective-permute-start(f32[4,64,128]{2,1,0:T(8,128)S(1)} %constant_dynamic-slice_fusion.3.refs_0_), channel_id=1, source_target_pairs={{0,2},{2,0},{4,6},{6,4},{1,3},{3,1},{5,7},{7,5},{8,10},{10,8},{12,... | collective-permute-start | bytes 393224 | tf_op jit(solution)/shard_map/ppermute | solution.py:25
  7.3 1.5 %collective-permute-start.1 = (f32[512,256]{1,0:T(8,128)}, f32[512,256]{1,0:T(8,128)S(1)}, u32[]{:S(2)}, u32[]{:S(2)}) collective-permute-start(f32[512,256]{1,0:T(8,128)} %refs_2_.1), channel_id=1, source_target_pairs={{0,1},{1,0},{2,3},{3,2},{4,5},{5,4},{6,7},{7,6},{8,9},{9,8},{10,11... | collective-permute-start | bytes 1572872 | tf_op jit(solution)/shard_map/ppermute | solution.py:25
  8.8 1.8 %constant_dynamic-slice_fusion = (f32[128,256]{1,0:T(8,128)}, f32[128,256]{1,0:T(8,128)}, f32[128,256]{1,0:T(8,128)S(1)}) fusion(f32[512,256]{1,0:T(8,128)} %refs_2_.1, s32[]{:T(128)S(6)} %select_n.35, s32[]{:T(128)S(6)} %select_n.34, s32[]{:T(128)S(6)} %select_n.33), kind=kLoop, calls=%fused_computation.3 | loop fusion | bytes 786444 | tf_op jit(solution)/shard_map/dynamic_slice | solution.py:300
  11.0 0.7 %copy-done.3 = s32[8,4]{0,1:T(4,128)S(1)} copy-done((s32[8,4]{0,1:T(4,128)S(1)}, s32[8,4]{0,1:T(4,128)}, u32[]{:S(2)}) %copy-start.3) | copy-done | bytes 152
  12.1 0.8 %shard_map.59.refs_2_ = f32[4,64,128]{2,1,0:T(8,128)S(1)} custom-call(s32[37]{0:T(128)S(1)} %concatenate.6.scalars, f32[8,64,64]{2,1,0:T(8,128)S(1)} %copy-done.2, f32[4,64,128]{2,1,0:T(8,128)S(1)} %collective-permute-done.lower), custom_call_target="tpu_custom_call" | custom-call | flops 99999997952 | bytes 262144 | tf_op jit(solution)/shard_map/pallas_call | solution.py:265
  12.9 1.5 %collective-permute-start.3 = (f32[4,64,128]{2,1,0:T(8,128)S(1)}, f32[4,64,128]{2,1,0:T(8,128)S(1)}, u32[]{:S(2)}, u32[]{:S(2)}) collective-permute-start(f32[4,64,128]{2,1,0:T(8,128)S(1)} %shard_map.59.refs_2_), channel_id=1, source_target_pairs={{0,2},{2,0},{4,6},{6,4},{1,3},{3,1},{5,7},{7,5},{8,10},{10,8},{12,... | collective-permute-start | bytes 393224 | tf_op jit(solution)/shard_map/ppermute | solution.py:25
  14.4 2.2 %collective-permute-start.7 = (f32[128,256]{1,0:T(8,128)}, f32[128,256]{1,0:T(8,128)}, u32[]{:S(2)}, u32[]{:S(2)}) collective-permute-start(f32[128,256]{1,0:T(8,128)} %get-tuple-element.59), channel_id=1, source_target_pairs={{0,6},{2,4},{4,2},{6,0},{1,7},{3,5},{5,3},{7,1},{8,14},{10,12},{12... | collective-permute-start | bytes 393224 | tf_op jit(solution)/shard_map/ppermute | solution.py:25
  17.1 2.2 %collective-permute-done.3.refs_3_ = f32[4,64,128]{2,1,0:T(8,128)S(1)} collective-permute-done((f32[4,64,128]{2,1,0:T(8,128)S(1)}, f32[4,64,128]{2,1,0:T(8,128)S(1)}, u32[]{:S(2)}, u32[]{:S(2)}) %collective-permute-start.3) | collective-permute-done | bytes 131104 | tf_op jit(solution)/shard_map/ppermute | solution.py:25
  19.8 0.8 %collective-permute-done.1.partner.refs_3_ = f32[512,256]{1,0:T(8,128)S(1)} collective-permute-done((f32[512,256]{1,0:T(8,128)}, f32[512,256]{1,0:T(8,128)S(1)}, u32[]{:S(2)}, u32[]{:S(2)}) %collective-permute-start.1) | collective-permute-done | bytes 524320 | tf_op jit(solution)/shard_map/ppermute | solution.py:25
  20.6 2.4 %shard_map.60 = (f32[256,256]{1,0:T(8,128)S(1)}, f32[4,4,64,128]{3,2,1,0:T(8,128)S(1)}, bf16[9,256,128]{2,1,0:T(8,128)(2,1)S(1)}, bf16[9,256,128]{2,1,0:T(8,128)...) custom-call(s32[37]{0:T(128)S(1)} %concatenate.6.scalars, f32[8,64,64]{2,1,0:T(8,128)S(1)} %copy-done.2, ...), custom_call_target="tpu_custom_call" | custom-call | flops 99999997952 | bytes 1703936 | tf_op jit(solution)/shard_map/pallas_call | solution.py:265
  23.0 0.6 %collective-permute-start.9 = (f32[4,4,64,128]{3,2,1,0:T(8,128)S(1)}, f32[4,4,64,128]{3,2,1,0:T(8,128)S(1)}, u32[]{:S(2)}, u32[]{:S(2)}) collective-permute-start(f32[4,4,64,128]{3,2,1,0:T(8,128)S(1)} %get-tuple-element.44.refs_0_), channel_id=1, source_target_pairs={{0,8},{8,0},{16,24},{24,16},{1,9},{9,1},{17,25},{25,17},{2,10},{10... | collective-permute-start | bytes 1572872 | tf_op jit(solution)/shard_map/ppermute | solution.py:25
  23.6 1.9 %shard_map.61 = f32[2,64,128]{2,1,0:T(8,128)S(1)} custom-call(s32[37]{0:T(128)S(1)} %concatenate.6.scalars, f32[256,256]{1,0:T(8,128)S(1)} %get-tuple-element.36.total, bf16[9,256,128]{2,1,0:T(8,128)(2,1)S(1)} %get-tuple-element.37.r_high, bf16[9,256,128]{2,1,0:T(8,128)(2,1)S(1)} %get-tuple-element.38.r_low, ...), custom_call_target="tpu_custom_call" | custom-call | flops 99999997952 | bytes 4980736 | tf_op jit(solution)/shard_map/pallas_call | solution.py:265
  25.5 1.6 %collective-permute-start.8 = (f32[2,64,128]{2,1,0:T(8,128)S(1)}, f32[2,64,128]{2,1,0:T(8,128)S(1)}, u32[]{:S(2)}, u32[]{:S(2)}) collective-permute-start(f32[2,64,128]{2,1,0:T(8,128)S(1)} %shard_map.61), channel_id=1, source_target_pairs={{0,16},{8,24},{16,0},{24,8},{1,17},{9,25},{17,1},{25,9},{2,18},{10... | collective-permute-start | bytes 196616 | tf_op jit(solution)/shard_map/ppermute | solution.py:25
  27.1 2.0 %collective-permute-done.12.refs_0_ = f32[128,256]{1,0:T(8,128)} collective-permute-done((f32[128,256]{1,0:T(8,128)}, f32[128,256]{1,0:T(8,128)}, u32[]{:S(2)}, u32[]{:S(2)}) %collective-permute-start.12) | collective-permute-done | bytes 131104 | tf_op jit(solution)/shard_map/ppermute | solution.py:25
  29.1 1.5 %collective-permute-start.14 = (f32[128,256]{1,0:T(8,128)}, f32[128,256]{1,0:T(8,128)S(1)}, u32[]{:S(2)}, u32[]{:S(2)}) collective-permute-start(f32[128,256]{1,0:T(8,128)} %collective-permute-done.12.refs_0_), channel_id=1, source_target_pairs={{0,1},{1,0},{2,3},{3,2},{4,5},{5,4},{6,7},{7,6},{8,9},{9,8},{10,11... | collective-permute-start | bytes 393224 | tf_op jit(solution)/shard_map/ppermute | solution.py:25
  31.1 0.9 %collective-permute-start.10 = (f32[2,64,128]{2,1,0:T(8,128)S(1)}, f32[2,64,128]{2,1,0:T(8,128)S(1)}, u32[]{:S(2)}, u32[]{:S(2)}) collective-permute-start(f32[2,64,128]{2,1,0:T(8,128)S(1)} %add.39), channel_id=1, source_target_pairs={{0,2},{2,0},{4,6},{6,4},{1,3},{3,1},{5,7},{7,5},{8,10},{10,8},{12,... | collective-permute-start | bytes 196616 | tf_op jit(solution)/shard_map/ppermute | solution.py:25
  32.1 1.7 %shard_map.62 = (bf16[4,8,64,128]{3,2,1,0:T(8,128)(2,1)S(1)}, bf16[4,8,64,128]{3,2,1,0:T(8,128)(2,1)S(1)}, bf16[8,128,128]{2,1,0:T(8,128)(2,1)S(1)}, bf16[8,128,128]{2,1,0:T(8,128)(2,1)S(1)}, f32[4,64,128]{2,1,0:T(8,128)S(1)}) custom-call(s32[37]{0:T(128)S(1)} %concatenate.6.scalars, f32[8,64,64]{2,1,0:T(8,128)S(1)} %copy-done.2, ...), custom_call_target="tpu_custom_call" | custom-call | flops 10000000 | bytes 2490368 | tf_op jit(solution)/shard_map/pallas_call | solution.py:265
  33.8 1.7 %collective-permute-done.10 = f32[2,64,128]{2,1,0:T(8,128)S(1)} collective-permute-done((f32[2,64,128]{2,1,0:T(8,128)S(1)}, f32[2,64,128]{2,1,0:T(8,128)S(1)}, u32[]{:S(2)}, u32[]{:S(2)}) %collective-permute-start.10) | collective-permute-done | bytes 65568 | tf_op jit(solution)/shard_map/ppermute | solution.py:25
  35.5 2.5 %collective-permute-start.13 = (f32[2,64,128]{2,1,0:T(8,128)S(1)}, f32[2,64,128]{2,1,0:T(8,128)S(1)}, u32[]{:S(2)}, u32[]{:S(2)}) collective-permute-start(f32[2,64,128]{2,1,0:T(8,128)S(1)} %add.40), channel_id=1, source_target_pairs={{0,4},{2,6},{4,0},{6,2},{1,5},{3,7},{5,1},{7,3},{8,12},{10,14},{12... | collective-permute-start | bytes 196616 | tf_op jit(solution)/shard_map/ppermute | solution.py:25
  38.0 2.6 %shard_map.63 = f32[8,64,128]{2,1,0:T(8,128)} custom-call(s32[37]{0:T(128)S(1)} %concatenate.6.scalars, bf16[4,8,64,128]{3,2,1,0:T(8,128)(2,1)S(1)} %get-tuple-element.49.n_high, bf16[4,8,64,128]{3,2,1,0:T(8,128)(2,1)S(1)} %get-tuple-element.50.n_low, bf16[8,128,128]{2,1,0:T(8,128)(2,1)S(1)} %get-tuple-element.51.early_high, ...), custom_call_target="tpu_custom_call" | custom-call | flops 99999997952 | bytes 3670016 | tf_op jit(solution)/shard_map/pallas_call | solution.py:265
  40.8 1.2 %collective-permute-done.16 = f32[2,64,128]{2,1,0:T(8,128)S(1)} collective-permute-done((f32[2,64,128]{2,1,0:T(8,128)S(1)}, f32[2,64,128]{2,1,0:T(8,128)S(1)}, u32[]{:S(2)}, u32[]{:S(2)}) %collective-permute-start.16) | collective-permute-done | bytes 65568 | tf_op jit(solution)/shard_map/ppermute | solution.py:25
  42.2 0.7 %pad_maximum_fusion = f32[8,64,64]{2,1,0:T(8,128)} fusion(f32[2,64,64]{2,1,0:T(8,128)S(1)} %get-tuple-element.67, f32[2,64,64]{2,1,0:T(8,128)S(1)} %get-tuple-element.68, f32[2,64,64]{2,1,0:T(8,128)S(1)} %get-tuple-element.64, f32[2,64,64]{2,1,0:T(8,128)S(1)} %get-tuple-element.63), kind=kLoop, calls=%fused_computation | loop fusion | flops 98304 | bytes 262144 | tf_op jit(solution)/shard_map/concatenate | solution.py:452
  (34 shorter events, 2.8 us)
Async XLA Ops:
  0.6 1.0 %copy-start = (f32[8,64,128]{2,1,0:T(8,128)S(1)}, f32[8,64,128]{2,1,0:T(8,128)}, u32[]{:S(2)}) copy-start(f32[8,64,128]{2,1,0:T(8,128)} %param.4) | copy-start | bytes 786436
  1.6 10.5 %collective-permute-start = (f32[4,64,128]{2,1,0:T(8,128)S(1)}, f32[4,64,128]{2,1,0:T(8,128)S(1)}, u32[]{:S(2)}, u32[]{:S(2)}) collective-permute-start(f32[4,64,128]{2,1,0:T(8,128)S(1)} %constant_dynamic-slice_fusion.3.refs_0_), channel_id=1, source_target_pairs={{0,4},{2,6},{4,0},{6,2},{1,5},{3,7},{5,1},{7,3},{8,12},{10,14},{12... | collective-permute-start | bytes 393224 | tf_op jit(solution)/shard_map/ppermute | solution.py:25
  5.7 8.7 %collective-permute-start.2 = (f32[4,64,128]{2,1,0:T(8,128)S(1)}, f32[4,64,128]{2,1,0:T(8,128)S(1)}, u32[]{:S(2)}, u32[]{:S(2)}) collective-permute-start(f32[4,64,128]{2,1,0:T(8,128)S(1)} %constant_dynamic-slice_fusion.3.refs_0_), channel_id=1, source_target_pairs={{0,2},{2,0},{4,6},{6,4},{1,3},{3,1},{5,7},{7,5},{8,10},{10,8},{12,... | collective-permute-start | bytes 393224 | tf_op jit(solution)/shard_map/ppermute | solution.py:25
  7.3 13.3 %collective-permute-start.1 = (f32[512,256]{1,0:T(8,128)}, f32[512,256]{1,0:T(8,128)S(1)}, u32[]{:S(2)}, u32[]{:S(2)}) collective-permute-start(f32[512,256]{1,0:T(8,128)} %refs_2_.1), channel_id=1, source_target_pairs={{0,1},{1,0},{2,3},{3,2},{4,5},{5,4},{6,7},{7,6},{8,9},{9,8},{10,11... | collective-permute-start | bytes 1572872 | tf_op jit(solution)/shard_map/ppermute | solution.py:25
  8.8 11.8 %collective-permute-start.4 = (f32[512,256]{1,0:T(8,128)}, f32[512,256]{1,0:T(8,128)S(1)}, u32[]{:S(2)}, u32[]{:S(2)}) collective-permute-start(f32[512,256]{1,0:T(8,128)} %refs_2_.1), channel_id=1, source_target_pairs={{0,8},{8,0},{16,24},{24,16},{1,9},{9,1},{17,25},{25,17},{2,10},{10... | collective-permute-start | bytes 1572872 | tf_op jit(solution)/shard_map/ppermute | solution.py:25
  8.8 3.3 %copy-start.2 = (f32[8,64,64]{2,1,0:T(8,128)S(1)}, f32[8,64,64]{2,1,0:T(8,128)}, u32[]{:S(2)}) copy-start(f32[8,64,64]{2,1,0:T(8,128)} %dinv.5) | copy-start | bytes 393220
  10.6 6.4 %collective-permute-start.6 = (f32[128,256]{1,0:T(8,128)S(1)}, f32[128,256]{1,0:T(8,128)}, u32[]{:S(2)}, u32[]{:S(2)}) collective-permute-start(f32[128,256]{1,0:T(8,128)S(1)} %get-tuple-element.60), channel_id=1, source_target_pairs={{0,2},{2,0},{4,6},{6,4},{1,3},{3,1},{5,7},{7,5},{8,10},{10,8},{12,... | collective-permute-start | bytes 393224 | tf_op jit(solution)/shard_map/ppermute | solution.py:25
  11.0 0.7 %copy-start.3 = (s32[8,4]{0,1:T(4,128)S(1)}, s32[8,4]{0,1:T(4,128)}, u32[]{:S(2)}) copy-start(s32[8,4]{0,1:T(4,128)} %param.7) | copy-start | bytes 388
  12.0 8.6 %copy-start.1 = (f32[512,256]{1,0:T(8,128)S(1)}, f32[512,256]{1,0:T(8,128)}, u32[]{:S(2)}) copy-start(f32[512,256]{1,0:T(8,128)} %refs_2_.1) | copy-start | bytes 1572868
  12.9 6.4 %collective-permute-start.3 = (f32[4,64,128]{2,1,0:T(8,128)S(1)}, f32[4,64,128]{2,1,0:T(8,128)S(1)}, u32[]{:S(2)}, u32[]{:S(2)}) collective-permute-start(f32[4,64,128]{2,1,0:T(8,128)S(1)} %shard_map.59.refs_2_), channel_id=1, source_target_pairs={{0,2},{2,0},{4,6},{6,4},{1,3},{3,1},{5,7},{7,5},{8,10},{10,8},{12,... | collective-permute-start | bytes 393224 | tf_op jit(solution)/shard_map/ppermute | solution.py:25
  14.4 11.2 %collective-permute-start.7 = (f32[128,256]{1,0:T(8,128)}, f32[128,256]{1,0:T(8,128)}, u32[]{:S(2)}, u32[]{:S(2)}) collective-permute-start(f32[128,256]{1,0:T(8,128)} %get-tuple-element.59), channel_id=1, source_target_pairs={{0,6},{2,4},{4,2},{6,0},{1,7},{3,5},{5,3},{7,1},{8,14},{10,12},{12... | collective-permute-start | bytes 393224 | tf_op jit(solution)/shard_map/ppermute | solution.py:25
  17.0 12.1 %collective-permute-start.12 = (f32[128,256]{1,0:T(8,128)}, f32[128,256]{1,0:T(8,128)}, u32[]{:S(2)}, u32[]{:S(2)}) collective-permute-start(f32[128,256]{1,0:T(8,128)} %get-tuple-element.58), channel_id=1, source_target_pairs={{0,4},{2,6},{4,0},{6,2},{1,5},{3,7},{5,1},{7,3},{8,12},{10,14},{12... | collective-permute-start | bytes 393224 | tf_op jit(solution)/shard_map/ppermute | solution.py:25
  19.3 12.8 %collective-permute-start.11 = (f32[128,256]{1,0:T(8,128)}, f32[128,256]{1,0:T(8,128)}, u32[]{:S(2)}, u32[]{:S(2)}) collective-permute-start(f32[128,256]{1,0:T(8,128)} %collective-permute-done.6.refs_4_), channel_id=1, source_target_pairs={{0,1},{1,0},{2,3},{3,2},{4,5},{5,4},{6,7},{7,6},{8,9},{9,8},{10,11... | collective-permute-start | bytes 393224 | tf_op jit(solution)/shard_map/ppermute | solution.py:25
  20.6 3.0 %collective-permute-start.5 = (f32[512,256]{1,0:T(8,128)S(1)}, f32[512,256]{1,0:T(8,128)S(1)}, u32[]{:S(2)}, u32[]{:S(2)}) collective-permute-start(f32[512,256]{1,0:T(8,128)S(1)} %collective-permute-done.1.partner.refs_3_), channel_id=1, source_target_pairs={{0,8},{8,0},{16,24},{24,16},{1,9},{9,1},{17,25},{25,17},{2,10},{10... | collective-permute-start | bytes 1572872 | tf_op jit(solution)/shard_map/ppermute | solution.py:25
  23.0 8.1 %collective-permute-start.9 = (f32[4,4,64,128]{3,2,1,0:T(8,128)S(1)}, f32[4,4,64,128]{3,2,1,0:T(8,128)S(1)}, u32[]{:S(2)}, u32[]{:S(2)}) collective-permute-start(f32[4,4,64,128]{3,2,1,0:T(8,128)S(1)} %get-tuple-element.44.refs_0_), channel_id=1, source_target_pairs={{0,8},{8,0},{16,24},{24,16},{1,9},{9,1},{17,25},{25,17},{2,10},{10... | collective-permute-start | bytes 1572872 | tf_op jit(solution)/shard_map/ppermute | solution.py:25
  25.5 5.6 %collective-permute-start.8 = (f32[2,64,128]{2,1,0:T(8,128)S(1)}, f32[2,64,128]{2,1,0:T(8,128)S(1)}, u32[]{:S(2)}, u32[]{:S(2)}) collective-permute-start(f32[2,64,128]{2,1,0:T(8,128)S(1)} %shard_map.61), channel_id=1, source_target_pairs={{0,16},{8,24},{16,0},{24,8},{1,17},{9,25},{17,1},{25,9},{2,18},{10... | collective-permute-start | bytes 196616 | tf_op jit(solution)/shard_map/ppermute | solution.py:25
  29.1 8.9 %collective-permute-start.14 = (f32[128,256]{1,0:T(8,128)}, f32[128,256]{1,0:T(8,128)S(1)}, u32[]{:S(2)}, u32[]{:S(2)}) collective-permute-start(f32[128,256]{1,0:T(8,128)} %collective-permute-done.12.refs_0_), channel_id=1, source_target_pairs={{0,1},{1,0},{2,3},{3,2},{4,5},{5,4},{6,7},{7,6},{8,9},{9,8},{10,11... | collective-permute-start | bytes 393224 | tf_op jit(solution)/shard_map/ppermute | solution.py:25
  30.6 7.4 %collective-permute-start.15 = (f32[128,256]{1,0:T(8,128)}, f32[128,256]{1,0:T(8,128)S(1)}, u32[]{:S(2)}, u32[]{:S(2)}) collective-permute-start(f32[128,256]{1,0:T(8,128)} %collective-permute-done.7.refs_1_), channel_id=1, source_target_pairs={{0,1},{1,0},{2,3},{3,2},{4,5},{5,4},{6,7},{7,6},{8,9},{9,8},{10,11... | collective-permute-start | bytes 393224 | tf_op jit(solution)/shard_map/ppermute | solution.py:25
  31.1 4.3 %collective-permute-start.10 = (f32[2,64,128]{2,1,0:T(8,128)S(1)}, f32[2,64,128]{2,1,0:T(8,128)S(1)}, u32[]{:S(2)}, u32[]{:S(2)}) collective-permute-start(f32[2,64,128]{2,1,0:T(8,128)S(1)} %add.39), channel_id=1, source_target_pairs={{0,2},{2,0},{4,6},{6,4},{1,3},{3,1},{5,7},{7,5},{8,10},{10,8},{12,... | collective-permute-start | bytes 196616 | tf_op jit(solution)/shard_map/ppermute | solution.py:25
  35.5 5.2 %collective-permute-start.13 = (f32[2,64,128]{2,1,0:T(8,128)S(1)}, f32[2,64,128]{2,1,0:T(8,128)S(1)}, u32[]{:S(2)}, u32[]{:S(2)}) collective-permute-start(f32[2,64,128]{2,1,0:T(8,128)S(1)} %add.40), channel_id=1, source_target_pairs={{0,4},{2,6},{4,0},{6,2},{1,5},{3,7},{5,1},{7,3},{8,12},{10,14},{12... | collective-permute-start | bytes 196616 | tf_op jit(solution)/shard_map/ppermute | solution.py:25
  40.7 1.3 %collective-permute-start.16 = (f32[2,64,128]{2,1,0:T(8,128)S(1)}, f32[2,64,128]{2,1,0:T(8,128)S(1)}, u32[]{:S(2)}, u32[]{:S(2)}) collective-permute-start(f32[2,64,128]{2,1,0:T(8,128)S(1)} %add.42), channel_id=1, source_target_pairs={{0,8},{8,0},{16,24},{24,16},{1,9},{9,1},{17,25},{25,17},{2,10},{10... | collective-permute-start | bytes 196616 | tf_op jit(solution)/shard_map/ppermute | solution.py:25

commit v7 on v4

--- a/solution.py
+++ b/solution.py
@@ -16,7 +16,7 @@
 GATE = {'mine0': 0, 'mine2': False, 'scalars': True}
 SPLIT = True
 RADIX = False
-MIX = False
+MIX = True
 TIED = False
 COST = [100000000000, 100000000000, 100000000000]
 

time: 43.2 us -> 43.2 us (level)
    ppermute x17 -> x15, starting transfers between devices: 19.9 us -> 16.4 us  [xor_permute(): lax.ppermute(value, axis, [(i, i ^ distance) for i in range(lax.axis_size...]
    ppermute x0 -> x2, starting transfers between devices: none -> 3.54 us  [per_device(): total = total + lax.ppermute(total, ('row', 'col'), pairs)]
    ppermute x17 -> x15, waiting for transfers between devices: 8.31 us -> 6.6 us  [xor_permute(): lax.ppermute(value, axis, [(i, i ^ distance) for i in range(lax.axis_size...]
    ppermute x0 -> x2, waiting for transfers between devices: none -> 1.71 us  [per_device(): total = total + lax.ppermute(total, ('row', 'col'), pairs)]
where the time goes in v7:
time: 43.2 us; the launch traced here: 43 us
  starting transfers between devices  19.9 us (46%)
  Pallas kernels  9.5 us (22%)
  waiting for transfers between devices  8.31 us (19%)
  local copies, waits for them, and re-layouts  3.76 us (9%)
  other arithmetic  0.77 us (2%)
  between operations  0.77 us (2%)
    ppermute x15, starting transfers between devices, xor_permute(): lax.ppermute(value, axis, [(i, i ^ distance) for i in range(lax.axis_size...  16.4 us
    pallas_call x5, Pallas kernels, call(): pl.pallas_call(kernel, out_shape=out_shape, in_specs=[smem] + [vmem] * le...  9.5 us
    ppermute x15, waiting for transfers between devices, xor_permute(): lax.ppermute(value, axis, [(i, i ^ distance) for i in range(lax.axis_size...  6.6 us
    ppermute x2, starting transfers between devices, per_device(): total = total + lax.ppermute(total, ('row', 'col'), pairs)  3.54 us
    dynamic_slice x1, local copies, waits for them, and re-layouts, per_device(): lax.dynamic_slice_in_dim(ancestor_inverse, (col_id ^ step) * own_rows, ow...  1.8 us
    ppermute x2, waiting for transfers between devices, per_device(): total = total + lax.ppermute(total, ('row', 'col'), pairs)  1.71 us
    unnamed x9, local copies, waits for them, and re-layouts  1.7 us
  transfers between devices with their start and end apart: 17, of which 8 were waited for; matrix products, arithmetic and copies ran while one was open for 5% of the time, Pallas kernels for 22%

profile of v7, /device:TPU:0, one launch (start us, length us, event | category | flops | bytes accessed | tf_op | source)
XLA Modules:
  0.0 43.0 jit_solution(18201263323210791033)
XLA Ops:
  0.7 0.9 %copy-done = f32[8,64,128]{2,1,0:T(8,128)S(1)} copy-done((f32[8,64,128]{2,1,0:T(8,128)S(1)}, f32[8,64,128]{2,1,0:T(8,128)}, u32[]{:S(2)}) %copy-start) | copy-done | bytes 262168
  1.6 4.1 %collective-permute-start = (f32[4,64,128]{2,1,0:T(8,128)S(1)}, f32[4,64,128]{2,1,0:T(8,128)S(1)}, u32[]{:S(2)}, u32[]{:S(2)}) collective-permute-start(f32[4,64,128]{2,1,0:T(8,128)S(1)} %constant_dynamic-slice_fusion.3.refs_0_), channel_id=1, source_target_pairs={{0,4},{2,6},{4,0},{6,2},{1,5},{3,7},{5,1},{7,3},{8,12},{10,14},{12... | collective-permute-start | bytes 393224 | tf_op jit(solution)/shard_map/ppermute | solution.py:25
  5.7 1.6 %collective-permute-start.2 = (f32[4,64,128]{2,1,0:T(8,128)S(1)}, f32[4,64,128]{2,1,0:T(8,128)S(1)}, u32[]{:S(2)}, u32[]{:S(2)}) collective-permute-start(f32[4,64,128]{2,1,0:T(8,128)S(1)} %constant_dynamic-slice_fusion.3.refs_0_), channel_id=1, source_target_pairs={{0,2},{2,0},{4,6},{6,4},{1,3},{3,1},{5,7},{7,5},{8,10},{10,8},{12,... | collective-permute-start | bytes 393224 | tf_op jit(solution)/shard_map/ppermute | solution.py:25
  7.3 1.5 %collective-permute-start.1 = (f32[512,256]{1,0:T(8,128)}, f32[512,256]{1,0:T(8,128)S(1)}, u32[]{:S(2)}, u32[]{:S(2)}) collective-permute-start(f32[512,256]{1,0:T(8,128)} %refs_2_.1), channel_id=1, source_target_pairs={{0,1},{1,0},{2,3},{3,2},{4,5},{5,4},{6,7},{7,6},{8,9},{9,8},{10,11... | collective-permute-start | bytes 1572872 | tf_op jit(solution)/shard_map/ppermute | solution.py:25
  8.8 1.8 %constant_dynamic-slice_fusion = (f32[128,256]{1,0:T(8,128)}, f32[128,256]{1,0:T(8,128)}, f32[128,256]{1,0:T(8,128)S(1)}) fusion(f32[512,256]{1,0:T(8,128)} %refs_2_.1, s32[]{:T(128)S(6)} %select_n.35, s32[]{:T(128)S(6)} %select_n.34, s32[]{:T(128)S(6)} %select_n.33), kind=kLoop, calls=%fused_computation.3 | loop fusion | bytes 786444 | tf_op jit(solution)/shard_map/dynamic_slice | solution.py:300
  11.0 0.7 %copy-done.3 = s32[8,4]{0,1:T(4,128)S(1)} copy-done((s32[8,4]{0,1:T(4,128)S(1)}, s32[8,4]{0,1:T(4,128)}, u32[]{:S(2)}) %copy-start.3) | copy-done | bytes 152
  12.1 0.9 %shard_map.59.refs_2_ = f32[4,64,128]{2,1,0:T(8,128)S(1)} custom-call(s32[37]{0:T(128)S(1)} %concatenate.6.scalars, f32[8,64,64]{2,1,0:T(8,128)S(1)} %copy-done.2, f32[4,64,128]{2,1,0:T(8,128)S(1)} %collective-permute-done.lower), custom_call_target="tpu_custom_call" | custom-call | flops 99999997952 | bytes 262144 | tf_op jit(solution)/shard_map/pallas_call | solution.py:265
  13.0 1.5 %collective-permute-start.3 = (f32[4,64,128]{2,1,0:T(8,128)S(1)}, f32[4,64,128]{2,1,0:T(8,128)S(1)}, u32[]{:S(2)}, u32[]{:S(2)}) collective-permute-start(f32[4,64,128]{2,1,0:T(8,128)S(1)} %shard_map.59.refs_2_), channel_id=1, source_target_pairs={{0,2},{2,0},{4,6},{6,4},{1,3},{3,1},{5,7},{7,5},{8,10},{10,8},{12,... | collective-permute-start | bytes 393224 | tf_op jit(solution)/shard_map/ppermute | solution.py:25
  14.5 2.2 %collective-permute-start.7 = (f32[128,256]{1,0:T(8,128)}, f32[128,256]{1,0:T(8,128)}, u32[]{:S(2)}, u32[]{:S(2)}) collective-permute-start(f32[128,256]{1,0:T(8,128)} %get-tuple-element.59), channel_id=1, source_target_pairs={{0,6},{2,4},{4,2},{6,0},{1,7},{3,5},{5,3},{7,1},{8,14},{10,12},{12... | collective-permute-start | bytes 393224 | tf_op jit(solution)/shard_map/ppermute | solution.py:25
  17.2 2.1 %collective-permute-done.3.refs_3_ = f32[4,64,128]{2,1,0:T(8,128)S(1)} collective-permute-done((f32[4,64,128]{2,1,0:T(8,128)S(1)}, f32[4,64,128]{2,1,0:T(8,128)S(1)}, u32[]{:S(2)}, u32[]{:S(2)}) %collective-permute-start.3) | collective-permute-done | bytes 131104 | tf_op jit(solution)/shard_map/ppermute | solution.py:25
  19.8 0.8 %collective-permute-done.1.partner.refs_3_ = f32[512,256]{1,0:T(8,128)S(1)} collective-permute-done((f32[512,256]{1,0:T(8,128)}, f32[512,256]{1,0:T(8,128)S(1)}, u32[]{:S(2)}, u32[]{:S(2)}) %collective-permute-start.1) | collective-permute-done | bytes 524320 | tf_op jit(solution)/shard_map/ppermute | solution.py:25
  20.6 2.4 %shard_map.60 = (f32[256,256]{1,0:T(8,128)S(1)}, f32[4,4,64,128]{3,2,1,0:T(8,128)S(1)}, bf16[9,256,128]{2,1,0:T(8,128)(2,1)S(1)}, bf16[9,256,128]{2,1,0:T(8,128)...) custom-call(s32[37]{0:T(128)S(1)} %concatenate.6.scalars, f32[8,64,64]{2,1,0:T(8,128)S(1)} %copy-done.2, ...), custom_call_target="tpu_custom_call" | custom-call | flops 99999997952 | bytes 1703936 | tf_op jit(solution)/shard_map/pallas_call | solution.py:265
  23.0 0.6 %collective-permute-start.9 = (f32[4,4,64,128]{3,2,1,0:T(8,128)S(1)}, f32[4,4,64,128]{3,2,1,0:T(8,128)S(1)}, u32[]{:S(2)}, u32[]{:S(2)}) collective-permute-start(f32[4,4,64,128]{3,2,1,0:T(8,128)S(1)} %get-tuple-element.44.refs_0_), channel_id=1, source_target_pairs={{0,8},{8,0},{16,24},{24,16},{1,9},{9,1},{17,25},{25,17},{2,10},{10... | collective-permute-start | bytes 1572872 | tf_op jit(solution)/shard_map/ppermute | solution.py:25
  23.6 1.9 %shard_map.61 = f32[2,64,128]{2,1,0:T(8,128)S(1)} custom-call(s32[37]{0:T(128)S(1)} %concatenate.6.scalars, f32[256,256]{1,0:T(8,128)S(1)} %get-tuple-element.36.total, bf16[9,256,128]{2,1,0:T(8,128)(2,1)S(1)} %get-tuple-element.37.r_high, bf16[9,256,128]{2,1,0:T(8,128)(2,1)S(1)} %get-tuple-element.38.r_low, ...), custom_call_target="tpu_custom_call" | custom-call | flops 99999997952 | bytes 4980736 | tf_op jit(solution)/shard_map/pallas_call | solution.py:265
  25.5 1.6 %collective-permute-start.8 = (f32[2,64,128]{2,1,0:T(8,128)S(1)}, f32[2,64,128]{2,1,0:T(8,128)S(1)}, u32[]{:S(2)}, u32[]{:S(2)}) collective-permute-start(f32[2,64,128]{2,1,0:T(8,128)S(1)} %shard_map.61), channel_id=1, source_target_pairs={{0,16},{8,24},{16,0},{24,8},{1,17},{9,25},{17,1},{25,9},{2,18},{10... | collective-permute-start | bytes 196616 | tf_op jit(solution)/shard_map/ppermute | solution.py:25
  27.1 2.1 %collective-permute-done.12.refs_0_ = f32[128,256]{1,0:T(8,128)} collective-permute-done((f32[128,256]{1,0:T(8,128)}, f32[128,256]{1,0:T(8,128)}, u32[]{:S(2)}, u32[]{:S(2)}) %collective-permute-start.12) | collective-permute-done | bytes 131104 | tf_op jit(solution)/shard_map/ppermute | solution.py:25
  29.2 1.5 %collective-permute-start.14 = (f32[128,256]{1,0:T(8,128)}, f32[128,256]{1,0:T(8,128)S(1)}, u32[]{:S(2)}, u32[]{:S(2)}) collective-permute-start(f32[128,256]{1,0:T(8,128)} %collective-permute-done.12.refs_0_), channel_id=1, source_target_pairs={{0,1},{1,0},{2,3},{3,2},{4,5},{5,4},{6,7},{7,6},{8,9},{9,8},{10,11... | collective-permute-start | bytes 393224 | tf_op jit(solution)/shard_map/ppermute | solution.py:25
  31.3 1.0 %collective-permute-start.10 = (f32[2,64,128]{2,1,0:T(8,128)S(1)}, f32[2,64,128]{2,1,0:T(8,128)S(1)}, u32[]{:S(2)}, u32[]{:S(2)}) collective-permute-start(f32[2,64,128]{2,1,0:T(8,128)S(1)} %add.39), channel_id=1, source_target_pairs={{0,2},{2,0},{4,6},{6,4},{8,12},{10,14},{12,8},{14,10},{16,18},{18,... | collective-permute-start | bytes 196616 | tf_op jit(solution)/shard_map/ppermute | solution.py:424
  32.2 1.7 %shard_map.62 = (bf16[4,8,64,128]{3,2,1,0:T(8,128)(2,1)S(1)}, bf16[4,8,64,128]{3,2,1,0:T(8,128)(2,1)S(1)}, bf16[8,128,128]{2,1,0:T(8,128)(2,1)S(1)}, bf16[8,128,128]{2,1,0:T(8,128)(2,1)S(1)}, f32[4,64,128]{2,1,0:T(8,128)S(1)}) custom-call(s32[37]{0:T(128)S(1)} %concatenate.6.scalars, f32[8,64,64]{2,1,0:T(8,128)S(1)} %copy-done.2, ...), custom_call_target="tpu_custom_call" | custom-call | flops 10000000 | bytes 2490368 | tf_op jit(solution)/shard_map/pallas_call | solution.py:265
  33.9 1.6 %collective-permute-done.10 = f32[2,64,128]{2,1,0:T(8,128)S(1)} collective-permute-done((f32[2,64,128]{2,1,0:T(8,128)S(1)}, f32[2,64,128]{2,1,0:T(8,128)S(1)}, u32[]{:S(2)}, u32[]{:S(2)}) %collective-permute-start.10) | collective-permute-done | bytes 65568 | tf_op jit(solution)/shard_map/ppermute | solution.py:424
  35.6 2.6 %collective-permute-start.13 = (f32[2,64,128]{2,1,0:T(8,128)S(1)}, f32[2,64,128]{2,1,0:T(8,128)S(1)}, u32[]{:S(2)}, u32[]{:S(2)}) collective-permute-start(f32[2,64,128]{2,1,0:T(8,128)S(1)} %add.40), channel_id=1, source_target_pairs={{0,4},{2,6},{4,0},{6,2},{8,10},{10,8},{12,14},{14,12},{16,20},{18,... | collective-permute-start | bytes 196616 | tf_op jit(solution)/shard_map/ppermute | solution.py:424
  38.2 2.6 %shard_map.63 = f32[8,64,128]{2,1,0:T(8,128)} custom-call(s32[37]{0:T(128)S(1)} %concatenate.6.scalars, bf16[4,8,64,128]{3,2,1,0:T(8,128)(2,1)S(1)} %get-tuple-element.49.n_high, bf16[4,8,64,128]{3,2,1,0:T(8,128)(2,1)S(1)} %get-tuple-element.50.n_low, bf16[8,128,128]{2,1,0:T(8,128)(2,1)S(1)} %get-tuple-element.51.early_high, ...), custom_call_target="tpu_custom_call" | custom-call | flops 99999997952 | bytes 3670016 | tf_op jit(solution)/shard_map/pallas_call | solution.py:265
  40.9 1.2 %collective-permute-done.16 = f32[2,64,128]{2,1,0:T(8,128)S(1)} collective-permute-done((f32[2,64,128]{2,1,0:T(8,128)S(1)}, f32[2,64,128]{2,1,0:T(8,128)S(1)}, u32[]{:S(2)}, u32[]{:S(2)}) %collective-permute-start.16) | collective-permute-done | bytes 65568 | tf_op jit(solution)/shard_map/ppermute | solution.py:25
  42.3 0.7 %pad_maximum_fusion = f32[8,64,64]{2,1,0:T(8,128)} fusion(f32[2,64,64]{2,1,0:T(8,128)S(1)} %get-tuple-element.67, f32[2,64,64]{2,1,0:T(8,128)S(1)} %get-tuple-element.68, f32[2,64,64]{2,1,0:T(8,128)S(1)} %get-tuple-element.64, f32[2,64,64]{2,1,0:T(8,128)S(1)} %get-tuple-element.63), kind=kLoop, calls=%fused_computation | loop fusion | flops 98304 | bytes 262144 | tf_op jit(solution)/shard_map/concatenate | solution.py:452
  (34 shorter events, 2.8 us)
Async XLA Ops:
  0.6 1.0 %copy-start = (f32[8,64,128]{2,1,0:T(8,128)S(1)}, f32[8,64,128]{2,1,0:T(8,128)}, u32[]{:S(2)}) copy-start(f32[8,64,128]{2,1,0:T(8,128)} %param.4) | copy-start | bytes 786436
  1.6 10.5 %collective-permute-start = (f32[4,64,128]{2,1,0:T(8,128)S(1)}, f32[4,64,128]{2,1,0:T(8,128)S(1)}, u32[]{:S(2)}, u32[]{:S(2)}) collective-permute-start(f32[4,64,128]{2,1,0:T(8,128)S(1)} %constant_dynamic-slice_fusion.3.refs_0_), channel_id=1, source_target_pairs={{0,4},{2,6},{4,0},{6,2},{1,5},{3,7},{5,1},{7,3},{8,12},{10,14},{12... | collective-permute-start | bytes 393224 | tf_op jit(solution)/shard_map/ppermute | solution.py:25
  5.7 8.8 %collective-permute-start.2 = (f32[4,64,128]{2,1,0:T(8,128)S(1)}, f32[4,64,128]{2,1,0:T(8,128)S(1)}, u32[]{:S(2)}, u32[]{:S(2)}) collective-permute-start(f32[4,64,128]{2,1,0:T(8,128)S(1)} %constant_dynamic-slice_fusion.3.refs_0_), channel_id=1, source_target_pairs={{0,2},{2,0},{4,6},{6,4},{1,3},{3,1},{5,7},{7,5},{8,10},{10,8},{12,... | collective-permute-start | bytes 393224 | tf_op jit(solution)/shard_map/ppermute | solution.py:25
  7.3 13.3 %collective-permute-start.1 = (f32[512,256]{1,0:T(8,128)}, f32[512,256]{1,0:T(8,128)S(1)}, u32[]{:S(2)}, u32[]{:S(2)}) collective-permute-start(f32[512,256]{1,0:T(8,128)} %refs_2_.1), channel_id=1, source_target_pairs={{0,1},{1,0},{2,3},{3,2},{4,5},{5,4},{6,7},{7,6},{8,9},{9,8},{10,11... | collective-permute-start | bytes 1572872 | tf_op jit(solution)/shard_map/ppermute | solution.py:25
  8.8 11.8 %collective-permute-start.4 = (f32[512,256]{1,0:T(8,128)}, f32[512,256]{1,0:T(8,128)S(1)}, u32[]{:S(2)}, u32[]{:S(2)}) collective-permute-start(f32[512,256]{1,0:T(8,128)} %refs_2_.1), channel_id=1, source_target_pairs={{0,8},{8,0},{16,24},{24,16},{1,9},{9,1},{17,25},{25,17},{2,10},{10... | collective-permute-start | bytes 1572872 | tf_op jit(solution)/shard_map/ppermute | solution.py:25
  8.8 3.3 %copy-start.2 = (f32[8,64,64]{2,1,0:T(8,128)S(1)}, f32[8,64,64]{2,1,0:T(8,128)}, u32[]{:S(2)}) copy-start(f32[8,64,64]{2,1,0:T(8,128)} %dinv.5) | copy-start | bytes 393220
  10.6 6.4 %collective-permute-start.6 = (f32[128,256]{1,0:T(8,128)S(1)}, f32[128,256]{1,0:T(8,128)}, u32[]{:S(2)}, u32[]{:S(2)}) collective-permute-start(f32[128,256]{1,0:T(8,128)S(1)} %get-tuple-element.60), channel_id=1, source_target_pairs={{0,2},{2,0},{4,6},{6,4},{1,3},{3,1},{5,7},{7,5},{8,10},{10,8},{12,... | collective-permute-start | bytes 393224 | tf_op jit(solution)/shard_map/ppermute | solution.py:25
  11.0 0.7 %copy-start.3 = (s32[8,4]{0,1:T(4,128)S(1)}, s32[8,4]{0,1:T(4,128)}, u32[]{:S(2)}) copy-start(s32[8,4]{0,1:T(4,128)} %param.7) | copy-start | bytes 388
  12.0 8.6 %copy-start.1 = (f32[512,256]{1,0:T(8,128)S(1)}, f32[512,256]{1,0:T(8,128)}, u32[]{:S(2)}) copy-start(f32[512,256]{1,0:T(8,128)} %refs_2_.1) | copy-start | bytes 1572868
  13.0 6.3 %collective-permute-start.3 = (f32[4,64,128]{2,1,0:T(8,128)S(1)}, f32[4,64,128]{2,1,0:T(8,128)S(1)}, u32[]{:S(2)}, u32[]{:S(2)}) collective-permute-start(f32[4,64,128]{2,1,0:T(8,128)S(1)} %shard_map.59.refs_2_), channel_id=1, source_target_pairs={{0,2},{2,0},{4,6},{6,4},{1,3},{3,1},{5,7},{7,5},{8,10},{10,8},{12,... | collective-permute-start | bytes 393224 | tf_op jit(solution)/shard_map/ppermute | solution.py:25
  14.5 11.0 %collective-permute-start.7 = (f32[128,256]{1,0:T(8,128)}, f32[128,256]{1,0:T(8,128)}, u32[]{:S(2)}, u32[]{:S(2)}) collective-permute-start(f32[128,256]{1,0:T(8,128)} %get-tuple-element.59), channel_id=1, source_target_pairs={{0,6},{2,4},{4,2},{6,0},{1,7},{3,5},{5,3},{7,1},{8,14},{10,12},{12... | collective-permute-start | bytes 393224 | tf_op jit(solution)/shard_map/ppermute | solution.py:25
  17.0 12.2 %collective-permute-start.12 = (f32[128,256]{1,0:T(8,128)}, f32[128,256]{1,0:T(8,128)}, u32[]{:S(2)}, u32[]{:S(2)}) collective-permute-start(f32[128,256]{1,0:T(8,128)} %get-tuple-element.58), channel_id=1, source_target_pairs={{0,4},{2,6},{4,0},{6,2},{1,5},{3,7},{5,1},{7,3},{8,12},{10,14},{12... | collective-permute-start | bytes 393224 | tf_op jit(solution)/shard_map/ppermute | solution.py:25
  19.3 12.9 %collective-permute-start.11 = (f32[128,256]{1,0:T(8,128)}, f32[128,256]{1,0:T(8,128)}, u32[]{:S(2)}, u32[]{:S(2)}) collective-permute-start(f32[128,256]{1,0:T(8,128)} %collective-permute-done.6.refs_4_), channel_id=1, source_target_pairs={{0,1},{1,0},{2,3},{3,2},{4,5},{5,4},{6,7},{7,6},{8,9},{9,8},{10,11... | collective-permute-start | bytes 393224 | tf_op jit(solution)/shard_map/ppermute | solution.py:25
  20.6 3.0 %collective-permute-start.5 = (f32[512,256]{1,0:T(8,128)S(1)}, f32[512,256]{1,0:T(8,128)S(1)}, u32[]{:S(2)}, u32[]{:S(2)}) collective-permute-start(f32[512,256]{1,0:T(8,128)S(1)} %collective-permute-done.1.partner.refs_3_), channel_id=1, source_target_pairs={{0,8},{8,0},{16,24},{24,16},{1,9},{9,1},{17,25},{25,17},{2,10},{10... | collective-permute-start | bytes 1572872 | tf_op jit(solution)/shard_map/ppermute | solution.py:25
  23.0 8.2 %collective-permute-start.9 = (f32[4,4,64,128]{3,2,1,0:T(8,128)S(1)}, f32[4,4,64,128]{3,2,1,0:T(8,128)S(1)}, u32[]{:S(2)}, u32[]{:S(2)}) collective-permute-start(f32[4,4,64,128]{3,2,1,0:T(8,128)S(1)} %get-tuple-element.44.refs_0_), channel_id=1, source_target_pairs={{0,8},{8,0},{16,24},{24,16},{1,9},{9,1},{17,25},{25,17},{2,10},{10... | collective-permute-start | bytes 1572872 | tf_op jit(solution)/shard_map/ppermute | solution.py:25
  25.5 5.7 %collective-permute-start.8 = (f32[2,64,128]{2,1,0:T(8,128)S(1)}, f32[2,64,128]{2,1,0:T(8,128)S(1)}, u32[]{:S(2)}, u32[]{:S(2)}) collective-permute-start(f32[2,64,128]{2,1,0:T(8,128)S(1)} %shard_map.61), channel_id=1, source_target_pairs={{0,16},{8,24},{16,0},{24,8},{1,17},{9,25},{17,1},{25,9},{2,18},{10... | collective-permute-start | bytes 196616 | tf_op jit(solution)/shard_map/ppermute | solution.py:25
  29.2 9.0 %collective-permute-start.14 = (f32[128,256]{1,0:T(8,128)}, f32[128,256]{1,0:T(8,128)S(1)}, u32[]{:S(2)}, u32[]{:S(2)}) collective-permute-start(f32[128,256]{1,0:T(8,128)} %collective-permute-done.12.refs_0_), channel_id=1, source_target_pairs={{0,1},{1,0},{2,3},{3,2},{4,5},{5,4},{6,7},{7,6},{8,9},{9,8},{10,11... | collective-permute-start | bytes 393224 | tf_op jit(solution)/shard_map/ppermute | solution.py:25
  30.7 7.4 %collective-permute-start.15 = (f32[128,256]{1,0:T(8,128)}, f32[128,256]{1,0:T(8,128)S(1)}, u32[]{:S(2)}, u32[]{:S(2)}) collective-permute-start(f32[128,256]{1,0:T(8,128)} %collective-permute-done.7.refs_1_), channel_id=1, source_target_pairs={{0,1},{1,0},{2,3},{3,2},{4,5},{5,4},{6,7},{7,6},{8,9},{9,8},{10,11... | collective-permute-start | bytes 393224 | tf_op jit(solution)/shard_map/ppermute | solution.py:25
  31.3 4.3 %collective-permute-start.10 = (f32[2,64,128]{2,1,0:T(8,128)S(1)}, f32[2,64,128]{2,1,0:T(8,128)S(1)}, u32[]{:S(2)}, u32[]{:S(2)}) collective-permute-start(f32[2,64,128]{2,1,0:T(8,128)S(1)} %add.39), channel_id=1, source_target_pairs={{0,2},{2,0},{4,6},{6,4},{8,12},{10,14},{12,8},{14,10},{16,18},{18,... | collective-permute-start | bytes 196616 | tf_op jit(solution)/shard_map/ppermute | solution.py:424
  35.6 5.2 %collective-permute-start.13 = (f32[2,64,128]{2,1,0:T(8,128)S(1)}, f32[2,64,128]{2,1,0:T(8,128)S(1)}, u32[]{:S(2)}, u32[]{:S(2)}) collective-permute-start(f32[2,64,128]{2,1,0:T(8,128)S(1)} %add.40), channel_id=1, source_target_pairs={{0,4},{2,6},{4,0},{6,2},{8,10},{10,8},{12,14},{14,12},{16,20},{18,... | collective-permute-start | bytes 196616 | tf_op jit(solution)/shard_map/ppermute | solution.py:424
  40.8 1.3 %collective-permute-start.16 = (f32[2,64,128]{2,1,0:T(8,128)S(1)}, f32[2,64,128]{2,1,0:T(8,128)S(1)}, u32[]{:S(2)}, u32[]{:S(2)}) collective-permute-start(f32[2,64,128]{2,1,0:T(8,128)S(1)} %add.42), channel_id=1, source_target_pairs={{0,8},{8,0},{16,24},{24,16},{1,9},{9,1},{17,25},{25,17},{2,10},{10... | collective-permute-start | bytes 196616 | tf_op jit(solution)/shard_map/ppermute | solution.py:25
